TPU v7x, 1024 devices: a whole 4x4x32 slice. The times are simulated.
1024 devices in a mesh: wide: 64 (over z, core), narrow: 16 (over y, x).
Axes of the slice: x: 4, y: 4, z: 32, core: 2. Of those that a mesh axis runs over, the one named last changes fastest.
Arguments:
- features: bfloat16 [16, 8192, 128], P('narrow', 'wide'), may hold values from -16 to 16
- weight: bfloat16 [128, 128], replicated, may hold values from -0.5 to 0.5
- tiles: bfloat16 [16, 8192, 8, 128], P('narrow', 'wide'), may hold values from -0.25 to 0.25
- tile_cols: int32 [16, 64, 8], P('narrow'), may hold values from 0 to 63, as said below
- tile_counts: int32 [16, 64], P('narrow'), may hold values from 2 to 8, as said below
- cotangent: bfloat16 [16, 8192, 128], P('narrow', 'wide'), may hold values from -6 to 6
Outputs:
- activated: bfloat16 [16, 8192, 128], P('narrow', 'wide')
- feature_grad: bfloat16 [16, 8192, 128], P('narrow', 'wide')
- weight_grad: float32 [128, 128], P('wide')
Inputs may be any that keep to these rules, and one draw needn't show every extreme that they name: `tile_cols`: slot 0 of each block row holds that block row's own diagonal tile (its column equals the block row); other slots may name any block column of the group, also repeatedly. `tile_counts`: each group has a block row that uses all 8 slots.
All inputs are finite; a program needn't handle non-finite values.
Results may differ from a plain program's by a relative error of at most 0.0062.
Values may be sent and summed in bfloat16 or wider, within the bound.
No kernel may reach another device: no remote copies, remote signals or barrier semaphores. Data moves between devices by JAX's collectives and lax.ppermute only.
A program may use at most 32 MiB of HBM per device.

v0:
```python
import jax
import jax.numpy as jnp
from jax import lax
from jax.sharding import PartitionSpec as P


def shards(features, weight, tiles, tile_cols, tile_counts, cotangent):
    feat_local = features[0]
    row_count = feat_local.shape[0]
    feat_width = feat_local.shape[1]
    slot_count = tiles.shape[2]
    tile_size = tiles.shape[3]
    block_count = tile_cols.shape[1]
    local_blocks = max(row_count // tile_size, 1)
    rows_per = row_count // local_blocks
    first_block = lax.axis_index("wide") * row_count // tile_size
    cols_here = lax.dynamic_slice_in_dim(tile_cols[0], first_block, local_blocks, 0)
    counts_here = lax.dynamic_slice_in_dim(tile_counts[0], first_block, local_blocks, 0)
    alive_mask = jnp.arange(slot_count)[None, :] < counts_here[:, None]
    projected = jnp.dot(feat_local, weight, preferred_element_type=jnp.float32).astype(jnp.bfloat16)
    whole = lax.all_gather(projected, "wide", axis=0, tiled=True)
    stacked = whole.reshape(block_count, tile_size, feat_width)
    picked = stacked[cols_here] * alive_mask[:, :, None, None].astype(jnp.bfloat16)
    tile_local = tiles[0].reshape(local_blocks, rows_per, slot_count, tile_size)
    pre_act = jnp.einsum("bnst,bstd->bnd", tile_local, picked, preferred_element_type=jnp.float32)
    pre_act = pre_act.reshape(row_count, feat_width)
    sig_val = jax.nn.sigmoid(pre_act)
    activated = (pre_act * sig_val).astype(jnp.bfloat16)
    act_grad = (
        cotangent[0].astype(jnp.float32) * sig_val * (1.0 + pre_act * (1.0 - sig_val))
    ).astype(jnp.bfloat16)
    contrib = jnp.einsum(
        "bnst,bnd->bstd",
        tile_local,
        act_grad.reshape(local_blocks, rows_per, feat_width),
        preferred_element_type=jnp.float32,
    )
    seg_ids = jnp.where(alive_mask, cols_here, block_count).reshape(-1)
    summed = jax.ops.segment_sum(
        contrib.reshape(local_blocks * slot_count, tile_size, feat_width),
        seg_ids,
        num_segments=block_count + 1,
    )
    term = summed[:block_count].reshape(block_count * tile_size, feat_width)
    proj_grad = lax.psum_scatter(term, "wide", scatter_dimension=0, tiled=True).astype(jnp.bfloat16)
    feature_grad = lax.dot_general(
        proj_grad, weight, (((1,), (1,)), ((), ())), preferred_element_type=jnp.float32
    ).astype(jnp.bfloat16)
    weight_part = lax.dot_general(
        feat_local, proj_grad, (((0,), (0,)), ((), ())), preferred_element_type=jnp.float32
    )
    row_share = feat_width // lax.axis_size("wide")
    weight_total = lax.psum(weight_part, ("wide", "narrow"))
    weight_grad = lax.dynamic_slice_in_dim(
        weight_total, lax.axis_index("wide") * row_share, row_share, 0
    )
    return (activated[None], feature_grad[None], weight_grad)


def solution(mesh):
    placed = (
        P("narrow", "wide", None),
        P(),
        P("narrow", "wide", None, None),
        P("narrow", None, None),
        P("narrow", None),
        P("narrow", "wide", None),
    )
    return jax.shard_map(
        shards,
        mesh=mesh,
        in_specs=placed,
        out_specs=(P("narrow", "wide", None), P("narrow", "wide", None), P("wide", None)),
        check_vma=False,
    )
```

profile of v0, /device:TPU:1, one launch (start us, length us, event | category | flops | bytes accessed | tf_op | source)
XLA Modules:
  0.0 1231.8 jit_solution(5348884543662774948)
XLA Ops:
  7.2 0.0 copy-start
  7.2 0.0 all-gather.2.cloned.1.call-start
  7.2 1.6 convolution_convert_fusion.1
  8.8 0.0 all-gather.2.cloned.1.call-update
  8.8 0.0 reduce-scatter.2.cloned.1.call-start
  8.9 1.2 constant_dynamic-slice_fusion.1
  10.1 0.9 dynamic-slice_reduce_fusion
  11.0 0.9 copy.17
  11.9 0.7 compare_convert_fusion
  12.6 0.7 fusion.14
  13.2 143.8 %all-gather.2.cloned.1.call-done = bf16[8192,128]{1,0:T(8,128)(2,1)} async-done(((bf16[128,128]{1,0:T(8,128)(2,1)}), bf16[8192,128]{1,0:T(8,128)(2,1)}) %all-gather.2.cloned.1.call-update) | async-done | bytes 2097168 | tf_op jit(solution)/shard_map/all_gather | solution.py:21
  157.0 2.2 gather_fusion
  159.2 0.0 copy-done
  159.2 0.3 convolution_bitcast_fusion.2
  159.6 0.2 convolution_bitcast_fusion
  159.8 0.2 copy.19
  160.0 2.5 broadcast_in_dim.16
  162.5 2.7 scatter_fusion
  165.2 4.6 slice.6
  169.8 0.0 copy-start.1
  169.8 0.0 reduce-scatter.2.cloned.1.call-update
  169.8 0.0 all-reduce.2.cloned.1.call-start
  169.9 0.7 copy.20
  170.6 202.3 %reduce-scatter.2.cloned.1.call-done = f32[128,128]{1,0:T(8,128)} async-done(((f32[8192,128]{1,0:T(8,128)}), f32[128,128]{1,0:T(8,128)}) %reduce-scatter.2.cloned.1.call-update) | async-done | bytes 65552 | tf_op jit(solution)/shard_map/reduce_scatter | solution.py:45
  373.0 0.0 copy-done.1
  373.0 1.7 convolution_bitcast_fusion.1
  374.6 0.0 all-reduce.2.cloned.1.call-update
  374.6 0.0 copy-done.2
  374.7 1.6 fusion
  376.3 847.4 %all-reduce.2.cloned.1.call-done = f32[128,128]{0,1:T(8,128)} async-done(((f32[128,128]{0,1:T(8,128)}), f32[128,128]{0,1:T(8,128)}) %all-reduce.2.cloned.1.call-update) | async-done | bytes 65552 | tf_op jit(solution)/shard_map/psum | solution.py:53
  1223.7 0.9 constant_dynamic-slice_fusion
  1224.6 0.6 copy.21
  (4 shorter events, 0.0 us)
Async XLA Ops:
  7.2 152.0 %copy-start = (bf16[1,128,8,128]{3,2,1,0:T(8,128)(2,1)S(1)}, bf16[1,128,8,128]{3,2,1,0:T(8,128)(2,1)}, u32[]{:S(2)}) copy-start(bf16[1,128,8,128]{3,2,1,0:T(8,128)(2,1)} %param.8) | copy-start | bytes 786436
  7.2 149.8 %all-gather.2.cloned.1.call-start = ((), (), s32[]{:S(2)}) async-start(), calls=%async_computation.1 | async-start | bytes 2129920 | tf_op jit(solution)/shard_map/all_gather | solution.py:21
  8.8 364.1 %reduce-scatter.2.cloned.1.call-start = ((), (), s32[]{:S(2)}) async-start(), calls=%async_computation.2 | async-start | bytes 4259840 | tf_op jit(solution)/shard_map/reduce_scatter | solution.py:45
  169.8 203.2 %copy-start.1 = (bf16[1,128,128]{2,1,0:T(8,128)(2,1)S(1)}, bf16[1,128,128]{2,1,0:T(8,128)(2,1)}, u32[]{:S(2)}) copy-start(bf16[1,128,128]{2,1,0:T(8,128)(2,1)} %param.6) | copy-start | bytes 98308
  169.8 204.8 %copy-start.2 = (bf16[128,128]{1,0:T(8,128)(2,1)S(1)}, bf16[128,128]{1,0:T(8,128)(2,1)}, u32[]{:S(2)}) copy-start(bf16[128,128]{1,0:T(8,128)(2,1)} %param.7) | copy-start | bytes 98308
  169.8 1053.8 %all-reduce.2.cloned.1.call-start = ((), (), s32[]{:S(2)}) async-start(), calls=%async_computation.3 | async-start | bytes 131072 | tf_op jit(solution)/shard_map/psum | solution.py:53
Sparse Core Ops, SparseCore 0:
  11.3 145.6 all-gather.1
  169.9 202.9 reduce-scatter.1
  379.3 844.3 all-reduce.1
where the time goes:
time: 1230 us
  waiting for transfers between devices  1190 us (97%)
  local copies, waits for them, and re-layouts  14.8 us (1%)
  between operations  13.9 us (1%)
    psum x1, waiting for transfers between devices, shards(): weight_total = lax.psum(weight_part, ('wide', 'narrow'))  847 us
    reduce_scatter x1, waiting for transfers between devices, shards(): lax.psum_scatter(term, 'wide', scatter_dimension=0, tiled=True)  202 us
    all_gather x1, waiting for transfers between devices, shards(): whole = lax.all_gather(projected, 'wide', axis=0, tiled=True)  144 us
  transfers between devices with their start and end apart: 3, of which 3 were waited for; matrix products, arithmetic and copies ran while one was open for 1% of the time, Pallas kernels for 0%

commit v1 on v0

v1 whole, which is shorter than its diff:
```python
import jax
import jax.numpy as jnp
from jax import lax
from jax.experimental import pallas as pl
from jax.experimental.pallas import tpu as pltpu
from jax.sharding import PartitionSpec as P

F32 = jnp.float32
BF16 = jnp.bfloat16
VMEM = pl.BlockSpec(memory_space=pltpu.VMEM)
SMEM = pl.BlockSpec(memory_space=pltpu.SMEM)
PARAMS = pltpu.CompilerParams(vmem_limit_bytes=32 * 1024 * 1024)

NEAR = (0, 1, 2, -1)
FAR = (0, 8, 16, -8)


def forward(pos, gathered, tile_rows, weight, partial, high, low):
    slots = pos.shape[1]
    for r in range(2):
        picked = jnp.concatenate([gathered[pos[r, s]] for s in range(slots)], axis=0)
        mixed = jnp.dot(tile_rows[r], picked, preferred_element_type=F32)
        top = mixed.astype(BF16)
        rest = (mixed - top.astype(F32)).astype(BF16)
        high[r] = top
        low[r] = rest
        partial[r] = jnp.dot(top, weight[...], preferred_element_type=F32) + jnp.dot(
            rest, weight[...], preferred_element_type=F32
        )


def backward(
    pos, mine, theirs, cot, tile_cols, weight, high, low, perm,
    activated, out0, out1, out2, out3, total,
):
    slots = pos.shape[1]
    tile = weight.shape[0]
    blocks = total.shape[0] - 1
    total[...] = jnp.zeros_like(total)
    grad = jnp.zeros((tile, tile), F32)
    for r in range(2):
        pre = mine[r] + theirs[1 - r]
        sig = jax.nn.sigmoid(pre)
        if r == 0:
            activated[...] = (pre * sig).astype(BF16)
        act_grad = (cot[r].astype(F32) * sig * (1.0 + pre * (1.0 - sig))).astype(BF16)
        moved = lax.dot_general(
            act_grad, weight[...], (((1,), (1,)), ((), ())), preferred_element_type=F32
        ).astype(BF16)
        for part in (high, low):
            grad += lax.dot_general(
                part[r], act_grad, (((0,), (0,)), ((), ())), preferred_element_type=F32
            )
        for s in range(slots):
            term = jnp.dot(
                tile_cols[r, pl.ds(s * tile, tile), :], moved, preferred_element_type=F32
            )
            total[pos[r, s]] += term
    top = grad.astype(BF16)
    rest = (grad - top.astype(F32)).astype(BF16)
    ordered_top = jnp.dot(perm[...], top, preferred_element_type=F32).astype(BF16)
    ordered_rest = jnp.dot(perm[...], rest, preferred_element_type=F32).astype(BF16)
    share = blocks // 4
    rows = tile // 4
    for a, out in enumerate((out0, out1, out2, out3)):
        for k in range(share):
            out[pl.ds(k * tile, tile), :] = total[a * share + k].astype(BF16)
        out[pl.ds(share * tile, rows), :] = ordered_top[a * rows : (a + 1) * rows]
        out[pl.ds(share * tile + rows, rows), :] = ordered_rest[a * rows : (a + 1) * rows]


def split(x):
    top = x.astype(BF16)
    return jnp.concatenate([top, (x - top.astype(F32)).astype(BF16)], 0)


def shards(features, weight, tiles, tile_cols, tile_counts, cotangent):
    feat = features[0]
    tile = feat.shape[0]
    slots = tiles.shape[2]
    wide = lax.axis_size("wide")
    chips = wide // 2
    w = lax.axis_index("wide")
    z, c = w // 2, w % 2
    sign = 1 - 2 * c

    def send(x, d):
        return lax.ppermute(
            x, "wide",
            [(2 * i + k, 2 * ((i + (d if k == 0 else -d)) % chips) + k) for i in range(chips) for k in range(2)],
        )

    def swap(x):
        return lax.ppermute(x, "wide", [(i, i ^ 1) for i in range(wide)])

    with jax.named_scope("gather_far"):
        held = jnp.stack([feat] + [send(feat, d) for d in FAR[1:]])
    with jax.named_scope("prepare"):
        rows = tiles[0].reshape(tile, slots * tile)
        both = jnp.concatenate([rows, cotangent[0]], axis=1)
        other = swap(both)
        tile_rows = jnp.stack([rows, other[:, : slots * tile]])
        tile_flip = jnp.swapaxes(tile_rows, 1, 2)
        cot = jnp.stack([cotangent[0], other[:, slots * tile :]])
        here = jnp.stack([w, w ^ 1])
        cols = tile_cols[0][here]
        counts = tile_counts[0][here]
        offset = (sign * (z - cols // 2)) % chips
        near = offset % 4
        far = ((offset + 1) // 4) % (chips // 4)
        place = near * (chips // 4) + (far % 2) * 4 + far // 2
        active = (jnp.arange(slots)[None, :] < counts[:, None]) & (cols % 2 == c)
        pos = jnp.where(active, place, chips).astype(jnp.int32)
        spot = jnp.arange(chips)
        near_at = jnp.where(spot // 8 == 3, -1, spot // 8)
        chip_at = (z - sign * (near_at + 4 * (spot % 8 // 4) + 8 * (spot % 4))) % chips
        row_share = tile // chips
        row_at = (chip_at[:, None] * row_share + jnp.arange(row_share)[None, :]).reshape(-1)
        perm = (row_at[:, None] == jnp.arange(tile)[None, :]).astype(BF16)
    with jax.named_scope("gather_middle"):
        held = jnp.concatenate([held, send(held, 4)], 0)
    with jax.named_scope("gather_near"):
        gathered = jnp.concatenate(
            [held] + [send(held, d) for d in NEAR[1:]] + [jnp.zeros((1, tile, tile), BF16)], 0
        )
    square = (2, tile, tile)
    partial, high, low = pl.pallas_call(
        forward,
        out_shape=[
            jax.ShapeDtypeStruct(square, F32),
            jax.ShapeDtypeStruct(square, BF16),
            jax.ShapeDtypeStruct(square, BF16),
        ],
        in_specs=[SMEM, VMEM, VMEM, VMEM],
        out_specs=[VMEM] * 3,
        compiler_params=PARAMS,
        name="forward",
    )(pos, gathered, tile_rows, weight)
    with jax.named_scope("pair"):
        theirs = swap(partial)
    share = chips // 4
    length = share * tile + tile // 2
    activated, part0, part1, part2, part3 = pl.pallas_call(
        backward,
        out_shape=[jax.ShapeDtypeStruct((tile, tile), BF16)]
        + [jax.ShapeDtypeStruct((length, tile), BF16)] * 4,
        in_specs=[SMEM] + [VMEM] * 8,
        out_specs=[VMEM] * 5,
        scratch_shapes=[pltpu.VMEM((chips + 1, tile, tile), F32)],
        compiler_params=PARAMS,
        name="backward",
    )(pos, partial, theirs, cot, tile_flip, weight, high, low, perm)

    def add(parts, count):
        wide_parts = [p.astype(F32) for p in parts]
        whole = sum(wide_parts[1:], wide_parts[0])
        main = whole[: count * tile].astype(BF16).reshape(count, tile, tile)
        grad = whole[count * tile :]
        half = grad.shape[0] // 2
        return main, grad[:half] + grad[half:]

    with jax.named_scope("scatter_near"):
        sent = [send(p, -d) for p, d in zip((part1, part2, part3), NEAR[1:])]
        main, grad = add([part0] + sent, share)
    with jax.named_scope("scatter_middle"):
        half = main.shape[0] // 2
        cut = grad.shape[0] // 2
        message = jnp.concatenate([main[half:].reshape(half * tile, tile), split(grad[cut:])], 0)
        keep = jnp.concatenate([main[:half].reshape(half * tile, tile), split(grad[:cut])], 0)
        main, grad = add([keep, send(message, -4)], half)
    with jax.named_scope("scatter_far"):
        parts = []
        for e, d in enumerate(FAR):
            message = jnp.concatenate([main[e], split(grad[e * row_share : (e + 1) * row_share])], 0)
            parts.append(send(message, -d) if d else message)
        wide_parts = [p.astype(F32) for p in parts]
        whole = sum(wide_parts[1:], wide_parts[0])
        feature_grad = whole[:tile].astype(BF16)
        grad = whole[tile : tile + row_share] + whole[tile + row_share :]
    with jax.named_scope("weight_sum"):
        mine_rows = row_share // 2
        grad = grad.reshape(2, mine_rows, tile)
        keep = lax.dynamic_index_in_dim(grad, c, 0, keepdims=False)
        give = lax.dynamic_index_in_dim(grad, 1 - c, 0, keepdims=False)
        grad = keep + swap(give)
        groups = lax.axis_size("narrow")
        copies = lax.all_to_all(
            jnp.broadcast_to(grad[None], (groups, mine_rows, tile)), "narrow", 0, 0
        )
        weight_grad = copies.sum(0)
    return (activated[None], feature_grad[None], weight_grad)


def solution(mesh):
    placed = (
        P("narrow", "wide", None),
        P(),
        P("narrow", "wide", None, None),
        P("narrow", None, None),
        P("narrow", None),
        P("narrow", "wide", None),
    )
    return jax.shard_map(
        shards,
        mesh=mesh,
        in_specs=placed,
        out_specs=(P("narrow", "wide", None), P("narrow", "wide", None), P("wide", None)),
        check_vma=False,
    )
```

time: 1230 us -> 180 us (0.15)
  waiting for transfers between devices: 1190 us -> 53.2 us
  starting transfers between devices: 0.12 us -> 109 us
  between operations: 13.9 us -> 1.09 us
    psum x1 -> x0, waiting for transfers between devices: 847 us -> none  [shards(): weight_total = lax.psum(weight_part, ('wide', 'narrow'))]
    reduce_scatter x1 -> x0, waiting for transfers between devices: 202 us -> none  [shards(): lax.psum_scatter(term, 'wide', scatter_dimension=0, tiled=True)]
    all_gather x1 -> x0, waiting for transfers between devices: 144 us -> none  [shards(): whole = lax.all_gather(projected, 'wide', axis=0, tiled=True)]
    ppermute x0 -> x17, starting transfers between devices: none -> 102 us  [the longest x14 87.4 us: send(): lax.ppermute(x, 'wide', [(2 * i + k, 2 * ((i + (d if k == 0 else -d)) % c...]
    ppermute x0 -> x17, waiting for transfers between devices: none -> 47.4 us  [the longest x14 45.8 us: send(): lax.ppermute(x, 'wide', [(2 * i + k, 2 * ((i + (d if k == 0 else -d)) % c...]
  transfers between devices with their start and end apart: 3 -> 18, of which waited for: 3 -> 12; matrix products, arithmetic and copies ran while one was open for 1% -> 6% of each run, Pallas kernels for 0% -> 0%
where the time goes in v1:
time: 180 us; the launch traced here: 179 us
  starting transfers between devices  109 us (61%)
  waiting for transfers between devices  53.2 us (30%)
  local copies, waits for them, and re-layouts  11.2 us (6%)
  Pallas kernels  3.03 us (2%)
    ppermute x14, starting transfers between devices, send(): lax.ppermute(x, 'wide', [(2 * i + k, 2 * ((i + (d if k == 0 else -d)) % c...  87.4 us
    ppermute x14, waiting for transfers between devices, send(): lax.ppermute(x, 'wide', [(2 * i + k, 2 * ((i + (d if k == 0 else -d)) % c...  45.8 us
    ppermute x3, starting transfers between devices, swap(): return lax.ppermute(x, 'wide', [(i, i ^ 1) for i in range(wide)])  15 us
    unnamed x18, local copies, waits for them, and re-layouts  7.56 us
    all_to_all x1, starting transfers between devices, shards(): lax.all_to_all(jnp.broadcast_to(grad[None], (groups, mine_rows, tile)), '...  6.55 us
    all_to_all x1, waiting for transfers between devices, shards(): lax.all_to_all(jnp.broadcast_to(grad[None], (groups, mine_rows, tile)), '...  5.81 us
  transfers between devices with their start and end apart: 18, of which 12 were waited for; matrix products, arithmetic and copies ran while one was open for 6% of the time, Pallas kernels for 0%

profile of v1, /device:TPU:1, one launch (start us, length us, event | category | flops | bytes accessed | tf_op | source)
XLA Modules:
  0.0 178.8 jit_solution(4288822789102434760)
XLA Ops:
  0.7 23.7 %collective-permute-start = (bf16[128,128]{1,0:T(8,128)(2,1)}, bf16[128,128]{1,0:T(8,128)(2,1)S(1)}, u32[]{:S(2)}, u32[]{:S(2)}) collective-permute-start(bf16[128,128]{1,0:T(8,128)(2,1)} %bitcast.37), channel_id=1, source_target_pairs={{0,256},{16,784},{32,288},{48,816},{64,320},{80,848},{96,352},{112... | collective-permute-start | bytes 98312 | tf_op jit(solution)/shard_map/gather_far/ppermute | solution.py:88
  24.4 7.9 %collective-permute-start.1 = (bf16[128,128]{1,0:T(8,128)(2,1)}, bf16[128,128]{1,0:T(8,128)(2,1)S(1)}, u32[]{:S(2)}, u32[]{:S(2)}) collective-permute-start(bf16[128,128]{1,0:T(8,128)(2,1)} %bitcast.38), channel_id=1, source_target_pairs={{0,512},{16,528},{32,544},{48,560},{64,576},{80,592},{96,608},{112... | collective-permute-start | bytes 98312 | tf_op jit(solution)/shard_map/gather_far/ppermute | solution.py:88
  32.3 12.1 %collective-permute-start.2 = (bf16[128,128]{1,0:T(8,128)(2,1)}, bf16[128,128]{1,0:T(8,128)(2,1)S(1)}, u32[]{:S(2)}, u32[]{:S(2)}) collective-permute-start(bf16[128,128]{1,0:T(8,128)(2,1)} %bitcast.39), channel_id=1, source_target_pairs={{0,768},{16,272},{32,800},{48,304},{64,832},{80,336},{96,864},{112... | collective-permute-start | bytes 98312 | tf_op jit(solution)/shard_map/gather_far/ppermute | solution.py:88
  44.3 1.2 copy.31
  46.4 3.4 %collective-permute-start.7 = (bf16[128,1152]{0,1:T(8,128)(2,1)S(1)}, bf16[128,1152]{0,1:T(8,128)(2,1)S(1)}, u32[]{:S(2)}, u32[]{:S(2)}) collective-permute-start(bf16[128,1152]{0,1:T(8,128)(2,1)S(1)} %pad_maximum_fusion.1), channel_id=1, source_target_pairs={{0,16},{16,0},{32,48},{48,32},{64,80},{80,64},{96,112},{112,96},{1... | collective-permute-start | bytes 884744 | tf_op jit(solution)/shard_map/prepare/ppermute | solution.py:94
  52.3 1.9 %collective-permute-start.3 = (bf16[4,128,128]{2,1,0:T(8,128)(2,1)S(1)}, bf16[4,128,128]{2,1,0:T(8,128)(2,1)S(1)}, u32[]{:S(2)}, u32[]{:S(2)}) collective-permute-start(bf16[4,128,128]{2,1,0:T(8,128)(2,1)S(1)} %pad_maximum_fusion.3), channel_id=1, source_target_pairs={{0,128},{16,912},{32,160},{48,944},{64,192},{80,976},{96,224},{112... | collective-permute-start | bytes 393224 | tf_op jit(solution)/shard_map/gather_middle/ppermute | solution.py:88
  56.1 10.0 %collective-permute-done.3 = bf16[4,128,128]{2,1,0:T(8,128)(2,1)S(1)} collective-permute-done((bf16[4,128,128]{2,1,0:T(8,128)(2,1)S(1)}, bf16[4,128,128]{2,1,0:T(8,128)(2,1)S(1)}, u32[]{:S(2)}, u32[]{:S(2)}) %collective-permute-start.3) | collective-permute-done | bytes 131104 | tf_op jit(solution)/shard_map/gather_middle/ppermute | solution.py:88
  66.8 1.9 %collective-permute-start.4 = (bf16[8,128,128]{2,1,0:T(8,128)(2,1)}, bf16[8,128,128]{2,1,0:T(8,128)(2,1)}, u32[]{:S(2)}, u32[]{:S(2)}) collective-permute-start(bf16[8,128,128]{2,1,0:T(8,128)(2,1)} %get-tuple-element.43), channel_id=1, source_target_pairs={{0,32},{16,1008},{32,64},{48,16},{64,96},{80,48},{96,128},{112,80}... | collective-permute-start | bytes 786440 | tf_op jit(solution)/shard_map/gather_near/ppermute | solution.py:88
  68.7 1.9 %collective-permute-start.5 = (bf16[8,128,128]{2,1,0:T(8,128)(2,1)}, bf16[8,128,128]{2,1,0:T(8,128)(2,1)}, u32[]{:S(2)}, u32[]{:S(2)}) collective-permute-start(bf16[8,128,128]{2,1,0:T(8,128)(2,1)} %get-tuple-element.43), channel_id=1, source_target_pairs={{0,64},{16,976},{32,96},{48,1008},{64,128},{80,16},{96,160},{112,4... | collective-permute-start | bytes 786440 | tf_op jit(solution)/shard_map/gather_near/ppermute | solution.py:88
  70.6 3.4 %collective-permute-start.6 = (bf16[8,128,128]{2,1,0:T(8,128)(2,1)}, bf16[8,128,128]{2,1,0:T(8,128)(2,1)}, u32[]{:S(2)}, u32[]{:S(2)}) collective-permute-start(bf16[8,128,128]{2,1,0:T(8,128)(2,1)} %get-tuple-element.43), channel_id=1, source_target_pairs={{0,992},{16,48},{32,0},{48,80},{64,32},{80,112},{96,64},{112,144},... | collective-permute-start | bytes 786440 | tf_op jit(solution)/shard_map/gather_near/ppermute | solution.py:88
  74.5 1.0 constant_dynamic-update-slice_fusion.8
  75.5 5.1 %collective-permute-done.5 = bf16[8,128,128]{2,1,0:T(8,128)(2,1)} collective-permute-done((bf16[8,128,128]{2,1,0:T(8,128)(2,1)}, bf16[8,128,128]{2,1,0:T(8,128)(2,1)}, u32[]{:S(2)}, u32[]{:S(2)}) %collective-permute-start.5) | collective-permute-done | bytes 262176 | tf_op jit(solution)/shard_map/gather_near/ppermute | solution.py:88
  81.6 1.4 collective-permute-done.6
  83.0 1.0 constant_dynamic-update-slice_fusion.6
  84.0 1.1 forward.1
  85.2 5.9 %collective-permute-start.8 = (f32[2,128,128]{2,1,0:T(8,128)S(1)}, f32[2,128,128]{2,1,0:T(8,128)S(1)}, u32[]{:S(2)}, u32[]{:S(2)}) collective-permute-start(f32[2,128,128]{2,1,0:T(8,128)S(1)} %get-tuple-element.11.mine), channel_id=1, source_target_pairs={{0,16},{16,0},{32,48},{48,32},{64,80},{80,64},{96,112},{112,96},{1... | collective-permute-start | bytes 393224 | tf_op jit(solution)/shard_map/pair/ppermute | solution.py:94
  92.0 1.9 %backward.1 = (bf16[128,128]{1,0:T(8,128)(2,1)}, bf16[1088,128]{1,0:T(8,128)(2,1)S(1)}, bf16[1088,128]{1,0:T(8,128)(2,1)S(1)}, bf16[1088,128]{1,0:T(8,128)(2,1)S(1)}, bf16[1088,128]{1,0:T(8,128)(2,1)S(1)}) custom-call(s32[2,8]{1,0:T(2,128)S(1)} %and_select_fusion.12.pos, f32[2,128,128]{2,1,0:T(8,128)S(1)} %get-tuple-element.11.mine, ...), custom_call_target="tpu_custom_call" | custom-call | tf_op jit(solution)/shard_map/backward/pallas_call | solution.py:143
  93.9 1.9 %collective-permute-start.10 = (bf16[1088,128]{1,0:T(8,128)(2,1)S(1)}, bf16[1088,128]{1,0:T(8,128)(2,1)S(1)}, u32[]{:S(2)}, u32[]{:S(2)}) collective-permute-start(bf16[1088,128]{1,0:T(8,128)(2,1)S(1)} %get-tuple-element.17), channel_id=1, source_target_pairs={{0,960},{16,80},{32,992},{48,112},{64,0},{80,144},{96,32},{112,176... | collective-permute-start | bytes 835592 | tf_op jit(solution)/shard_map/scatter_near/ppermute | solution.py:88
  95.9 3.9 %collective-permute-start.11 = (bf16[1088,128]{1,0:T(8,128)(2,1)S(1)}, bf16[1088,128]{1,0:T(8,128)(2,1)S(1)}, u32[]{:S(2)}, u32[]{:S(2)}) collective-permute-start(bf16[1088,128]{1,0:T(8,128)(2,1)S(1)} %get-tuple-element.18), channel_id=1, source_target_pairs={{0,32},{16,1008},{32,64},{48,16},{64,96},{80,48},{96,128},{112,80}... | collective-permute-start | bytes 835592 | tf_op jit(solution)/shard_map/scatter_near/ppermute | solution.py:88
  99.8 1.9 %collective-permute-start.9 = (bf16[1088,128]{1,0:T(8,128)(2,1)S(1)}, bf16[1088,128]{1,0:T(8,128)(2,1)S(1)}, u32[]{:S(2)}, u32[]{:S(2)}) collective-permute-start(bf16[1088,128]{1,0:T(8,128)(2,1)S(1)} %get-tuple-element.16), channel_id=1, source_target_pairs={{0,992},{16,48},{32,0},{48,80},{64,32},{80,112},{96,64},{112,144},... | collective-permute-start | bytes 835592 | tf_op jit(solution)/shard_map/scatter_near/ppermute | solution.py:88
  101.7 4.7 %collective-permute-done.10 = bf16[1088,128]{1,0:T(8,128)(2,1)S(1)} collective-permute-done((bf16[1088,128]{1,0:T(8,128)(2,1)S(1)}, bf16[1088,128]{1,0:T(8,128)(2,1)S(1)}, u32[]{:S(2)}, u32[]{:S(2)}) %collective-permute-start.10) | collective-permute-done | bytes 278560 | tf_op jit(solution)/shard_map/scatter_near/ppermute | solution.py:88
  106.4 2.8 %collective-permute-done.11 = bf16[1088,128]{1,0:T(8,128)(2,1)S(1)} collective-permute-done((bf16[1088,128]{1,0:T(8,128)(2,1)S(1)}, bf16[1088,128]{1,0:T(8,128)(2,1)S(1)}, u32[]{:S(2)}, u32[]{:S(2)}) %collective-permute-start.11) | collective-permute-done | bytes 278560 | tf_op jit(solution)/shard_map/scatter_near/ppermute | solution.py:88
  109.3 1.6 collective-permute-done.9
  111.1 4.5 %collective-permute-start.12 = (bf16[544,128]{1,0:T(8,128)(2,1)S(1)}, bf16[544,128]{1,0:T(8,128)(2,1)S(1)}, u32[]{:S(2)}, u32[]{:S(2)}) collective-permute-start(bf16[544,128]{1,0:T(8,128)(2,1)S(1)} %pad_maximum_fusion.2), channel_id=1, source_target_pairs={{0,896},{16,144},{32,928},{48,176},{64,960},{80,208},{96,992},{112... | collective-permute-start | bytes 417800 | tf_op jit(solution)/shard_map/scatter_middle/ppermute | solution.py:88
  115.6 9.6 %collective-permute-done.12 = bf16[544,128]{1,0:T(8,128)(2,1)S(1)} collective-permute-done((bf16[544,128]{1,0:T(8,128)(2,1)S(1)}, bf16[544,128]{1,0:T(8,128)(2,1)S(1)}, u32[]{:S(2)}, u32[]{:S(2)}) %collective-permute-start.12) | collective-permute-done | bytes 139296 | tf_op jit(solution)/shard_map/scatter_middle/ppermute | solution.py:88
  125.3 8.7 %collective-permute-start.13 = (bf16[136,128]{1,0:T(8,128)(2,1)S(1)}, bf16[136,128]{1,0:T(8,128)(2,1)S(1)}, u32[]{:S(2)}, u32[]{:S(2)}) collective-permute-start(bf16[136,128]{1,0:T(8,128)(2,1)S(1)} %pad_maximum_fusion.5), channel_id=1, source_target_pairs={{0,768},{16,272},{32,800},{48,304},{64,832},{80,336},{96,864},{112... | collective-permute-start | bytes 104456 | tf_op jit(solution)/shard_map/scatter_far/ppermute | solution.py:88
  134.0 7.5 %collective-permute-start.14 = (bf16[136,128]{1,0:T(8,128)(2,1)S(1)}, bf16[136,128]{1,0:T(8,128)(2,1)S(1)}, u32[]{:S(2)}, u32[]{:S(2)}) collective-permute-start(bf16[136,128]{1,0:T(8,128)(2,1)S(1)} %pad_maximum_fusion.6), channel_id=1, source_target_pairs={{0,512},{16,528},{32,544},{48,560},{64,576},{80,592},{96,608},{112... | collective-permute-start | bytes 104456 | tf_op jit(solution)/shard_map/scatter_far/ppermute | solution.py:88
  141.5 6.3 %collective-permute-start.15 = (bf16[136,128]{1,0:T(8,128)(2,1)S(1)}, bf16[136,128]{1,0:T(8,128)(2,1)S(1)}, u32[]{:S(2)}, u32[]{:S(2)}) collective-permute-start(bf16[136,128]{1,0:T(8,128)(2,1)S(1)} %pad_maximum_fusion.7), channel_id=1, source_target_pairs={{0,256},{16,784},{32,288},{48,816},{64,320},{80,848},{96,352},{112... | collective-permute-start | bytes 104456 | tf_op jit(solution)/shard_map/scatter_far/ppermute | solution.py:88
  147.7 10.3 %collective-permute-done.14 = bf16[136,128]{1,0:T(8,128)(2,1)S(1)} collective-permute-done((bf16[136,128]{1,0:T(8,128)(2,1)S(1)}, bf16[136,128]{1,0:T(8,128)(2,1)S(1)}, u32[]{:S(2)}, u32[]{:S(2)}) %collective-permute-start.14) | collective-permute-done | bytes 34848 | tf_op jit(solution)/shard_map/scatter_far/ppermute | solution.py:88
  158.1 5.7 %collective-permute-start.16 = (f32[2,128]{1,0:T(2,128)S(1)}, f32[2,128]{1,0:T(2,128)S(1)}, u32[]{:S(2)}, u32[]{:S(2)}) collective-permute-start(f32[2,128]{1,0:T(2,128)S(1)} %dynamic-slice_bitcast_fusion), channel_id=1, source_target_pairs={{0,16},{16,0},{32,48},{48,32},{64,80},{80,64},{96,112},{112,96},{1... | collective-permute-start | bytes 3080 | tf_op jit(solution)/shard_map/weight_sum/ppermute | solution.py:94
  165.2 6.5 %all-to-all-start = ((f32[16,2,128]{2,1,0:T(2,128)}), f32[16,2,128]{2,1,0:T(2,128)S(1)}, u32[]{:S(2)}, u32[]{:S(2)}) async-start(f32[16,2,128]{2,1,0:T(2,128)} %broadcast_in_dim.15), calls=%async_computation | async-start | bytes 32768 | tf_op jit(solution)/shard_map/weight_sum/all_to_all | solution.py:187
  172.4 5.8 %all-to-all-done = f32[16,2,128]{2,1,0:T(2,128)S(1)} async-done(((f32[16,2,128]{2,1,0:T(2,128)}), f32[16,2,128]{2,1,0:T(2,128)S(1)}, u32[]{:S(2)}, u32[]{:S(2)}) %all-to-all-start) | async-done | bytes 16416 | tf_op jit(solution)/shard_map/weight_sum/all_to_all | solution.py:187
  (62 shorter events, 11.2 us)
Async XLA Ops:
  0.6 50.0 %copy-start = (s32[1,64]{1,0:T(1,128)S(1)}, s32[1,64]{1,0:T(1,128)}, u32[]{:S(2)}) copy-start(s32[1,64]{1,0:T(1,128)} %param.10) | copy-start | bytes 772
  0.6 51.0 %copy-start.2 = (bf16[1,128,128]{2,1,0:T(8,128)(2,1)S(1)}, bf16[1,128,128]{2,1,0:T(8,128)(2,1)}, u32[]{:S(2)}) copy-start(bf16[1,128,128]{2,1,0:T(8,128)(2,1)} %param.6) | copy-start | bytes 98308
  0.7 49.3 %copy-start.3 = (s32[1,64,8]{1,2,0:T(8,128)S(1)}, s32[1,64,8]{1,2,0:T(8,128)}, u32[]{:S(2)}) copy-start(s32[1,64,8]{1,2,0:T(8,128)} %param.9) | copy-start | bytes 6148
  0.7 51.6 %collective-permute-start = (bf16[128,128]{1,0:T(8,128)(2,1)}, bf16[128,128]{1,0:T(8,128)(2,1)S(1)}, u32[]{:S(2)}, u32[]{:S(2)}) collective-permute-start(bf16[128,128]{1,0:T(8,128)(2,1)} %bitcast.37), channel_id=1, source_target_pairs={{0,256},{16,784},{32,288},{48,816},{64,320},{80,848},{96,352},{112... | collective-permute-start | bytes 98312 | tf_op jit(solution)/shard_map/gather_far/ppermute | solution.py:88
  24.4 27.9 %collective-permute-start.1 = (bf16[128,128]{1,0:T(8,128)(2,1)}, bf16[128,128]{1,0:T(8,128)(2,1)S(1)}, u32[]{:S(2)}, u32[]{:S(2)}) collective-permute-start(bf16[128,128]{1,0:T(8,128)(2,1)} %bitcast.38), channel_id=1, source_target_pairs={{0,512},{16,528},{32,544},{48,560},{64,576},{80,592},{96,608},{112... | collective-permute-start | bytes 98312 | tf_op jit(solution)/shard_map/gather_far/ppermute | solution.py:88
  32.3 20.0 %collective-permute-start.2 = (bf16[128,128]{1,0:T(8,128)(2,1)}, bf16[128,128]{1,0:T(8,128)(2,1)S(1)}, u32[]{:S(2)}, u32[]{:S(2)}) collective-permute-start(bf16[128,128]{1,0:T(8,128)(2,1)} %bitcast.39), channel_id=1, source_target_pairs={{0,768},{16,272},{32,800},{48,304},{64,832},{80,336},{96,864},{112... | collective-permute-start | bytes 98312 | tf_op jit(solution)/shard_map/gather_far/ppermute | solution.py:88
  46.4 27.6 %collective-permute-start.7 = (bf16[128,1152]{0,1:T(8,128)(2,1)S(1)}, bf16[128,1152]{0,1:T(8,128)(2,1)S(1)}, u32[]{:S(2)}, u32[]{:S(2)}) collective-permute-start(bf16[128,1152]{0,1:T(8,128)(2,1)S(1)} %pad_maximum_fusion.1), channel_id=1, source_target_pairs={{0,16},{16,0},{32,48},{48,32},{64,80},{80,64},{96,112},{112,96},{1... | collective-permute-start | bytes 884744 | tf_op jit(solution)/shard_map/prepare/ppermute | solution.py:94
  52.3 13.8 %collective-permute-start.3 = (bf16[4,128,128]{2,1,0:T(8,128)(2,1)S(1)}, bf16[4,128,128]{2,1,0:T(8,128)(2,1)S(1)}, u32[]{:S(2)}, u32[]{:S(2)}) collective-permute-start(bf16[4,128,128]{2,1,0:T(8,128)(2,1)S(1)} %pad_maximum_fusion.3), channel_id=1, source_target_pairs={{0,128},{16,912},{32,160},{48,944},{64,192},{80,976},{96,224},{112... | collective-permute-start | bytes 393224 | tf_op jit(solution)/shard_map/gather_middle/ppermute | solution.py:88
  66.8 7.7 %collective-permute-start.4 = (bf16[8,128,128]{2,1,0:T(8,128)(2,1)}, bf16[8,128,128]{2,1,0:T(8,128)(2,1)}, u32[]{:S(2)}, u32[]{:S(2)}) collective-permute-start(bf16[8,128,128]{2,1,0:T(8,128)(2,1)} %get-tuple-element.43), channel_id=1, source_target_pairs={{0,32},{16,1008},{32,64},{48,16},{64,96},{80,48},{96,128},{112,80}... | collective-permute-start | bytes 786440 | tf_op jit(solution)/shard_map/gather_near/ppermute | solution.py:88
  68.7 11.9 %collective-permute-start.5 = (bf16[8,128,128]{2,1,0:T(8,128)(2,1)}, bf16[8,128,128]{2,1,0:T(8,128)(2,1)}, u32[]{:S(2)}, u32[]{:S(2)}) collective-permute-start(bf16[8,128,128]{2,1,0:T(8,128)(2,1)} %get-tuple-element.43), channel_id=1, source_target_pairs={{0,64},{16,976},{32,96},{48,1008},{64,128},{80,16},{96,160},{112,4... | collective-permute-start | bytes 786440 | tf_op jit(solution)/shard_map/gather_near/ppermute | solution.py:88
  70.6 12.4 %collective-permute-start.6 = (bf16[8,128,128]{2,1,0:T(8,128)(2,1)}, bf16[8,128,128]{2,1,0:T(8,128)(2,1)}, u32[]{:S(2)}, u32[]{:S(2)}) collective-permute-start(bf16[8,128,128]{2,1,0:T(8,128)(2,1)} %get-tuple-element.43), channel_id=1, source_target_pairs={{0,992},{16,48},{32,0},{48,80},{64,32},{80,112},{96,64},{112,144},... | collective-permute-start | bytes 786440 | tf_op jit(solution)/shard_map/gather_near/ppermute | solution.py:88
  74.1 9.9 %copy-start.1 = (bf16[128,128]{1,0:T(8,128)(2,1)S(1)}, bf16[128,128]{1,0:T(8,128)(2,1)}, u32[]{:S(2)}) copy-start(bf16[128,128]{1,0:T(8,128)(2,1)} %weight.3) | copy-start | bytes 98308
  85.2 6.9 %collective-permute-start.8 = (f32[2,128,128]{2,1,0:T(8,128)S(1)}, f32[2,128,128]{2,1,0:T(8,128)S(1)}, u32[]{:S(2)}, u32[]{:S(2)}) collective-permute-start(f32[2,128,128]{2,1,0:T(8,128)S(1)} %get-tuple-element.11.mine), channel_id=1, source_target_pairs={{0,16},{16,0},{32,48},{48,32},{64,80},{80,64},{96,112},{112,96},{1... | collective-permute-start | bytes 393224 | tf_op jit(solution)/shard_map/pair/ppermute | solution.py:94
  93.9 12.5 %collective-permute-start.10 = (bf16[1088,128]{1,0:T(8,128)(2,1)S(1)}, bf16[1088,128]{1,0:T(8,128)(2,1)S(1)}, u32[]{:S(2)}, u32[]{:S(2)}) collective-permute-start(bf16[1088,128]{1,0:T(8,128)(2,1)S(1)} %get-tuple-element.17), channel_id=1, source_target_pairs={{0,960},{16,80},{32,992},{48,112},{64,0},{80,144},{96,32},{112,176... | collective-permute-start | bytes 835592 | tf_op jit(solution)/shard_map/scatter_near/ppermute | solution.py:88
  95.9 13.4 %collective-permute-start.11 = (bf16[1088,128]{1,0:T(8,128)(2,1)S(1)}, bf16[1088,128]{1,0:T(8,128)(2,1)S(1)}, u32[]{:S(2)}, u32[]{:S(2)}) collective-permute-start(bf16[1088,128]{1,0:T(8,128)(2,1)S(1)} %get-tuple-element.18), channel_id=1, source_target_pairs={{0,32},{16,1008},{32,64},{48,16},{64,96},{80,48},{96,128},{112,80}... | collective-permute-start | bytes 835592 | tf_op jit(solution)/shard_map/scatter_near/ppermute | solution.py:88
  99.8 11.1 %collective-permute-start.9 = (bf16[1088,128]{1,0:T(8,128)(2,1)S(1)}, bf16[1088,128]{1,0:T(8,128)(2,1)S(1)}, u32[]{:S(2)}, u32[]{:S(2)}) collective-permute-start(bf16[1088,128]{1,0:T(8,128)(2,1)S(1)} %get-tuple-element.16), channel_id=1, source_target_pairs={{0,992},{16,48},{32,0},{48,80},{64,32},{80,112},{96,64},{112,144},... | collective-permute-start | bytes 835592 | tf_op jit(solution)/shard_map/scatter_near/ppermute | solution.py:88
  111.1 14.1 %collective-permute-start.12 = (bf16[544,128]{1,0:T(8,128)(2,1)S(1)}, bf16[544,128]{1,0:T(8,128)(2,1)S(1)}, u32[]{:S(2)}, u32[]{:S(2)}) collective-permute-start(bf16[544,128]{1,0:T(8,128)(2,1)S(1)} %pad_maximum_fusion.2), channel_id=1, source_target_pairs={{0,896},{16,144},{32,928},{48,176},{64,960},{80,208},{96,992},{112... | collective-permute-start | bytes 417800 | tf_op jit(solution)/shard_map/scatter_middle/ppermute | solution.py:88
  125.3 22.4 %collective-permute-start.13 = (bf16[136,128]{1,0:T(8,128)(2,1)S(1)}, bf16[136,128]{1,0:T(8,128)(2,1)S(1)}, u32[]{:S(2)}, u32[]{:S(2)}) collective-permute-start(bf16[136,128]{1,0:T(8,128)(2,1)S(1)} %pad_maximum_fusion.5), channel_id=1, source_target_pairs={{0,768},{16,272},{32,800},{48,304},{64,832},{80,336},{96,864},{112... | collective-permute-start | bytes 104456 | tf_op jit(solution)/shard_map/scatter_far/ppermute | solution.py:88
  134.0 24.1 %collective-permute-start.14 = (bf16[136,128]{1,0:T(8,128)(2,1)S(1)}, bf16[136,128]{1,0:T(8,128)(2,1)S(1)}, u32[]{:S(2)}, u32[]{:S(2)}) collective-permute-start(bf16[136,128]{1,0:T(8,128)(2,1)S(1)} %pad_maximum_fusion.6), channel_id=1, source_target_pairs={{0,512},{16,528},{32,544},{48,560},{64,576},{80,592},{96,608},{112... | collective-permute-start | bytes 104456 | tf_op jit(solution)/shard_map/scatter_far/ppermute | solution.py:88
  141.5 16.6 %collective-permute-start.15 = (bf16[136,128]{1,0:T(8,128)(2,1)S(1)}, bf16[136,128]{1,0:T(8,128)(2,1)S(1)}, u32[]{:S(2)}, u32[]{:S(2)}) collective-permute-start(bf16[136,128]{1,0:T(8,128)(2,1)S(1)} %pad_maximum_fusion.7), channel_id=1, source_target_pairs={{0,256},{16,784},{32,288},{48,816},{64,320},{80,848},{96,352},{112... | collective-permute-start | bytes 104456 | tf_op jit(solution)/shard_map/scatter_far/ppermute | solution.py:88
  158.1 6.5 %collective-permute-start.16 = (f32[2,128]{1,0:T(2,128)S(1)}, f32[2,128]{1,0:T(2,128)S(1)}, u32[]{:S(2)}, u32[]{:S(2)}) collective-permute-start(f32[2,128]{1,0:T(2,128)S(1)} %dynamic-slice_bitcast_fusion), channel_id=1, source_target_pairs={{0,16},{16,0},{32,48},{48,32},{64,80},{80,64},{96,112},{112,96},{1... | collective-permute-start | bytes 3080 | tf_op jit(solution)/shard_map/weight_sum/ppermute | solution.py:94
  165.2 13.0 %all-to-all-start = ((f32[16,2,128]{2,1,0:T(2,128)}), f32[16,2,128]{2,1,0:T(2,128)S(1)}, u32[]{:S(2)}, u32[]{:S(2)}) async-start(f32[16,2,128]{2,1,0:T(2,128)} %broadcast_in_dim.15), calls=%async_computation | async-start | bytes 32768 | tf_op jit(solution)/shard_map/weight_sum/all_to_all | solution.py:187

commit v2 on v1

v2 whole, which is shorter than its diff:
```python
import jax
import jax.numpy as jnp
from jax import lax
from jax.experimental import pallas as pl
from jax.experimental.pallas import tpu as pltpu
from jax.sharding import PartitionSpec as P

F32 = jnp.float32
BF16 = jnp.bfloat16
VMEM = pl.BlockSpec(memory_space=pltpu.VMEM)
SMEM = pl.BlockSpec(memory_space=pltpu.SMEM)
PARAMS = pltpu.CompilerParams(vmem_limit_bytes=32 * 1024 * 1024)

NEAR = (0, 1, 2, -1)
CLASSES = len(NEAR)


def forward(pos, held0, held1, held2, held3, tile_rows, mixed):
    slots = pos.shape[1]
    share = held0.shape[0]
    for r in range(2):
        picked = []
        for s in range(slots):
            near, far = pos[r, s] // share, pos[r, s] % share
            block = jnp.zeros(held0.shape[1:], BF16)
            for a, held in enumerate((held0, held1, held2, held3)):
                block = jnp.where(near == a, held[far], block)
            picked.append(block)
        mixed[r] = jnp.dot(tile_rows[r], jnp.concatenate(picked, 0), preferred_element_type=F32)


def backward(
    pos, mine, theirs, cot, tile_cols, weight, perm,
    activated, out0, out1, out2, out3, total,
):
    slots = pos.shape[1]
    tile = weight.shape[0]
    blocks = total.shape[0] - 1
    total[...] = jnp.zeros_like(total)
    grad = jnp.zeros((tile, tile), F32)
    for r in range(2):
        mixed = mine[r] + theirs[1 - r]
        high = mixed.astype(BF16)
        low = (mixed - high.astype(F32)).astype(BF16)
        pre = jnp.dot(high, weight[...], preferred_element_type=F32) + jnp.dot(
            low, weight[...], preferred_element_type=F32
        )
        sig = jax.nn.sigmoid(pre)
        if r == 0:
            activated[...] = (pre * sig).astype(BF16)
        act_grad = (cot[r].astype(F32) * sig * (1.0 + pre * (1.0 - sig))).astype(BF16)
        moved = lax.dot_general(
            act_grad, weight[...], (((1,), (1,)), ((), ())), preferred_element_type=F32
        ).astype(BF16)
        for part in (high, low):
            grad += lax.dot_general(
                part, act_grad, (((0,), (0,)), ((), ())), preferred_element_type=F32
            )
        for s in range(slots):
            term = jnp.dot(
                tile_cols[r, pl.ds(s * tile, tile), :], moved, preferred_element_type=F32
            )
            total[pos[r, s]] += term
    top = grad.astype(BF16)
    rest = (grad - top.astype(F32)).astype(BF16)
    ordered_top = jnp.dot(perm[...], top, preferred_element_type=F32).astype(BF16)
    ordered_rest = jnp.dot(perm[...], rest, preferred_element_type=F32).astype(BF16)
    share = blocks // CLASSES
    rows = perm.shape[0] // CLASSES
    for a, out in enumerate((out0, out1, out2, out3)):
        for k in range(share):
            out[pl.ds(k * tile, tile), :] = total[a * share + k].astype(BF16)
        out[pl.ds(share * tile, rows), :] = ordered_top[a * rows : (a + 1) * rows]
        out[pl.ds(share * tile + rows, rows), :] = ordered_rest[a * rows : (a + 1) * rows]


def shards(features, weight, tiles, tile_cols, tile_counts, cotangent):
    feat = features[0]
    tile = feat.shape[0]
    slots = tiles.shape[2]
    wide = lax.axis_size("wide")
    chips = wide // 2
    share = chips // CLASSES
    w = lax.axis_index("wide")
    z, c = w // 2, w % 2
    sign = 1 - 2 * c

    def send(x, d):
        return lax.ppermute(
            x, "wide",
            [(2 * i + k, 2 * ((i + (d if k == 0 else -d)) % chips) + k) for i in range(chips) for k in range(2)],
        )

    def swap(x):
        return lax.ppermute(x, "wide", [(i, i ^ 1) for i in range(wide)])

    def within_class(x):
        return lax.all_to_all(
            x, "wide", 0, 0,
            axis_index_groups=[
                [2 * (CLASSES * m + k) + core for m in range(share)] for k in range(CLASSES) for core in range(2)
            ],
        )

    with jax.named_scope("gather_far"):
        held = within_class(jnp.broadcast_to(feat[None], (share, tile, tile)))
    with jax.named_scope("prepare"):
        rows = tiles[0].reshape(tile, slots * tile)
        both = jnp.concatenate([rows, cotangent[0]], axis=1)
        other = swap(both)
        tile_rows = jnp.stack([rows, other[:, : slots * tile]])
        tile_flip = jnp.swapaxes(tile_rows, 1, 2)
        cot = jnp.stack([cotangent[0], other[:, slots * tile :]])
        here = jnp.stack([w, w ^ 1])
        cols = tile_cols[0][here]
        counts = tile_counts[0][here]
        chip = cols // 2
        place = (sign * (z - chip)) % CLASSES * share + chip // CLASSES
        active = (jnp.arange(slots)[None, :] < counts[:, None]) & (cols % 2 == c)
        pos = jnp.where(active, place, chips).astype(jnp.int32)
        spot = jnp.arange(chips)
        chip_at = (z - sign * (spot // share)) % CLASSES + CLASSES * (spot % share)
        row_share = tile // wide
        row_at = ((2 * chip_at + c)[:, None] * row_share + jnp.arange(row_share)[None, :]).reshape(-1)
        perm = (row_at[:, None] == jnp.arange(tile)[None, :]).astype(BF16)
    with jax.named_scope("gather_near"):
        gathered = [held] + [send(held, d) for d in NEAR[1:]]
    mixed = pl.pallas_call(
        forward,
        out_shape=jax.ShapeDtypeStruct((2, tile, tile), F32),
        in_specs=[SMEM] + [VMEM] * 5,
        out_specs=VMEM,
        compiler_params=PARAMS,
        name="forward",
    )(pos, *gathered, tile_rows)
    with jax.named_scope("pair"):
        theirs = swap(mixed)
    extra = share * row_share
    activated, *parts = pl.pallas_call(
        backward,
        out_shape=[jax.ShapeDtypeStruct((tile, tile), BF16)]
        + [jax.ShapeDtypeStruct((share * tile + 2 * extra, tile), BF16)] * CLASSES,
        in_specs=[SMEM] + [VMEM] * 6,
        out_specs=[VMEM] * (1 + CLASSES),
        scratch_shapes=[pltpu.VMEM((chips + 1, tile, tile), F32)],
        compiler_params=PARAMS,
        name="backward",
    )(pos, mixed, theirs, cot, tile_flip, weight, perm)
    with jax.named_scope("scatter_near"):
        whole = parts[0].astype(F32)
        for part, d in zip(parts[1:], NEAR[1:]):
            whole += send(part, -d).astype(F32)
        main = whole[: share * tile].reshape(share, tile, tile).astype(BF16)
        grad = whole[share * tile : share * tile + extra] + whole[share * tile + extra :]
        grad = grad.reshape(share, row_share, tile)
    with jax.named_scope("scatter_far"):
        top = grad.astype(BF16)
        rest = (grad - top.astype(F32)).astype(BF16)
        whole = within_class(jnp.concatenate([main, top, rest], 1)).astype(F32).sum(0)
        feature_grad = whole[:tile].astype(BF16)
        grad = whole[tile : tile + row_share] + whole[tile + row_share :]
    with jax.named_scope("weight_sum"):
        groups = lax.axis_size("narrow")
        copies = lax.all_to_all(
            jnp.broadcast_to(grad[None], (groups, row_share, tile)), "narrow", 0, 0
        )
        weight_grad = copies.sum(0)
    return (activated[None], feature_grad[None], weight_grad)


def solution(mesh):
    placed = (
        P("narrow", "wide", None),
        P(),
        P("narrow", "wide", None, None),
        P("narrow", None, None),
        P("narrow", None),
        P("narrow", "wide", None),
    )
    return jax.shard_map(
        shards,
        mesh=mesh,
        in_specs=placed,
        out_specs=(P("narrow", "wide", None), P("narrow", "wide", None), P("wide", None)),
        check_vma=False,
    )
```

time: 180 us -> 176 us (0.978)
  the two profiles are of different devices: /device:TPU:1 before, /device:TPU:64 now
where the time goes in v2:
time: 176 us
  waiting for transfers between devices  60 us (34%)
  starting transfers between devices  57.8 us (33%)
  blocking collectives  46.5 us (26%)
  local copies, waits for them, and re-layouts  6.05 us (3%)
  Pallas kernels  3.19 us (2%)
    all_to_all x1, blocking collectives, within_class(): lax.all_to_all(x, 'wide', 0, 0, axis_index_groups=[[2 * (CLASSES * m + k)...  46.5 us
    all_to_all x1, waiting for transfers between devices, within_class(): lax.all_to_all(x, 'wide', 0, 0, axis_index_groups=[[2 * (CLASSES * m + k)...  36.1 us
    all_to_all x1, starting transfers between devices, within_class(): lax.all_to_all(x, 'wide', 0, 0, axis_index_groups=[[2 * (CLASSES * m + k)...  26.7 us
    ppermute x6, starting transfers between devices, send(): lax.ppermute(x, 'wide', [(2 * i + k, 2 * ((i + (d if k == 0 else -d)) % c...  19 us
    ppermute x6, waiting for transfers between devices, send(): lax.ppermute(x, 'wide', [(2 * i + k, 2 * ((i + (d if k == 0 else -d)) % c...  16.2 us
    all_to_all x1, starting transfers between devices, shards(): lax.all_to_all(jnp.broadcast_to(grad[None], (groups, row_share, tile)), '...  7.04 us
    all_to_all x1, waiting for transfers between devices, shards(): lax.all_to_all(jnp.broadcast_to(grad[None], (groups, row_share, tile)), '...  6.96 us
    ppermute x2, starting transfers between devices, swap(): return lax.ppermute(x, 'wide', [(i, i ^ 1) for i in range(wide)])  5.12 us
  transfers between devices with their start and end apart: 10, of which 6 were waited for; matrix products, arithmetic and copies ran while one was open for 2% of the time, Pallas kernels for 0%

profile of v2, /device:TPU:64, one launch (start us, length us, event | category | flops | bytes accessed | tf_op | source)
XLA Modules:
  0.0 175.7 jit_solution(14115655872735235413)
XLA Ops:
  0.6 1.5 broadcast_in_dim.16
  2.1 26.7 %all-to-all-start = ((bf16[8,128,128]{2,1,0:T(8,128)(2,1)}), bf16[8,128,128]{2,1,0:T(8,128)(2,1)S(1)}, u32[]{:S(2)}, u32[]{:S(2)}) async-start(bf16[8,128,128]{2,1,0:T(8,128)(2,1)} %broadcast_in_dim.16), calls=%async_computation | async-start | bytes 524288 | tf_op jit(solution)/shard_map/gather_far/all_to_all | solution.py:98
  28.8 0.2 copy.31
  29.1 0.5 copy-done.3
  29.6 0.1 copy.33
  29.7 1.9 %collective-permute-start.3 = (bf16[128,1152]{0,1:T(8,128)(2,1)S(1)}, bf16[128,1152]{0,1:T(8,128)(2,1)S(1)}, u32[]{:S(2)}, u32[]{:S(2)}) collective-permute-start(bf16[128,1152]{0,1:T(8,128)(2,1)S(1)} %pad_maximum_fusion.1), channel_id=1, source_target_pairs={{0,16},{16,0},{32,48},{48,32},{64,80},{80,64},{96,112},{112,96},{1... | collective-permute-start | bytes 884744 | tf_op jit(solution)/shard_map/prepare/ppermute | solution.py:95
  31.7 0.7 copy-done.4
  32.5 0.6 gather_fusion.1
  33.1 0.6 gather_fusion
  34.1 36.1 %all-to-all-done.held0 = bf16[8,128,128]{2,1,0:T(8,128)(2,1)S(1)} async-done(((bf16[8,128,128]{2,1,0:T(8,128)(2,1)}), bf16[8,128,128]{2,1,0:T(8,128)(2,1)S(1)}, u32[]{:S(2)}, u32[]{:S(2)}) %all-to-all-start) | async-done | bytes 262176 | tf_op jit(solution)/shard_map/gather_far/all_to_all | solution.py:98
  70.1 1.9 %collective-permute-start = (bf16[8,128,128]{2,1,0:T(8,128)(2,1)S(1)}, bf16[8,128,128]{2,1,0:T(8,128)(2,1)S(1)}, u32[]{:S(2)}, u32[]{:S(2)}) collective-permute-start(bf16[8,128,128]{2,1,0:T(8,128)(2,1)S(1)} %all-to-all-done.held0), channel_id=1, source_target_pairs={{0,32},{16,1008},{32,64},{48,16},{64,96},{80,48},{96,128},{112,80}... | collective-permute-start | bytes 786440 | tf_op jit(solution)/shard_map/gather_near/ppermute | solution.py:89
  72.1 3.8 %collective-permute-start.1 = (bf16[8,128,128]{2,1,0:T(8,128)(2,1)S(1)}, bf16[8,128,128]{2,1,0:T(8,128)(2,1)S(1)}, u32[]{:S(2)}, u32[]{:S(2)}) collective-permute-start(bf16[8,128,128]{2,1,0:T(8,128)(2,1)S(1)} %all-to-all-done.held0), channel_id=1, source_target_pairs={{0,64},{16,976},{32,96},{48,1008},{64,128},{80,16},{96,160},{112,4... | collective-permute-start | bytes 786440 | tf_op jit(solution)/shard_map/gather_near/ppermute | solution.py:89
  75.9 3.0 %collective-permute-start.2 = (bf16[8,128,128]{2,1,0:T(8,128)(2,1)S(1)}, bf16[8,128,128]{2,1,0:T(8,128)(2,1)S(1)}, u32[]{:S(2)}, u32[]{:S(2)}) collective-permute-start(bf16[8,128,128]{2,1,0:T(8,128)(2,1)S(1)} %all-to-all-done.held0), channel_id=1, source_target_pairs={{0,992},{16,48},{32,0},{48,80},{64,32},{80,112},{96,64},{112,144},... | collective-permute-start | bytes 786440 | tf_op jit(solution)/shard_map/gather_near/ppermute | solution.py:89
  79.0 0.2 copy.34.tile_rows
  79.3 4.9 %collective-permute-done.1.held2 = bf16[8,128,128]{2,1,0:T(8,128)(2,1)S(1)} collective-permute-done((bf16[8,128,128]{2,1,0:T(8,128)(2,1)S(1)}, bf16[8,128,128]{2,1,0:T(8,128)(2,1)S(1)}, u32[]{:S(2)}, u32[]{:S(2)}) %collective-permute-start.1) | collective-permute-done | bytes 262176 | tf_op jit(solution)/shard_map/gather_near/ppermute | solution.py:89
  84.2 1.1 collective-permute-done.2.held3
  85.2 1.1 forward.1.mine
  86.3 3.2 %collective-permute-start.4 = (f32[2,128,128]{2,1,0:T(8,128)S(1)}, f32[2,128,128]{2,1,0:T(8,128)S(1)}, u32[]{:S(2)}, u32[]{:S(2)}) collective-permute-start(f32[2,128,128]{2,1,0:T(8,128)S(1)} %forward.1.mine), channel_id=1, source_target_pairs={{0,16},{16,0},{32,48},{48,32},{64,80},{80,64},{96,112},{112,96},{1... | collective-permute-start | bytes 393224 | tf_op jit(solution)/shard_map/pair/ppermute | solution.py:95
  89.6 0.1 copy.36.cot
  89.7 0.8 collective-permute-done.4.theirs
  90.5 2.1 %backward.1 = (bf16[128,128]{1,0:T(8,128)(2,1)}, bf16[1056,128]{1,0:T(8,128)(2,1)S(1)}, bf16[1056,128]{1,0:T(8,128)(2,1)S(1)}, bf16[1056,128]{1,0:T(8,128)(2,1)S(1)}, bf16[1056,128]{1,0:T(8,128)(2,1)S(1)}) custom-call(s32[2,8]{1,0:T(2,128)S(1)} %and_select_fusion.6.pos, f32[2,128,128]{2,1,0:T(8,128)S(1)} %forward.1.mine, ...), custom_call_target="tpu_custom_call" | custom-call | tf_op jit(solution)/shard_map/backward/pallas_call | solution.py:139
  92.6 4.9 %collective-permute-start.5 = (bf16[1056,128]{1,0:T(8,128)(2,1)S(1)}, bf16[1056,128]{1,0:T(8,128)(2,1)S(1)}, u32[]{:S(2)}, u32[]{:S(2)}) collective-permute-start(bf16[1056,128]{1,0:T(8,128)(2,1)S(1)} %get-tuple-element.10), channel_id=1, source_target_pairs={{0,992},{16,48},{32,0},{48,80},{64,32},{80,112},{96,64},{112,144},... | collective-permute-start | bytes 811016 | tf_op jit(solution)/shard_map/scatter_near/ppermute | solution.py:89
  97.6 2.6 %collective-permute-start.6 = (bf16[1056,128]{1,0:T(8,128)(2,1)S(1)}, bf16[1056,128]{1,0:T(8,128)(2,1)S(1)}, u32[]{:S(2)}, u32[]{:S(2)}) collective-permute-start(bf16[1056,128]{1,0:T(8,128)(2,1)S(1)} %get-tuple-element.11), channel_id=1, source_target_pairs={{0,960},{16,80},{32,992},{48,112},{64,0},{80,144},{96,32},{112,176... | collective-permute-start | bytes 811016 | tf_op jit(solution)/shard_map/scatter_near/ppermute | solution.py:89
  100.1 2.7 %collective-permute-start.7 = (bf16[1056,128]{1,0:T(8,128)(2,1)S(1)}, bf16[1056,128]{1,0:T(8,128)(2,1)S(1)}, u32[]{:S(2)}, u32[]{:S(2)}) collective-permute-start(bf16[1056,128]{1,0:T(8,128)(2,1)S(1)} %get-tuple-element.12), channel_id=1, source_target_pairs={{0,32},{16,1008},{32,64},{48,16},{64,96},{80,48},{96,128},{112,80}... | collective-permute-start | bytes 811016 | tf_op jit(solution)/shard_map/scatter_near/ppermute | solution.py:89
  102.9 10.2 %collective-permute-done.6 = bf16[1056,128]{1,0:T(8,128)(2,1)S(1)} collective-permute-done((bf16[1056,128]{1,0:T(8,128)(2,1)S(1)}, bf16[1056,128]{1,0:T(8,128)(2,1)S(1)}, u32[]{:S(2)}, u32[]{:S(2)}) %collective-permute-start.6) | collective-permute-done | bytes 270368 | tf_op jit(solution)/shard_map/scatter_near/ppermute | solution.py:89
  113.1 0.1 convert_add_fusion
  113.3 46.5 %all_to_all.15 = bf16[8,132,128]{2,1,0:T(8,128)(2,1)S(1)} all-to-all(bf16[8,132,128]{2,1,0:T(8,128)(2,1)S(1)} %pad_maximum_fusion.2), channel_id=1, replica_groups={{0,128,256,384,512,640,768,896},{16,144,272,400,528,656,784,912},{32,16..., dimensions={0} | all-to-all | bytes 540672 | tf_op jit(solution)/shard_map/scatter_far/all_to_all | solution.py:98
  159.9 0.6 broadcast_in_dim.35
  160.5 7.0 %all-to-all-start.2 = ((f32[16,2,128]{2,1,0:T(2,128)}), f32[16,2,128]{2,1,0:T(2,128)S(1)}, u32[]{:S(2)}, u32[]{:S(2)}) async-start(f32[16,2,128]{2,1,0:T(2,128)} %broadcast_in_dim.35), calls=%async_computation.2 | async-start | bytes 32768 | tf_op jit(solution)/shard_map/weight_sum/all_to_all | solution.py:164
  167.5 0.6 fusion
  168.1 7.0 %all-to-all-done.2 = f32[16,2,128]{2,1,0:T(2,128)S(1)} async-done(((f32[16,2,128]{2,1,0:T(2,128)}), f32[16,2,128]{2,1,0:T(2,128)S(1)}, u32[]{:S(2)}, u32[]{:S(2)}) %all-to-all-start.2) | async-done | bytes 16416 | tf_op jit(solution)/shard_map/weight_sum/all_to_all | solution.py:164
  175.1 0.6 reduce_sum.19
  (31 shorter events, 0.8 us)
Async XLA Ops:
  0.6 32.5 %copy-start = (s32[1,64]{1,0:T(1,128)S(1)}, s32[1,64]{1,0:T(1,128)}, u32[]{:S(2)}) copy-start(s32[1,64]{1,0:T(1,128)} %param.10) | copy-start | bytes 772
  2.1 26.7 %copy-start.2 = (bf16[1,128,8,128]{3,2,1,0:T(8,128)(2,1)S(1)}, bf16[1,128,8,128]{3,2,1,0:T(8,128)(2,1)}, u32[]{:S(2)}) copy-start(bf16[1,128,8,128]{3,2,1,0:T(8,128)(2,1)} %param.8) | copy-start | bytes 786436
  2.1 68.0 %all-to-all-start = ((bf16[8,128,128]{2,1,0:T(8,128)(2,1)}), bf16[8,128,128]{2,1,0:T(8,128)(2,1)S(1)}, u32[]{:S(2)}, u32[]{:S(2)}) async-start(bf16[8,128,128]{2,1,0:T(8,128)(2,1)} %broadcast_in_dim.16), calls=%async_computation | async-start | bytes 524288 | tf_op jit(solution)/shard_map/gather_far/all_to_all | solution.py:98
  28.8 0.8 copy-start.3
  29.7 49.2 %collective-permute-start.3 = (bf16[128,1152]{0,1:T(8,128)(2,1)S(1)}, bf16[128,1152]{0,1:T(8,128)(2,1)S(1)}, u32[]{:S(2)}, u32[]{:S(2)}) collective-permute-start(bf16[128,1152]{0,1:T(8,128)(2,1)S(1)} %pad_maximum_fusion.1), channel_id=1, source_target_pairs={{0,16},{16,0},{32,48},{48,32},{64,80},{80,64},{96,112},{112,96},{1... | collective-permute-start | bytes 884744 | tf_op jit(solution)/shard_map/prepare/ppermute | solution.py:95
  31.7 0.7 copy-start.4
  70.1 9.1 %collective-permute-start = (bf16[8,128,128]{2,1,0:T(8,128)(2,1)S(1)}, bf16[8,128,128]{2,1,0:T(8,128)(2,1)S(1)}, u32[]{:S(2)}, u32[]{:S(2)}) collective-permute-start(bf16[8,128,128]{2,1,0:T(8,128)(2,1)S(1)} %all-to-all-done.held0), channel_id=1, source_target_pairs={{0,32},{16,1008},{32,64},{48,16},{64,96},{80,48},{96,128},{112,80}... | collective-permute-start | bytes 786440 | tf_op jit(solution)/shard_map/gather_near/ppermute | solution.py:89
  72.1 12.1 %collective-permute-start.1 = (bf16[8,128,128]{2,1,0:T(8,128)(2,1)S(1)}, bf16[8,128,128]{2,1,0:T(8,128)(2,1)S(1)}, u32[]{:S(2)}, u32[]{:S(2)}) collective-permute-start(bf16[8,128,128]{2,1,0:T(8,128)(2,1)S(1)} %all-to-all-done.held0), channel_id=1, source_target_pairs={{0,64},{16,976},{32,96},{48,1008},{64,128},{80,16},{96,160},{112,4... | collective-permute-start | bytes 786440 | tf_op jit(solution)/shard_map/gather_near/ppermute | solution.py:89
  75.9 9.3 %collective-permute-start.2 = (bf16[8,128,128]{2,1,0:T(8,128)(2,1)S(1)}, bf16[8,128,128]{2,1,0:T(8,128)(2,1)S(1)}, u32[]{:S(2)}, u32[]{:S(2)}) collective-permute-start(bf16[8,128,128]{2,1,0:T(8,128)(2,1)S(1)} %all-to-all-done.held0), channel_id=1, source_target_pairs={{0,992},{16,48},{32,0},{48,80},{64,32},{80,112},{96,64},{112,144},... | collective-permute-start | bytes 786440 | tf_op jit(solution)/shard_map/gather_near/ppermute | solution.py:89
  86.3 4.2 %collective-permute-start.4 = (f32[2,128,128]{2,1,0:T(8,128)S(1)}, f32[2,128,128]{2,1,0:T(8,128)S(1)}, u32[]{:S(2)}, u32[]{:S(2)}) collective-permute-start(f32[2,128,128]{2,1,0:T(8,128)S(1)} %forward.1.mine), channel_id=1, source_target_pairs={{0,16},{16,0},{32,48},{48,32},{64,80},{80,64},{96,112},{112,96},{1... | collective-permute-start | bytes 393224 | tf_op jit(solution)/shard_map/pair/ppermute | solution.py:95
  89.5 0.9 copy-start.1
  92.6 10.3 %collective-permute-start.5 = (bf16[1056,128]{1,0:T(8,128)(2,1)S(1)}, bf16[1056,128]{1,0:T(8,128)(2,1)S(1)}, u32[]{:S(2)}, u32[]{:S(2)}) collective-permute-start(bf16[1056,128]{1,0:T(8,128)(2,1)S(1)} %get-tuple-element.10), channel_id=1, source_target_pairs={{0,992},{16,48},{32,0},{48,80},{64,32},{80,112},{96,64},{112,144},... | collective-permute-start | bytes 811016 | tf_op jit(solution)/shard_map/scatter_near/ppermute | solution.py:89
  97.6 15.5 %collective-permute-start.6 = (bf16[1056,128]{1,0:T(8,128)(2,1)S(1)}, bf16[1056,128]{1,0:T(8,128)(2,1)S(1)}, u32[]{:S(2)}, u32[]{:S(2)}) collective-permute-start(bf16[1056,128]{1,0:T(8,128)(2,1)S(1)} %get-tuple-element.11), channel_id=1, source_target_pairs={{0,960},{16,80},{32,992},{48,112},{64,0},{80,144},{96,32},{112,176... | collective-permute-start | bytes 811016 | tf_op jit(solution)/shard_map/scatter_near/ppermute | solution.py:89
  100.1 12.9 %collective-permute-start.7 = (bf16[1056,128]{1,0:T(8,128)(2,1)S(1)}, bf16[1056,128]{1,0:T(8,128)(2,1)S(1)}, u32[]{:S(2)}, u32[]{:S(2)}) collective-permute-start(bf16[1056,128]{1,0:T(8,128)(2,1)S(1)} %get-tuple-element.12), channel_id=1, source_target_pairs={{0,32},{16,1008},{32,64},{48,16},{64,96},{80,48},{96,128},{112,80}... | collective-permute-start | bytes 811016 | tf_op jit(solution)/shard_map/scatter_near/ppermute | solution.py:89
  160.5 14.6 %all-to-all-start.2 = ((f32[16,2,128]{2,1,0:T(2,128)}), f32[16,2,128]{2,1,0:T(2,128)S(1)}, u32[]{:S(2)}, u32[]{:S(2)}) async-start(f32[16,2,128]{2,1,0:T(2,128)} %broadcast_in_dim.35), calls=%async_computation.2 | async-start | bytes 32768 | tf_op jit(solution)/shard_map/weight_sum/all_to_all | solution.py:164

commit v3 on v2

--- a/solution.py
+++ b/solution.py
@@ -12,19 +12,19 @@
 PARAMS = pltpu.CompilerParams(vmem_limit_bytes=32 * 1024 * 1024)
 
 NEAR = (0, 1, 2, -1)
-CLASSES = len(NEAR)
-
-
-def forward(pos, held0, held1, held2, held3, tile_rows, mixed):
+CLASSES = 8
+
+
+def forward(pos, own, beside, tile_rows, mixed):
     slots = pos.shape[1]
-    share = held0.shape[0]
+    share = own.shape[0]
     for r in range(2):
         picked = []
         for s in range(slots):
-            near, far = pos[r, s] // share, pos[r, s] % share
-            block = jnp.zeros(held0.shape[1:], BF16)
-            for a, held in enumerate((held0, held1, held2, held3)):
-                block = jnp.where(near == a, held[far], block)
+            which, far = pos[r, s] // share, pos[r, s] % share
+            block = jnp.zeros(own.shape[1:], BF16)
+            block = jnp.where(which == 0, own[far], block)
+            block = jnp.where(which == 1, beside[far], block)
             picked.append(block)
         mixed[r] = jnp.dot(tile_rows[r], jnp.concatenate(picked, 0), preferred_element_type=F32)
 
@@ -65,8 +65,8 @@
     rest = (grad - top.astype(F32)).astype(BF16)
     ordered_top = jnp.dot(perm[...], top, preferred_element_type=F32).astype(BF16)
     ordered_rest = jnp.dot(perm[...], rest, preferred_element_type=F32).astype(BF16)
-    share = blocks // CLASSES
-    rows = perm.shape[0] // CLASSES
+    share = blocks // len(NEAR)
+    rows = perm.shape[0] // len(NEAR)
     for a, out in enumerate((out0, out1, out2, out3)):
         for k in range(share):
             out[pl.ds(k * tile, tile), :] = total[a * share + k].astype(BF16)
@@ -80,7 +80,8 @@
     slots = tiles.shape[2]
     wide = lax.axis_size("wide")
     chips = wide // 2
-    share = chips // CLASSES
+    far = chips // CLASSES
+    share = 2 * far
     w = lax.axis_index("wide")
     z, c = w // 2, w % 2
     sign = 1 - 2 * c
@@ -94,16 +95,18 @@
     def swap(x):
         return lax.ppermute(x, "wide", [(i, i ^ 1) for i in range(wide)])
 
-    def within_class(x):
-        return lax.all_to_all(
-            x, "wide", 0, 0,
-            axis_index_groups=[
-                [2 * (CLASSES * m + k) + core for m in range(share)] for k in range(CLASSES) for core in range(2)
-            ],
-        )
+    def every(step):
+        return [
+            [2 * (m + k) + core for m in range(0, chips, step)] for k in range(step) for core in range(2)
+        ]
 
     with jax.named_scope("gather_far"):
-        held = within_class(jnp.broadcast_to(feat[None], (share, tile, tile)))
+        held = lax.all_gather(feat, "wide", axis_index_groups=every(2))
+        held, tiles, cotangent, tile_cols, tile_counts = lax.optimization_barrier(
+            (held, tiles, cotangent, tile_cols, tile_counts)
+        )
+    with jax.named_scope("gather_near"):
+        beside = send(held, 1)
     with jax.named_scope("prepare"):
         rows = tiles[0].reshape(tile, slots * tile)
         both = jnp.concatenate([rows, cotangent[0]], axis=1)
@@ -115,48 +118,62 @@
         cols = tile_cols[0][here]
         counts = tile_counts[0][here]
         chip = cols // 2
-        place = (sign * (z - chip)) % CLASSES * share + chip // CLASSES
         active = (jnp.arange(slots)[None, :] < counts[:, None]) & (cols % 2 == c)
-        pos = jnp.where(active, place, chips).astype(jnp.int32)
+        source = (z - chip) % 2 * (chips // 2) + chip // 2
+        source = jnp.where(active, source, chips).astype(jnp.int32)
+        offset = (sign * (z - chip)) % CLASSES
+        place = offset % 4 * share + (offset + 1) // 4 % 2 * far + chip // CLASSES
+        place = jnp.where(active, place, chips).astype(jnp.int32)
         spot = jnp.arange(chips)
-        chip_at = (z - sign * (spot // share)) % CLASSES + CLASSES * (spot % share)
+        near_at = jnp.where(spot // share == 3, -1, spot // share)
+        chip_at = (z - sign * (near_at + 4 * (spot % share // far))) % CLASSES + CLASSES * (spot % far)
         row_share = tile // wide
         row_at = ((2 * chip_at + c)[:, None] * row_share + jnp.arange(row_share)[None, :]).reshape(-1)
         perm = (row_at[:, None] == jnp.arange(tile)[None, :]).astype(BF16)
-    with jax.named_scope("gather_near"):
-        gathered = [held] + [send(held, d) for d in NEAR[1:]]
     mixed = pl.pallas_call(
         forward,
         out_shape=jax.ShapeDtypeStruct((2, tile, tile), F32),
-        in_specs=[SMEM] + [VMEM] * 5,
+        in_specs=[SMEM] + [VMEM] * 3,
         out_specs=VMEM,
         compiler_params=PARAMS,
         name="forward",
-    )(pos, *gathered, tile_rows)
+    )(source, held, beside, tile_rows)
     with jax.named_scope("pair"):
         theirs = swap(mixed)
     extra = share * row_share
     activated, *parts = pl.pallas_call(
         backward,
         out_shape=[jax.ShapeDtypeStruct((tile, tile), BF16)]
-        + [jax.ShapeDtypeStruct((share * tile + 2 * extra, tile), BF16)] * CLASSES,
+        + [jax.ShapeDtypeStruct((share * tile + 2 * extra, tile), BF16)] * len(NEAR),
         in_specs=[SMEM] + [VMEM] * 6,
-        out_specs=[VMEM] * (1 + CLASSES),
+        out_specs=[VMEM] * (1 + len(NEAR)),
         scratch_shapes=[pltpu.VMEM((chips + 1, tile, tile), F32)],
         compiler_params=PARAMS,
         name="backward",
-    )(pos, mixed, theirs, cot, tile_flip, weight, perm)
+    )(place, mixed, theirs, cot, tile_flip, weight, perm)
+    def parted(whole, count):
+        main = whole[: count * tile].astype(BF16)
+        grad = whole[count * tile :]
+        half = grad.shape[0] // 2
+        grad = grad[:half] + grad[half:]
+        top = grad.astype(BF16)
+        return main, top, (grad - top.astype(F32)).astype(BF16)
+
     with jax.named_scope("scatter_near"):
         whole = parts[0].astype(F32)
         for part, d in zip(parts[1:], NEAR[1:]):
             whole += send(part, -d).astype(F32)
-        main = whole[: share * tile].reshape(share, tile, tile).astype(BF16)
-        grad = whole[share * tile : share * tile + extra] + whole[share * tile + extra :]
-        grad = grad.reshape(share, row_share, tile)
+        pieces = parted(whole, share)
+        keep, give = (
+            jnp.concatenate([jnp.split(piece, 2)[half] for piece in pieces], 0) for half in range(2)
+        )
+    with jax.named_scope("scatter_middle"):
+        whole = keep.astype(F32) + send(give, -4).astype(F32)
+        pieces = parted(whole, far)
     with jax.named_scope("scatter_far"):
-        top = grad.astype(BF16)
-        rest = (grad - top.astype(F32)).astype(BF16)
-        whole = within_class(jnp.concatenate([main, top, rest], 1)).astype(F32).sum(0)
+        message = jnp.concatenate([piece.reshape(far, -1, tile) for piece in pieces], 1)
+        got = lax.all_to_all(message, "wide", 0, 0, axis_index_groups=every(CLASSES))
+        whole = got.astype(F32).sum(0)
         feature_grad = whole[:tile].astype(BF16)
         grad = whole[tile : tile + row_share] + whole[tile + row_share :]
     with jax.named_scope("weight_sum"):

time: 176 us -> 162 us (0.920)
  the two profiles are of different devices: /device:TPU:64 before, /device:TPU:33 now
where the time goes in v3:
time: 162 us
  blocking collectives  89.7 us (55%)
  starting transfers between devices  36.6 us (23%)
  waiting for transfers between devices  25.9 us (16%)
  local copies, waits for them, and re-layouts  3.99 us (2%)
  Pallas kernels  3.04 us (2%)
    all_to_all x1, blocking collectives, shards(): lax.all_to_all(message, 'wide', 0, 0, axis_index_groups=every(CLASSES))  46.1 us
    all_gather x1, blocking collectives, shards(): held = lax.all_gather(feat, 'wide', axis_index_groups=every(2))  43.6 us
    ppermute x5, waiting for transfers between devices, send(): lax.ppermute(x, 'wide', [(2 * i + k, 2 * ((i + (d if k == 0 else -d)) % c...  19.3 us
    ppermute x5, starting transfers between devices, send(): lax.ppermute(x, 'wide', [(2 * i + k, 2 * ((i + (d if k == 0 else -d)) % c...  18.1 us
    ppermute x2, starting transfers between devices, swap(): return lax.ppermute(x, 'wide', [(i, i ^ 1) for i in range(wide)])  11.8 us
    all_to_all x1, starting transfers between devices, shards(): lax.all_to_all(jnp.broadcast_to(grad[None], (groups, row_share, tile)), '...  6.76 us
    all_to_all x1, waiting for transfers between devices, shards(): lax.all_to_all(jnp.broadcast_to(grad[None], (groups, row_share, tile)), '...  5.81 us
  transfers between devices with their start and end apart: 8, of which 6 were waited for; matrix products, arithmetic and copies ran while one was open for 2% of the time, Pallas kernels for 0%

profile of v3, /device:TPU:33, one launch (start us, length us, event | category | flops | bytes accessed | tf_op | source)
XLA Modules:
  0.0 161.5 jit_solution(8013803609138174869)
XLA Ops:
  0.7 43.6 %all_gather.3.own = bf16[16,128,128]{2,1,0:T(8,128)(2,1)S(1)} all-gather(bf16[1,128,128]{2,1,0:T(8,128)(2,1)} %param.6), channel_id=1, replica_groups={{0,64,128,192,256,320,384,448,512,576,640,704,768,832,896,960},{16,80,1..., dimensions={0}, use_global_device_ids=true | all-gather | bytes 557056 | tf_op jit(solution)/shard_map/gather_far/all_gather | solution.py:104
  44.3 0.1 copy.40
  44.4 0.2 copy.38
  44.7 9.0 %collective-permute-start.1 = (bf16[128,1152]{0,1:T(8,128)(2,1)S(1)}, bf16[128,1152]{0,1:T(8,128)(2,1)S(1)}, u32[]{:S(2)}, u32[]{:S(2)}) collective-permute-start(bf16[128,1152]{0,1:T(8,128)(2,1)S(1)} %pad_maximum_fusion.1), channel_id=1, source_target_pairs={{0,16},{16,0},{32,48},{48,32},{64,80},{80,64},{96,112},{112,96},{1... | collective-permute-start | bytes 884744 | tf_op jit(solution)/shard_map/prepare/ppermute | solution.py:96
  53.7 2.7 %collective-permute-start = (bf16[16,128,128]{2,1,0:T(8,128)(2,1)S(1)}, bf16[16,128,128]{2,1,0:T(8,128)(2,1)S(1)}, u32[]{:S(2)}, u32[]{:S(2)}) collective-permute-start(bf16[16,128,128]{2,1,0:T(8,128)(2,1)S(1)} %all_gather.3.own), channel_id=1, source_target_pairs={{0,32},{16,1008},{32,64},{48,16},{64,96},{80,48},{96,128},{112,80}... | collective-permute-start | bytes 1572872 | tf_op jit(solution)/shard_map/gather_near/ppermute | solution.py:90
  56.4 0.1 fusion.22
  56.6 0.1 add.176
  56.8 0.6 copy-done.4
  57.4 0.1 copy.37
  57.5 0.6 gather_fusion
  58.1 0.6 gather_fusion.1
  58.9 0.2 copy.41.tile_rows
  59.1 4.8 %collective-permute-done.beside = bf16[16,128,128]{2,1,0:T(8,128)(2,1)S(1)} collective-permute-done((bf16[16,128,128]{2,1,0:T(8,128)(2,1)S(1)}, bf16[16,128,128]{2,1,0:T(8,128)(2,1)S(1)}, u32[]{:S(2)}, u32[]{:S(2)}) %collective-permute-start) | collective-permute-done | bytes 524320 | tf_op jit(solution)/shard_map/gather_near/ppermute | solution.py:90
  63.9 0.9 forward.1.mine
  64.8 2.8 %collective-permute-start.2 = (f32[2,128,128]{2,1,0:T(8,128)S(1)}, f32[2,128,128]{2,1,0:T(8,128)S(1)}, u32[]{:S(2)}, u32[]{:S(2)}) collective-permute-start(f32[2,128,128]{2,1,0:T(8,128)S(1)} %forward.1.mine), channel_id=1, source_target_pairs={{0,16},{16,0},{32,48},{48,32},{64,80},{80,64},{96,112},{112,96},{1... | collective-permute-start | bytes 393224 | tf_op jit(solution)/shard_map/pair/ppermute | solution.py:96
  67.6 0.1 copy.43.cot
  67.7 0.8 collective-permute-done.2.theirs
  68.5 2.1 %backward.1 = (bf16[128,128]{1,0:T(8,128)(2,1)}, bf16[1056,128]{1,0:T(8,128)(2,1)S(1)}, bf16[1056,128]{1,0:T(8,128)(2,1)S(1)}, bf16[1056,128]{1,0:T(8,128)(2,1)S(1)}, bf16[1056,128]{1,0:T(8,128)(2,1)S(1)}) custom-call(s32[2,8]{1,0:T(2,128)S(1)} %fusion.15.pos, f32[2,128,128]{2,1,0:T(8,128)S(1)} %forward.1.mine, ...), custom_call_target="tpu_custom_call" | custom-call | tf_op jit(solution)/shard_map/backward/pallas_call | solution.py:144
  70.7 1.9 %collective-permute-start.3 = (bf16[1056,128]{1,0:T(8,128)(2,1)S(1)}, bf16[1056,128]{1,0:T(8,128)(2,1)S(1)}, u32[]{:S(2)}, u32[]{:S(2)}) collective-permute-start(bf16[1056,128]{1,0:T(8,128)(2,1)S(1)} %get-tuple-element.20), channel_id=1, source_target_pairs={{0,992},{16,48},{32,0},{48,80},{64,32},{80,112},{96,64},{112,144},... | collective-permute-start | bytes 811016 | tf_op jit(solution)/shard_map/scatter_near/ppermute | solution.py:90
  72.6 6.3 %collective-permute-start.4 = (bf16[1056,128]{1,0:T(8,128)(2,1)S(1)}, bf16[1056,128]{1,0:T(8,128)(2,1)S(1)}, u32[]{:S(2)}, u32[]{:S(2)}) collective-permute-start(bf16[1056,128]{1,0:T(8,128)(2,1)S(1)} %get-tuple-element.21), channel_id=1, source_target_pairs={{0,960},{16,80},{32,992},{48,112},{64,0},{80,144},{96,32},{112,176... | collective-permute-start | bytes 811016 | tf_op jit(solution)/shard_map/scatter_near/ppermute | solution.py:90
  78.9 1.9 %collective-permute-start.5 = (bf16[1056,128]{1,0:T(8,128)(2,1)S(1)}, bf16[1056,128]{1,0:T(8,128)(2,1)S(1)}, u32[]{:S(2)}, u32[]{:S(2)}) collective-permute-start(bf16[1056,128]{1,0:T(8,128)(2,1)S(1)} %get-tuple-element.22), channel_id=1, source_target_pairs={{0,32},{16,1008},{32,64},{48,16},{64,96},{80,48},{96,128},{112,80}... | collective-permute-start | bytes 811016 | tf_op jit(solution)/shard_map/scatter_near/ppermute | solution.py:90
  80.8 7.4 %collective-permute-done.4 = bf16[1056,128]{1,0:T(8,128)(2,1)S(1)} collective-permute-done((bf16[1056,128]{1,0:T(8,128)(2,1)S(1)}, bf16[1056,128]{1,0:T(8,128)(2,1)S(1)}, u32[]{:S(2)}, u32[]{:S(2)}) %collective-permute-start.4) | collective-permute-done | bytes 270368 | tf_op jit(solution)/shard_map/scatter_near/ppermute | solution.py:90
  88.2 0.6 collective-permute-done.5
  88.8 0.1 fusion.25
  89.0 5.3 %collective-permute-start.6 = (bf16[528,128]{1,0:T(8,128)(2,1)S(1)}, bf16[528,128]{1,0:T(8,128)(2,1)S(1)}, u32[]{:S(2)}, u32[]{:S(2)}) collective-permute-start(bf16[528,128]{1,0:T(8,128)(2,1)S(1)} %pad_maximum_fusion.3), channel_id=1, source_target_pairs={{0,896},{16,144},{32,928},{48,176},{64,960},{80,208},{96,992},{112... | collective-permute-start | bytes 405512 | tf_op jit(solution)/shard_map/scatter_middle/ppermute | solution.py:90
  94.3 6.6 %collective-permute-done.6 = bf16[528,128]{1,0:T(8,128)(2,1)S(1)} collective-permute-done((bf16[528,128]{1,0:T(8,128)(2,1)S(1)}, bf16[528,128]{1,0:T(8,128)(2,1)S(1)}, u32[]{:S(2)}, u32[]{:S(2)}) %collective-permute-start.6) | collective-permute-done | bytes 135200 | tf_op jit(solution)/shard_map/scatter_middle/ppermute | solution.py:90
  101.0 46.1 %all_to_all.10 = bf16[4,132,128]{2,1,0:T(8,128)(2,1)S(1)} all-to-all(bf16[4,132,128]{2,1,0:T(8,128)(2,1)S(1)} %pad_maximum_fusion.2), channel_id=1, replica_groups={{0,256,512,768},{16,272,528,784},{32,288,544,800},{48,304,560,816},{64,..., dimensions={0} | all-to-all | bytes 270336 | tf_op jit(solution)/shard_map/scatter_far/all_to_all | solution.py:175
  147.1 0.6 broadcast_in_dim.16
  147.7 6.8 %all-to-all-start.1 = ((f32[16,2,128]{2,1,0:T(2,128)}), f32[16,2,128]{2,1,0:T(2,128)S(1)}, u32[]{:S(2)}, u32[]{:S(2)}) async-start(f32[16,2,128]{2,1,0:T(2,128)} %broadcast_in_dim.16), calls=%async_computation.1 | async-start | bytes 32768 | tf_op jit(solution)/shard_map/weight_sum/all_to_all | solution.py:181
  154.5 0.6 fusion
  155.1 5.8 %all-to-all-done.1 = f32[16,2,128]{2,1,0:T(2,128)S(1)} async-done(((f32[16,2,128]{2,1,0:T(2,128)}), f32[16,2,128]{2,1,0:T(2,128)S(1)}, u32[]{:S(2)}, u32[]{:S(2)}) %all-to-all-start.1) | async-done | bytes 16416 | tf_op jit(solution)/shard_map/weight_sum/all_to_all | solution.py:181
  160.9 0.6 reduce_sum.19
  (32 shorter events, 0.6 us)
Async XLA Ops:
  0.6 56.8 %copy-start = (s32[1,64]{1,0:T(1,128)S(1)}, s32[1,64]{1,0:T(1,128)}, u32[]{:S(2)}) copy-start(s32[1,64]{1,0:T(1,128)} %param.10) | copy-start | bytes 772
  0.6 43.6 %copy-start.3 = (bf16[1,128,128]{2,1,0:T(8,128)(2,1)S(1)}, bf16[1,128,128]{2,1,0:T(8,128)(2,1)}, u32[]{:S(2)}) copy-start(bf16[1,128,128]{2,1,0:T(8,128)(2,1)} %param.11) | copy-start | bytes 98308
  0.7 43.7 %copy-start.2 = (bf16[1,128,8,128]{3,2,1,0:T(8,128)(2,1)S(1)}, bf16[1,128,8,128]{3,2,1,0:T(8,128)(2,1)}, u32[]{:S(2)}) copy-start(bf16[1,128,8,128]{3,2,1,0:T(8,128)(2,1)} %param.8) | copy-start | bytes 786436
  44.7 14.1 %collective-permute-start.1 = (bf16[128,1152]{0,1:T(8,128)(2,1)S(1)}, bf16[128,1152]{0,1:T(8,128)(2,1)S(1)}, u32[]{:S(2)}, u32[]{:S(2)}) collective-permute-start(bf16[128,1152]{0,1:T(8,128)(2,1)S(1)} %pad_maximum_fusion.1), channel_id=1, source_target_pairs={{0,16},{16,0},{32,48},{48,32},{64,80},{80,64},{96,112},{112,96},{1... | collective-permute-start | bytes 884744 | tf_op jit(solution)/shard_map/prepare/ppermute | solution.py:96
  53.7 10.2 %collective-permute-start = (bf16[16,128,128]{2,1,0:T(8,128)(2,1)S(1)}, bf16[16,128,128]{2,1,0:T(8,128)(2,1)S(1)}, u32[]{:S(2)}, u32[]{:S(2)}) collective-permute-start(bf16[16,128,128]{2,1,0:T(8,128)(2,1)S(1)} %all_gather.3.own), channel_id=1, source_target_pairs={{0,32},{16,1008},{32,64},{48,16},{64,96},{80,48},{96,128},{112,80}... | collective-permute-start | bytes 1572872 | tf_op jit(solution)/shard_map/gather_near/ppermute | solution.py:90
  56.7 0.7 copy-start.4
  64.8 3.7 %collective-permute-start.2 = (f32[2,128,128]{2,1,0:T(8,128)S(1)}, f32[2,128,128]{2,1,0:T(8,128)S(1)}, u32[]{:S(2)}, u32[]{:S(2)}) collective-permute-start(f32[2,128,128]{2,1,0:T(8,128)S(1)} %forward.1.mine), channel_id=1, source_target_pairs={{0,16},{16,0},{32,48},{48,32},{64,80},{80,64},{96,112},{112,96},{1... | collective-permute-start | bytes 393224 | tf_op jit(solution)/shard_map/pair/ppermute | solution.py:96
  67.6 0.9 copy-start.1
  70.7 10.1 %collective-permute-start.3 = (bf16[1056,128]{1,0:T(8,128)(2,1)S(1)}, bf16[1056,128]{1,0:T(8,128)(2,1)S(1)}, u32[]{:S(2)}, u32[]{:S(2)}) collective-permute-start(bf16[1056,128]{1,0:T(8,128)(2,1)S(1)} %get-tuple-element.20), channel_id=1, source_target_pairs={{0,992},{16,48},{32,0},{48,80},{64,32},{80,112},{96,64},{112,144},... | collective-permute-start | bytes 811016 | tf_op jit(solution)/shard_map/scatter_near/ppermute | solution.py:90
  72.6 15.6 %collective-permute-start.4 = (bf16[1056,128]{1,0:T(8,128)(2,1)S(1)}, bf16[1056,128]{1,0:T(8,128)(2,1)S(1)}, u32[]{:S(2)}, u32[]{:S(2)}) collective-permute-start(bf16[1056,128]{1,0:T(8,128)(2,1)S(1)} %get-tuple-element.21), channel_id=1, source_target_pairs={{0,960},{16,80},{32,992},{48,112},{64,0},{80,144},{96,32},{112,176... | collective-permute-start | bytes 811016 | tf_op jit(solution)/shard_map/scatter_near/ppermute | solution.py:90
  78.9 9.9 %collective-permute-start.5 = (bf16[1056,128]{1,0:T(8,128)(2,1)S(1)}, bf16[1056,128]{1,0:T(8,128)(2,1)S(1)}, u32[]{:S(2)}, u32[]{:S(2)}) collective-permute-start(bf16[1056,128]{1,0:T(8,128)(2,1)S(1)} %get-tuple-element.22), channel_id=1, source_target_pairs={{0,32},{16,1008},{32,64},{48,16},{64,96},{80,48},{96,128},{112,80}... | collective-permute-start | bytes 811016 | tf_op jit(solution)/shard_map/scatter_near/ppermute | solution.py:90
  89.0 11.8 %collective-permute-start.6 = (bf16[528,128]{1,0:T(8,128)(2,1)S(1)}, bf16[528,128]{1,0:T(8,128)(2,1)S(1)}, u32[]{:S(2)}, u32[]{:S(2)}) collective-permute-start(bf16[528,128]{1,0:T(8,128)(2,1)S(1)} %pad_maximum_fusion.3), channel_id=1, source_target_pairs={{0,896},{16,144},{32,928},{48,176},{64,960},{80,208},{96,992},{112... | collective-permute-start | bytes 405512 | tf_op jit(solution)/shard_map/scatter_middle/ppermute | solution.py:90
  147.7 13.2 %all-to-all-start.1 = ((f32[16,2,128]{2,1,0:T(2,128)}), f32[16,2,128]{2,1,0:T(2,128)S(1)}, u32[]{:S(2)}, u32[]{:S(2)}) async-start(f32[16,2,128]{2,1,0:T(2,128)} %broadcast_in_dim.16), calls=%async_computation.1 | async-start | bytes 32768 | tf_op jit(solution)/shard_map/weight_sum/all_to_all | solution.py:181

commit v4 on v2

--- a/solution.py
+++ b/solution.py
@@ -12,25 +12,26 @@
 PARAMS = pltpu.CompilerParams(vmem_limit_bytes=32 * 1024 * 1024)
 
 NEAR = (0, 1, 2, -1)
-CLASSES = len(NEAR)
+CLASSES = 4
 
 
-def forward(pos, held0, held1, held2, held3, tile_rows, mixed):
+def forward(pos, own, beside, rows_mine, rows_theirs, cot, out):
     slots = pos.shape[1]
-    share = held0.shape[0]
-    for r in range(2):
+    share = own.shape[0]
+    for r, rows in enumerate((rows_mine, rows_theirs)):
         picked = []
         for s in range(slots):
-            near, far = pos[r, s] // share, pos[r, s] % share
-            block = jnp.zeros(held0.shape[1:], BF16)
-            for a, held in enumerate((held0, held1, held2, held3)):
-                block = jnp.where(near == a, held[far], block)
+            which, far = pos[r, s] // share, pos[r, s] % share
+            block = jnp.zeros(own.shape[1:], BF16)
+            block = jnp.where(which == 0, own[far], block)
+            block = jnp.where(which == 1, beside[far], block)
             picked.append(block)
-        mixed[r] = jnp.dot(tile_rows[r], jnp.concatenate(picked, 0), preferred_element_type=F32)
+        out[r] = jnp.dot(rows[...], jnp.concatenate(picked, 0), preferred_element_type=F32)
+    out[2] = cot[...].astype(F32)
 
 
 def backward(
-    pos, mine, theirs, cot, tile_cols, weight, perm,
+    pos, mine, theirs, cols_mine, cols_theirs, weight, perm,
     activated, out0, out1, out2, out3, total,
 ):
     slots = pos.shape[1]
@@ -38,7 +39,7 @@
     blocks = total.shape[0] - 1
     total[...] = jnp.zeros_like(total)
     grad = jnp.zeros((tile, tile), F32)
-    for r in range(2):
+    for r, (cols, cot) in enumerate(((cols_mine, mine), (cols_theirs, theirs))):
         mixed = mine[r] + theirs[1 - r]
         high = mixed.astype(BF16)
         low = (mixed - high.astype(F32)).astype(BF16)
@@ -48,7 +49,7 @@
         sig = jax.nn.sigmoid(pre)
         if r == 0:
             activated[...] = (pre * sig).astype(BF16)
-        act_grad = (cot[r].astype(F32) * sig * (1.0 + pre * (1.0 - sig))).astype(BF16)
+        act_grad = (cot[2] * sig * (1.0 + pre * (1.0 - sig))).astype(BF16)
         moved = lax.dot_general(
             act_grad, weight[...], (((1,), (1,)), ((), ())), preferred_element_type=F32
         ).astype(BF16)
@@ -58,7 +59,7 @@
             )
         for s in range(slots):
             term = jnp.dot(
-                tile_cols[r, pl.ds(s * tile, tile), :], moved, preferred_element_type=F32
+                cols[pl.ds(s * tile, tile), :], moved, preferred_element_type=F32
             )
             total[pos[r, s]] += term
     top = grad.astype(BF16)
@@ -94,45 +95,44 @@
     def swap(x):
         return lax.ppermute(x, "wide", [(i, i ^ 1) for i in range(wide)])
 
-    def within_class(x):
-        return lax.all_to_all(
-            x, "wide", 0, 0,
-            axis_index_groups=[
-                [2 * (CLASSES * m + k) + core for m in range(share)] for k in range(CLASSES) for core in range(2)
-            ],
-        )
+    def every(step):
+        return [
+            [2 * (m + k) + core for m in range(0, chips, step)] for k in range(step) for core in range(2)
+        ]
 
     with jax.named_scope("gather_far"):
-        held = within_class(jnp.broadcast_to(feat[None], (share, tile, tile)))
+        other = swap(tiles)
+        held = lax.all_gather(feat, "wide", axis_index_groups=every(2))
+        held, tiles, other, tile_cols, tile_counts = lax.optimization_barrier(
+            (held, tiles, other, tile_cols, tile_counts)
+        )
+    with jax.named_scope("gather_near"):
+        beside = send(held, 1)
     with jax.named_scope("prepare"):
-        rows = tiles[0].reshape(tile, slots * tile)
-        both = jnp.concatenate([rows, cotangent[0]], axis=1)
-        other = swap(both)
-        tile_rows = jnp.stack([rows, other[:, : slots * tile]])
-        tile_flip = jnp.swapaxes(tile_rows, 1, 2)
-        cot = jnp.stack([cotangent[0], other[:, slots * tile :]])
+        rows = [t[0].reshape(tile, slots * tile) for t in (tiles, other)]
+        flipped = [r.T for r in rows]
         here = jnp.stack([w, w ^ 1])
         cols = tile_cols[0][here]
         counts = tile_counts[0][here]
         chip = cols // 2
+        active = (jnp.arange(slots)[None, :] < counts[:, None]) & (cols % 2 == c)
+        source = (z - chip) % 2 * (chips // 2) + chip // 2
+        source = jnp.where(active, source, chips).astype(jnp.int32)
         place = (sign * (z - chip)) % CLASSES * share + chip // CLASSES
-        active = (jnp.arange(slots)[None, :] < counts[:, None]) & (cols % 2 == c)
-        pos = jnp.where(active, place, chips).astype(jnp.int32)
+        place = jnp.where(active, place, chips).astype(jnp.int32)
         spot = jnp.arange(chips)
         chip_at = (z - sign * (spot // share)) % CLASSES + CLASSES * (spot % share)
         row_share = tile // wide
         row_at = ((2 * chip_at + c)[:, None] * row_share + jnp.arange(row_share)[None, :]).reshape(-1)
         perm = (row_at[:, None] == jnp.arange(tile)[None, :]).astype(BF16)
-    with jax.named_scope("gather_near"):
-        gathered = [held] + [send(held, d) for d in NEAR[1:]]
     mixed = pl.pallas_call(
         forward,
-        out_shape=jax.ShapeDtypeStruct((2, tile, tile), F32),
+        out_shape=jax.ShapeDtypeStruct((3, tile, tile), F32),
         in_specs=[SMEM] + [VMEM] * 5,
         out_specs=VMEM,
         compiler_params=PARAMS,
         name="forward",
-    )(pos, *gathered, tile_rows)
+    )(source, held, beside, *rows, cotangent[0])
     with jax.named_scope("pair"):
         theirs = swap(mixed)
     extra = share * row_share
@@ -145,7 +145,7 @@
         scratch_shapes=[pltpu.VMEM((chips + 1, tile, tile), F32)],
         compiler_params=PARAMS,
         name="backward",
-    )(pos, mixed, theirs, cot, tile_flip, weight, perm)
+    )(place, mixed, theirs, *flipped, weight, perm)
     with jax.named_scope("scatter_near"):
         whole = parts[0].astype(F32)
         for part, d in zip(parts[1:], NEAR[1:]):
@@ -156,7 +156,9 @@
     with jax.named_scope("scatter_far"):
         top = grad.astype(BF16)
         rest = (grad - top.astype(F32)).astype(BF16)
-        whole = within_class(jnp.concatenate([main, top, rest], 1)).astype(F32).sum(0)
+        message = jnp.concatenate([main, top, rest], 1)
+        got = lax.all_to_all(message, "wide", 0, 0, axis_index_groups=every(CLASSES))
+        whole = got.astype(F32).sum(0)
         feature_grad = whole[:tile].astype(BF16)
         grad = whole[tile : tile + row_share] + whole[tile + row_share :]
     with jax.named_scope("weight_sum"):

time: 176 us -> 161 us (0.915)
  blocking collectives: 46.5 us -> 104 us
  waiting for transfers between devices: 60 us -> 19.3 us
  starting transfers between devices: 57.8 us -> 26.8 us
    all_gather x0 -> x1, blocking collectives: none -> 48.7 us  [shards(): held = lax.all_gather(feat, 'wide', axis_index_groups=every(2))]
    all_to_all x1 -> x0, waiting for transfers between devices: 36.1 us -> none  [within_class(): lax.all_to_all(x, 'wide', 0, 0, axis_index_groups=[[2 * (CLASSES * m + k)...]
    all_to_all x1 -> x0, starting transfers between devices: 26.7 us -> none  [within_class(): lax.all_to_all(x, 'wide', 0, 0, axis_index_groups=[[2 * (CLASSES * m + k)...]
    all_to_all x1, blocking collectives: 46.5 us -> 55.4 us  [shards(): lax.all_to_all(message, 'wide', 0, 0, axis_index_groups=every(CLASSES))]
    ppermute x6 -> x4, waiting for transfers between devices: 16.2 us -> 10.9 us  [send(): lax.ppermute(x, 'wide', [(2 * i + k, 2 * ((i + (d if k == 0 else -d)) % c...]
    ppermute x6 -> x4, starting transfers between devices: 19 us -> 16 us  [send(): lax.ppermute(x, 'wide', [(2 * i + k, 2 * ((i + (d if k == 0 else -d)) % c...]
  transfers between devices with their start and end apart: 10 -> 7, of which waited for: 6 -> 5; matrix products, arithmetic and copies ran while one was open for 2% -> 2% of each run, Pallas kernels for 0% -> 0%
where the time goes in v4:
time: 161 us; the launch traced here: 160 us
  blocking collectives  104 us (65%)
  starting transfers between devices  26.8 us (17%)
  waiting for transfers between devices  19.3 us (12%)
  local copies, waits for them, and re-layouts  4.79 us (3%)
  Pallas kernels  3.04 us (2%)
    all_to_all x1, blocking collectives, shards(): lax.all_to_all(message, 'wide', 0, 0, axis_index_groups=every(CLASSES))  55.4 us
    all_gather x1, blocking collectives, shards(): held = lax.all_gather(feat, 'wide', axis_index_groups=every(2))  48.7 us
    ppermute x4, starting transfers between devices, send(): lax.ppermute(x, 'wide', [(2 * i + k, 2 * ((i + (d if k == 0 else -d)) % c...  16 us
    ppermute x4, waiting for transfers between devices, send(): lax.ppermute(x, 'wide', [(2 * i + k, 2 * ((i + (d if k == 0 else -d)) % c...  10.9 us
    all_to_all x1, starting transfers between devices, shards(): lax.all_to_all(jnp.broadcast_to(grad[None], (groups, row_share, tile)), '...  7.03 us
    all_to_all x1, waiting for transfers between devices, shards(): lax.all_to_all(jnp.broadcast_to(grad[None], (groups, row_share, tile)), '...  6.96 us
    ppermute x2, starting transfers between devices, swap(): return lax.ppermute(x, 'wide', [(i, i ^ 1) for i in range(wide)])  3.84 us
  transfers between devices with their start and end apart: 7, of which 5 were waited for; matrix products, arithmetic and copies ran while one was open for 2% of the time, Pallas kernels for 0%

profile of v4, /device:TPU:64, one launch (start us, length us, event | category | flops | bytes accessed | tf_op | source)
XLA Modules:
  0.0 160.1 jit_solution(2204580509965358493)
XLA Ops:
  0.6 1.9 %collective-permute-start = (bf16[1,128,8,128]{3,2,1,0:T(8,128)(2,1)}, bf16[1,128,8,128]{3,2,1,0:T(8,128)(2,1)S(1)}, u32[]{:S(2)}, u32[]{:S(2)}) collective-permute-start(bf16[1,128,8,128]{3,2,1,0:T(8,128)(2,1)} %param.8), channel_id=1, source_target_pairs={{0,16},{16,0},{32,48},{48,32},{64,80},{80,64},{96,112},{112,96},{1... | collective-permute-start | bytes 786440 | tf_op jit(solution)/shard_map/gather_far/ppermute | solution.py:96
  2.7 0.1 fusion.18
  2.8 0.1 add.129
  2.9 0.5 copy-done.4
  3.3 48.7 %all_gather.3.own = bf16[16,128,128]{2,1,0:T(8,128)(2,1)S(1)} all-gather(bf16[1,128,128]{2,1,0:T(8,128)(2,1)S(1)} %copy-done.4), channel_id=1, replica_groups={{0,64,128,192,256,320,384,448,512,576,640,704,768,832,896,960},{16,80,1..., dimensions={0}, use_global_device_ids=true | all-gather | bytes 557056 | tf_op jit(solution)/shard_map/gather_far/all_gather | solution.py:105
  52.1 2.7 %collective-permute-start.1 = (bf16[16,128,128]{2,1,0:T(8,128)(2,1)S(1)}, bf16[16,128,128]{2,1,0:T(8,128)(2,1)S(1)}, u32[]{:S(2)}, u32[]{:S(2)}) collective-permute-start(bf16[16,128,128]{2,1,0:T(8,128)(2,1)S(1)} %all_gather.3.own), channel_id=1, source_target_pairs={{0,32},{16,1008},{32,64},{48,16},{64,96},{80,48},{96,128},{112,80}... | collective-permute-start | bytes 1572872 | tf_op jit(solution)/shard_map/gather_near/ppermute | solution.py:90
  54.8 0.6 copy-done.5
  55.4 0.1 copy.29
  55.5 0.6 gather_fusion.1
  56.1 0.6 gather_fusion
  56.7 0.3 copy-done.3
  57.0 0.2 copy.30
  57.3 0.1 copy.32.rows_mine
  57.4 0.2 copy.31
  57.7 0.1 copy.33.rows_theirs
  57.9 5.2 %collective-permute-done.1.beside = bf16[16,128,128]{2,1,0:T(8,128)(2,1)S(1)} collective-permute-done((bf16[16,128,128]{2,1,0:T(8,128)(2,1)S(1)}, bf16[16,128,128]{2,1,0:T(8,128)(2,1)S(1)}, u32[]{:S(2)}, u32[]{:S(2)}) %collective-permute-start.1) | collective-permute-done | bytes 524320 | tf_op jit(solution)/shard_map/gather_near/ppermute | solution.py:90
  63.1 0.9 forward.1.mine
  64.1 1.9 %collective-permute-start.2 = (f32[3,128,128]{2,1,0:T(8,128)S(1)}, f32[3,128,128]{2,1,0:T(8,128)S(1)}, u32[]{:S(2)}, u32[]{:S(2)}) collective-permute-start(f32[3,128,128]{2,1,0:T(8,128)S(1)} %forward.1.mine), channel_id=1, source_target_pairs={{0,16},{16,0},{32,48},{48,32},{64,80},{80,64},{96,112},{112,96},{1... | collective-permute-start | bytes 589832 | tf_op jit(solution)/shard_map/pair/ppermute | solution.py:96
  66.0 1.4 collective-permute-done.2.theirs
  67.4 2.1 %backward.1 = (bf16[128,128]{1,0:T(8,128)(2,1)}, bf16[1056,128]{1,0:T(8,128)(2,1)S(1)}, bf16[1056,128]{1,0:T(8,128)(2,1)S(1)}, bf16[1056,128]{1,0:T(8,128)(2,1)S(1)}, bf16[1056,128]{1,0:T(8,128)(2,1)S(1)}) custom-call(s32[2,8]{1,0:T(2,128)S(1)} %fusion.9.pos, f32[3,128,128]{2,1,0:T(8,128)S(1)} %forward.1.mine, ...), custom_call_target="tpu_custom_call" | custom-call | tf_op jit(solution)/shard_map/backward/pallas_call | solution.py:139
  69.5 3.2 %collective-permute-start.5 = (bf16[1056,128]{1,0:T(8,128)(2,1)S(1)}, bf16[1056,128]{1,0:T(8,128)(2,1)S(1)}, u32[]{:S(2)}, u32[]{:S(2)}) collective-permute-start(bf16[1056,128]{1,0:T(8,128)(2,1)S(1)} %get-tuple-element.22), channel_id=1, source_target_pairs={{0,32},{16,1008},{32,64},{48,16},{64,96},{80,48},{96,128},{112,80}... | collective-permute-start | bytes 811016 | tf_op jit(solution)/shard_map/scatter_near/ppermute | solution.py:90
  72.7 5.0 %collective-permute-start.4 = (bf16[1056,128]{1,0:T(8,128)(2,1)S(1)}, bf16[1056,128]{1,0:T(8,128)(2,1)S(1)}, u32[]{:S(2)}, u32[]{:S(2)}) collective-permute-start(bf16[1056,128]{1,0:T(8,128)(2,1)S(1)} %get-tuple-element.21), channel_id=1, source_target_pairs={{0,960},{16,80},{32,992},{48,112},{64,0},{80,144},{96,32},{112,176... | collective-permute-start | bytes 811016 | tf_op jit(solution)/shard_map/scatter_near/ppermute | solution.py:90
  77.7 5.1 %collective-permute-start.3 = (bf16[1056,128]{1,0:T(8,128)(2,1)S(1)}, bf16[1056,128]{1,0:T(8,128)(2,1)S(1)}, u32[]{:S(2)}, u32[]{:S(2)}) collective-permute-start(bf16[1056,128]{1,0:T(8,128)(2,1)S(1)} %get-tuple-element.20), channel_id=1, source_target_pairs={{0,992},{16,48},{32,0},{48,80},{64,32},{80,112},{96,64},{112,144},... | collective-permute-start | bytes 811016 | tf_op jit(solution)/shard_map/scatter_near/ppermute | solution.py:90
  82.9 0.4 collective-permute-done.4
  83.3 5.3 %collective-permute-done.3 = bf16[1056,128]{1,0:T(8,128)(2,1)S(1)} collective-permute-done((bf16[1056,128]{1,0:T(8,128)(2,1)S(1)}, bf16[1056,128]{1,0:T(8,128)(2,1)S(1)}, u32[]{:S(2)}, u32[]{:S(2)}) %collective-permute-start.3) | collective-permute-done | bytes 270368 | tf_op jit(solution)/shard_map/scatter_near/ppermute | solution.py:90
  88.6 0.1 convert_add_fusion
  88.8 55.4 %all_to_all.10 = bf16[8,132,128]{2,1,0:T(8,128)(2,1)S(1)} all-to-all(bf16[8,132,128]{2,1,0:T(8,128)(2,1)S(1)} %pad_maximum_fusion), channel_id=1, replica_groups={{0,128,256,384,512,640,768,896},{16,144,272,400,528,656,784,912},{32,16..., dimensions={0} | all-to-all | bytes 540672 | tf_op jit(solution)/shard_map/scatter_far/all_to_all | solution.py:160
  144.3 0.6 broadcast_in_dim.14
  144.9 7.0 %all-to-all-start.1 = ((f32[16,2,128]{2,1,0:T(2,128)}), f32[16,2,128]{2,1,0:T(2,128)S(1)}, u32[]{:S(2)}, u32[]{:S(2)}) async-start(f32[16,2,128]{2,1,0:T(2,128)} %broadcast_in_dim.14), calls=%async_computation.1 | async-start | bytes 32768 | tf_op jit(solution)/shard_map/weight_sum/all_to_all | solution.py:166
  151.9 0.6 fusion
  152.6 7.0 %all-to-all-done.1 = f32[16,2,128]{2,1,0:T(2,128)S(1)} async-done(((f32[16,2,128]{2,1,0:T(2,128)}), f32[16,2,128]{2,1,0:T(2,128)S(1)}, u32[]{:S(2)}, u32[]{:S(2)}) %all-to-all-start.1) | async-done | bytes 16416 | tf_op jit(solution)/shard_map/weight_sum/all_to_all | solution.py:166
  159.5 0.6 reduce_sum.19
  (23 shorter events, 0.4 us)
Async XLA Ops:
  0.6 55.5 %copy-start = (s32[1,64]{1,0:T(1,128)S(1)}, s32[1,64]{1,0:T(1,128)}, u32[]{:S(2)}) copy-start(s32[1,64]{1,0:T(1,128)} %param.10) | copy-start | bytes 772
  0.6 51.4 %collective-permute-start = (bf16[1,128,8,128]{3,2,1,0:T(8,128)(2,1)}, bf16[1,128,8,128]{3,2,1,0:T(8,128)(2,1)S(1)}, u32[]{:S(2)}, u32[]{:S(2)}) collective-permute-start(bf16[1,128,8,128]{3,2,1,0:T(8,128)(2,1)} %param.8), channel_id=1, source_target_pairs={{0,16},{16,0},{32,48},{48,32},{64,80},{80,64},{96,112},{112,96},{1... | collective-permute-start | bytes 786440 | tf_op jit(solution)/shard_map/gather_far/ppermute | solution.py:96
  2.6 0.8 copy-start.4
  52.1 11.1 %collective-permute-start.1 = (bf16[16,128,128]{2,1,0:T(8,128)(2,1)S(1)}, bf16[16,128,128]{2,1,0:T(8,128)(2,1)S(1)}, u32[]{:S(2)}, u32[]{:S(2)}) collective-permute-start(bf16[16,128,128]{2,1,0:T(8,128)(2,1)S(1)} %all_gather.3.own), channel_id=1, source_target_pairs={{0,32},{16,1008},{32,64},{48,16},{64,96},{80,48},{96,128},{112,80}... | collective-permute-start | bytes 1572872 | tf_op jit(solution)/shard_map/gather_near/ppermute | solution.py:90
  54.8 0.7 copy-start.5
  56.1 1.0 copy-start.3
  57.7 5.5 %copy-start.1 = (bf16[1,128,128]{2,1,0:T(8,128)(2,1)S(1)}, bf16[1,128,128]{2,1,0:T(8,128)(2,1)}, u32[]{:S(2)}) copy-start(bf16[1,128,128]{2,1,0:T(8,128)(2,1)} %param.11) | copy-start | bytes 98308
  63.1 4.3 %copy-start.2 = (bf16[128,128]{1,0:T(8,128)(2,1)S(1)}, bf16[128,128]{1,0:T(8,128)(2,1)}, u32[]{:S(2)}) copy-start(bf16[128,128]{1,0:T(8,128)(2,1)} %weight.1) | copy-start | bytes 98308
  64.1 3.3 %collective-permute-start.2 = (f32[3,128,128]{2,1,0:T(8,128)S(1)}, f32[3,128,128]{2,1,0:T(8,128)S(1)}, u32[]{:S(2)}, u32[]{:S(2)}) collective-permute-start(f32[3,128,128]{2,1,0:T(8,128)S(1)} %forward.1.mine), channel_id=1, source_target_pairs={{0,16},{16,0},{32,48},{48,32},{64,80},{80,64},{96,112},{112,96},{1... | collective-permute-start | bytes 589832 | tf_op jit(solution)/shard_map/pair/ppermute | solution.py:96
  69.5 13.3 %collective-permute-start.5 = (bf16[1056,128]{1,0:T(8,128)(2,1)S(1)}, bf16[1056,128]{1,0:T(8,128)(2,1)S(1)}, u32[]{:S(2)}, u32[]{:S(2)}) collective-permute-start(bf16[1056,128]{1,0:T(8,128)(2,1)S(1)} %get-tuple-element.22), channel_id=1, source_target_pairs={{0,32},{16,1008},{32,64},{48,16},{64,96},{80,48},{96,128},{112,80}... | collective-permute-start | bytes 811016 | tf_op jit(solution)/shard_map/scatter_near/ppermute | solution.py:90
  72.7 10.6 %collective-permute-start.4 = (bf16[1056,128]{1,0:T(8,128)(2,1)S(1)}, bf16[1056,128]{1,0:T(8,128)(2,1)S(1)}, u32[]{:S(2)}, u32[]{:S(2)}) collective-permute-start(bf16[1056,128]{1,0:T(8,128)(2,1)S(1)} %get-tuple-element.21), channel_id=1, source_target_pairs={{0,960},{16,80},{32,992},{48,112},{64,0},{80,144},{96,32},{112,176... | collective-permute-start | bytes 811016 | tf_op jit(solution)/shard_map/scatter_near/ppermute | solution.py:90
  77.7 10.8 %collective-permute-start.3 = (bf16[1056,128]{1,0:T(8,128)(2,1)S(1)}, bf16[1056,128]{1,0:T(8,128)(2,1)S(1)}, u32[]{:S(2)}, u32[]{:S(2)}) collective-permute-start(bf16[1056,128]{1,0:T(8,128)(2,1)S(1)} %get-tuple-element.20), channel_id=1, source_target_pairs={{0,992},{16,48},{32,0},{48,80},{64,32},{80,112},{96,64},{112,144},... | collective-permute-start | bytes 811016 | tf_op jit(solution)/shard_map/scatter_near/ppermute | solution.py:90
  144.9 14.6 %all-to-all-start.1 = ((f32[16,2,128]{2,1,0:T(2,128)}), f32[16,2,128]{2,1,0:T(2,128)S(1)}, u32[]{:S(2)}, u32[]{:S(2)}) async-start(f32[16,2,128]{2,1,0:T(2,128)} %broadcast_in_dim.14), calls=%async_computation.1 | async-start | bytes 32768 | tf_op jit(solution)/shard_map/weight_sum/all_to_all | solution.py:166

commit v5 on v4

--- a/solution.py
+++ b/solution.py
@@ -97,8 +97,12 @@
 
     def every(step):
         return [
-            [2 * (m + k) + core for m in range(0, chips, step)] for k in range(step) for core in range(2)
+            [2 * (m + k) + core for m in range(0, chips, step)][:: 1 - 2 * core]
+            for k in range(step) for core in range(2)
         ]
+
+    def order(chip, step):
+        return jnp.where(c == 0, chip // step, chips // step - 1 - chip // step)
 
     with jax.named_scope("gather_far"):
         other = swap(tiles)
@@ -116,12 +120,12 @@
         counts = tile_counts[0][here]
         chip = cols // 2
         active = (jnp.arange(slots)[None, :] < counts[:, None]) & (cols % 2 == c)
-        source = (z - chip) % 2 * (chips // 2) + chip // 2
+        source = (z - chip) % 2 * (chips // 2) + order(chip, 2)
         source = jnp.where(active, source, chips).astype(jnp.int32)
-        place = (sign * (z - chip)) % CLASSES * share + chip // CLASSES
+        place = (sign * (z - chip)) % CLASSES * share + order(chip, CLASSES)
         place = jnp.where(active, place, chips).astype(jnp.int32)
         spot = jnp.arange(chips)
-        chip_at = (z - sign * (spot // share)) % CLASSES + CLASSES * (spot % share)
+        chip_at = (z - sign * (spot // share)) % CLASSES + CLASSES * order(CLASSES * (spot % share), CLASSES)
         row_share = tile // wide
         row_at = ((2 * chip_at + c)[:, None] * row_share + jnp.arange(row_share)[None, :]).reshape(-1)
         perm = (row_at[:, None] == jnp.arange(tile)[None, :]).astype(BF16)

time: 161 us -> 160 us (level)
  the two profiles are of different devices: /device:TPU:64 before, /device:TPU:1 now
where the time goes in v5:
time: 160 us; the launch traced here: 159 us
  blocking collectives  82.4 us (52%)
  starting transfers between devices  45.6 us (28%)
  waiting for transfers between devices  21.6 us (14%)
  local copies, waits for them, and re-layouts  4.79 us (3%)
  Pallas kernels  3.04 us (2%)
    all_to_all x1, blocking collectives, shards(): lax.all_to_all(message, 'wide', 0, 0, axis_index_groups=every(CLASSES))  51.1 us
    all_gather x1, blocking collectives, shards(): held = lax.all_gather(feat, 'wide', axis_index_groups=every(2))  31.3 us
    ppermute x2, starting transfers between devices, swap(): return lax.ppermute(x, 'wide', [(i, i ^ 1) for i in range(wide)])  29 us
    ppermute x4, waiting for transfers between devices, send(): lax.ppermute(x, 'wide', [(2 * i + k, 2 * ((i + (d if k == 0 else -d)) % c...  14.8 us
    ppermute x4, starting transfers between devices, send(): lax.ppermute(x, 'wide', [(2 * i + k, 2 * ((i + (d if k == 0 else -d)) % c...  9.85 us
    all_to_all x1, starting transfers between devices, shards(): lax.all_to_all(jnp.broadcast_to(grad[None], (groups, row_share, tile)), '...  6.75 us
    all_to_all x1, waiting for transfers between devices, shards(): lax.all_to_all(jnp.broadcast_to(grad[None], (groups, row_share, tile)), '...  5.81 us
  transfers between devices with their start and end apart: 7, of which 6 were waited for; matrix products, arithmetic and copies ran while one was open for 2% of the time, Pallas kernels for 0%

profile of v5, /device:TPU:1, one launch (start us, length us, event | category | flops | bytes accessed | tf_op | source)
XLA Modules:
  0.0 159.5 jit_solution(9820086698557145415)
XLA Ops:
  0.6 16.1 %collective-permute-start = (bf16[1,128,8,128]{3,2,1,0:T(8,128)(2,1)}, bf16[1,128,8,128]{3,2,1,0:T(8,128)(2,1)S(1)}, u32[]{:S(2)}, u32[]{:S(2)}) collective-permute-start(bf16[1,128,8,128]{3,2,1,0:T(8,128)(2,1)} %param.8), channel_id=1, source_target_pairs={{0,16},{16,0},{32,48},{48,32},{64,80},{80,64},{96,112},{112,96},{1... | collective-permute-start | bytes 786440 | tf_op jit(solution)/shard_map/gather_far/ppermute | solution.py:96
  16.9 0.1 add.136
  17.0 0.5 copy-done.4
  17.5 31.3 %all_gather.3.own = bf16[16,128,128]{2,1,0:T(8,128)(2,1)S(1)} all-gather(bf16[1,128,128]{2,1,0:T(8,128)(2,1)S(1)} %copy-done.4), channel_id=1, replica_groups={{0,64,128,192,256,320,384,448,512,576,640,704,768,832,896,960},{976,912..., dimensions={0}, use_global_device_ids=true | all-gather | bytes 557056 | tf_op jit(solution)/shard_map/gather_far/all_gather | solution.py:109
  48.8 2.7 %collective-permute-start.1 = (bf16[16,128,128]{2,1,0:T(8,128)(2,1)S(1)}, bf16[16,128,128]{2,1,0:T(8,128)(2,1)S(1)}, u32[]{:S(2)}, u32[]{:S(2)}) collective-permute-start(bf16[16,128,128]{2,1,0:T(8,128)(2,1)S(1)} %all_gather.3.own), channel_id=1, source_target_pairs={{0,32},{16,1008},{32,64},{48,16},{64,96},{80,48},{96,128},{112,80}... | collective-permute-start | bytes 1572872 | tf_op jit(solution)/shard_map/gather_near/ppermute | solution.py:90
  51.5 0.6 copy-done.5
  52.1 0.1 copy.29
  52.2 0.6 gather_fusion.1
  52.8 0.6 gather_fusion
  53.4 0.3 copy-done.3
  53.7 0.2 copy.30
  54.0 0.1 copy.32.rows_mine
  54.1 0.2 copy.31
  54.4 0.1 copy.33.rows_theirs
  54.6 4.1 %collective-permute-done.1.beside = bf16[16,128,128]{2,1,0:T(8,128)(2,1)S(1)} collective-permute-done((bf16[16,128,128]{2,1,0:T(8,128)(2,1)S(1)}, bf16[16,128,128]{2,1,0:T(8,128)(2,1)S(1)}, u32[]{:S(2)}, u32[]{:S(2)}) %collective-permute-start.1) | collective-permute-done | bytes 524320 | tf_op jit(solution)/shard_map/gather_near/ppermute | solution.py:90
  58.7 0.9 forward.1.mine
  59.6 12.9 %collective-permute-start.2 = (f32[3,128,128]{2,1,0:T(8,128)S(1)}, f32[3,128,128]{2,1,0:T(8,128)S(1)}, u32[]{:S(2)}, u32[]{:S(2)}) collective-permute-start(f32[3,128,128]{2,1,0:T(8,128)S(1)} %forward.1.mine), channel_id=1, source_target_pairs={{0,16},{16,0},{32,48},{48,32},{64,80},{80,64},{96,112},{112,96},{1... | collective-permute-start | bytes 589832 | tf_op jit(solution)/shard_map/pair/ppermute | solution.py:96
  72.6 1.0 collective-permute-done.2.theirs
  73.6 2.1 %backward.1 = (bf16[128,128]{1,0:T(8,128)(2,1)}, bf16[1056,128]{1,0:T(8,128)(2,1)S(1)}, bf16[1056,128]{1,0:T(8,128)(2,1)S(1)}, bf16[1056,128]{1,0:T(8,128)(2,1)S(1)}, bf16[1056,128]{1,0:T(8,128)(2,1)S(1)}) custom-call(s32[2,8]{1,0:T(2,128)S(1)} %fusion.3.pos, f32[3,128,128]{2,1,0:T(8,128)S(1)} %forward.1.mine, ...), custom_call_target="tpu_custom_call" | custom-call | tf_op jit(solution)/shard_map/backward/pallas_call | solution.py:143
  75.7 1.9 %collective-permute-start.5 = (bf16[1056,128]{1,0:T(8,128)(2,1)S(1)}, bf16[1056,128]{1,0:T(8,128)(2,1)S(1)}, u32[]{:S(2)}, u32[]{:S(2)}) collective-permute-start(bf16[1056,128]{1,0:T(8,128)(2,1)S(1)} %get-tuple-element.22), channel_id=1, source_target_pairs={{0,32},{16,1008},{32,64},{48,16},{64,96},{80,48},{96,128},{112,80}... | collective-permute-start | bytes 811016 | tf_op jit(solution)/shard_map/scatter_near/ppermute | solution.py:90
  77.6 1.9 %collective-permute-start.4 = (bf16[1056,128]{1,0:T(8,128)(2,1)S(1)}, bf16[1056,128]{1,0:T(8,128)(2,1)S(1)}, u32[]{:S(2)}, u32[]{:S(2)}) collective-permute-start(bf16[1056,128]{1,0:T(8,128)(2,1)S(1)} %get-tuple-element.21), channel_id=1, source_target_pairs={{0,960},{16,80},{32,992},{48,112},{64,0},{80,144},{96,32},{112,176... | collective-permute-start | bytes 811016 | tf_op jit(solution)/shard_map/scatter_near/ppermute | solution.py:90
  79.6 3.4 %collective-permute-start.3 = (bf16[1056,128]{1,0:T(8,128)(2,1)S(1)}, bf16[1056,128]{1,0:T(8,128)(2,1)S(1)}, u32[]{:S(2)}, u32[]{:S(2)}) collective-permute-start(bf16[1056,128]{1,0:T(8,128)(2,1)S(1)} %get-tuple-element.20), channel_id=1, source_target_pairs={{0,992},{16,48},{32,0},{48,80},{64,32},{80,112},{96,64},{112,144},... | collective-permute-start | bytes 811016 | tf_op jit(solution)/shard_map/scatter_near/ppermute | solution.py:90
  82.9 0.3 collective-permute-done.5
  83.2 5.3 %collective-permute-done.4 = bf16[1056,128]{1,0:T(8,128)(2,1)S(1)} collective-permute-done((bf16[1056,128]{1,0:T(8,128)(2,1)S(1)}, bf16[1056,128]{1,0:T(8,128)(2,1)S(1)}, u32[]{:S(2)}, u32[]{:S(2)}) %collective-permute-start.4) | collective-permute-done | bytes 270368 | tf_op jit(solution)/shard_map/scatter_near/ppermute | solution.py:90
  88.5 5.2 %collective-permute-done.3 = bf16[1056,128]{1,0:T(8,128)(2,1)S(1)} collective-permute-done((bf16[1056,128]{1,0:T(8,128)(2,1)S(1)}, bf16[1056,128]{1,0:T(8,128)(2,1)S(1)}, u32[]{:S(2)}, u32[]{:S(2)}) %collective-permute-start.3) | collective-permute-done | bytes 270368 | tf_op jit(solution)/shard_map/scatter_near/ppermute | solution.py:90
  93.6 0.1 convert_add_fusion
  93.9 51.1 %all_to_all.10 = bf16[8,132,128]{2,1,0:T(8,128)(2,1)S(1)} all-to-all(bf16[8,132,128]{2,1,0:T(8,128)(2,1)S(1)} %pad_maximum_fusion), channel_id=1, replica_groups={{0,128,256,384,512,640,768,896},{912,784,656,528,400,272,144,16},{32,16..., dimensions={0} | all-to-all | bytes 540672 | tf_op jit(solution)/shard_map/scatter_far/all_to_all | solution.py:164
  145.1 0.6 broadcast_in_dim.14
  145.7 6.8 %all-to-all-start.1 = ((f32[16,2,128]{2,1,0:T(2,128)}), f32[16,2,128]{2,1,0:T(2,128)S(1)}, u32[]{:S(2)}, u32[]{:S(2)}) async-start(f32[16,2,128]{2,1,0:T(2,128)} %broadcast_in_dim.14), calls=%async_computation.1 | async-start | bytes 32768 | tf_op jit(solution)/shard_map/weight_sum/all_to_all | solution.py:170
  152.4 0.6 fusion
  153.1 5.8 %all-to-all-done.1 = f32[16,2,128]{2,1,0:T(2,128)S(1)} async-done(((f32[16,2,128]{2,1,0:T(2,128)}), f32[16,2,128]{2,1,0:T(2,128)S(1)}, u32[]{:S(2)}, u32[]{:S(2)}) %all-to-all-start.1) | async-done | bytes 16416 | tf_op jit(solution)/shard_map/weight_sum/all_to_all | solution.py:170
  158.9 0.6 reduce_sum.19
  (23 shorter events, 0.5 us)
Async XLA Ops:
  0.6 52.2 %copy-start = (s32[1,64]{1,0:T(1,128)S(1)}, s32[1,64]{1,0:T(1,128)}, u32[]{:S(2)}) copy-start(s32[1,64]{1,0:T(1,128)} %param.10) | copy-start | bytes 772
  0.6 48.1 %collective-permute-start = (bf16[1,128,8,128]{3,2,1,0:T(8,128)(2,1)}, bf16[1,128,8,128]{3,2,1,0:T(8,128)(2,1)S(1)}, u32[]{:S(2)}, u32[]{:S(2)}) collective-permute-start(bf16[1,128,8,128]{3,2,1,0:T(8,128)(2,1)} %param.8), channel_id=1, source_target_pairs={{0,16},{16,0},{32,48},{48,32},{64,80},{80,64},{96,112},{112,96},{1... | collective-permute-start | bytes 786440 | tf_op jit(solution)/shard_map/gather_far/ppermute | solution.py:96
  16.7 0.8 copy-start.4
  48.8 9.9 %collective-permute-start.1 = (bf16[16,128,128]{2,1,0:T(8,128)(2,1)S(1)}, bf16[16,128,128]{2,1,0:T(8,128)(2,1)S(1)}, u32[]{:S(2)}, u32[]{:S(2)}) collective-permute-start(bf16[16,128,128]{2,1,0:T(8,128)(2,1)S(1)} %all_gather.3.own), channel_id=1, source_target_pairs={{0,32},{16,1008},{32,64},{48,16},{64,96},{80,48},{96,128},{112,80}... | collective-permute-start | bytes 1572872 | tf_op jit(solution)/shard_map/gather_near/ppermute | solution.py:90
  51.5 0.7 copy-start.5
  52.8 1.0 copy-start.3
  54.4 4.3 %copy-start.1 = (bf16[1,128,128]{2,1,0:T(8,128)(2,1)S(1)}, bf16[1,128,128]{2,1,0:T(8,128)(2,1)}, u32[]{:S(2)}) copy-start(bf16[1,128,128]{2,1,0:T(8,128)(2,1)} %param.11) | copy-start | bytes 98308
  58.7 14.9 %copy-start.2 = (bf16[128,128]{1,0:T(8,128)(2,1)S(1)}, bf16[128,128]{1,0:T(8,128)(2,1)}, u32[]{:S(2)}) copy-start(bf16[128,128]{1,0:T(8,128)(2,1)} %weight.1) | copy-start | bytes 98308
  59.6 14.0 %collective-permute-start.2 = (f32[3,128,128]{2,1,0:T(8,128)S(1)}, f32[3,128,128]{2,1,0:T(8,128)S(1)}, u32[]{:S(2)}, u32[]{:S(2)}) collective-permute-start(f32[3,128,128]{2,1,0:T(8,128)S(1)} %forward.1.mine), channel_id=1, source_target_pairs={{0,16},{16,0},{32,48},{48,32},{64,80},{80,64},{96,112},{112,96},{1... | collective-permute-start | bytes 589832 | tf_op jit(solution)/shard_map/pair/ppermute | solution.py:96
  75.7 7.5 %collective-permute-start.5 = (bf16[1056,128]{1,0:T(8,128)(2,1)S(1)}, bf16[1056,128]{1,0:T(8,128)(2,1)S(1)}, u32[]{:S(2)}, u32[]{:S(2)}) collective-permute-start(bf16[1056,128]{1,0:T(8,128)(2,1)S(1)} %get-tuple-element.22), channel_id=1, source_target_pairs={{0,32},{16,1008},{32,64},{48,16},{64,96},{80,48},{96,128},{112,80}... | collective-permute-start | bytes 811016 | tf_op jit(solution)/shard_map/scatter_near/ppermute | solution.py:90
  77.6 10.8 %collective-permute-start.4 = (bf16[1056,128]{1,0:T(8,128)(2,1)S(1)}, bf16[1056,128]{1,0:T(8,128)(2,1)S(1)}, u32[]{:S(2)}, u32[]{:S(2)}) collective-permute-start(bf16[1056,128]{1,0:T(8,128)(2,1)S(1)} %get-tuple-element.21), channel_id=1, source_target_pairs={{0,960},{16,80},{32,992},{48,112},{64,0},{80,144},{96,32},{112,176... | collective-permute-start | bytes 811016 | tf_op jit(solution)/shard_map/scatter_near/ppermute | solution.py:90
  79.6 14.1 %collective-permute-start.3 = (bf16[1056,128]{1,0:T(8,128)(2,1)S(1)}, bf16[1056,128]{1,0:T(8,128)(2,1)S(1)}, u32[]{:S(2)}, u32[]{:S(2)}) collective-permute-start(bf16[1056,128]{1,0:T(8,128)(2,1)S(1)} %get-tuple-element.20), channel_id=1, source_target_pairs={{0,992},{16,48},{32,0},{48,80},{64,32},{80,112},{96,64},{112,144},... | collective-permute-start | bytes 811016 | tf_op jit(solution)/shard_map/scatter_near/ppermute | solution.py:90
  145.7 13.2 %all-to-all-start.1 = ((f32[16,2,128]{2,1,0:T(2,128)}), f32[16,2,128]{2,1,0:T(2,128)S(1)}, u32[]{:S(2)}, u32[]{:S(2)}) async-start(f32[16,2,128]{2,1,0:T(2,128)} %broadcast_in_dim.14), calls=%async_computation.1 | async-start | bytes 32768 | tf_op jit(solution)/shard_map/weight_sum/all_to_all | solution.py:170

commit v6 on v4

--- a/solution.py
+++ b/solution.py
@@ -101,14 +101,13 @@
         ]
 
     with jax.named_scope("gather_far"):
-        other = swap(tiles)
         held = lax.all_gather(feat, "wide", axis_index_groups=every(2))
-        held, tiles, other, tile_cols, tile_counts = lax.optimization_barrier(
-            (held, tiles, other, tile_cols, tile_counts)
-        )
     with jax.named_scope("gather_near"):
         beside = send(held, 1)
     with jax.named_scope("prepare"):
+        after = lax.optimization_barrier(held[0, :8] + held[-1, :8])
+        _, tiles, tile_cols, tile_counts = lax.optimization_barrier((after, tiles, tile_cols, tile_counts))
+        other = swap(tiles)
         rows = [t[0].reshape(tile, slots * tile) for t in (tiles, other)]
         flipped = [r.T for r in rows]
         here = jnp.stack([w, w ^ 1])

time: 161 us -> 158 us (0.981)
  the two profiles are of different devices: /device:TPU:64 before, /device:TPU:1 now
where the time goes in v6:
time: 158 us; the launch traced here: 155 us
  blocking collectives  97 us (61%)
  starting transfers between devices  30.9 us (20%)
  waiting for transfers between devices  17.6 us (11%)
  local copies, waits for them, and re-layouts  4.7 us (3%)
  Pallas kernels  3.04 us (2%)
    all_to_all x1, blocking collectives, shards(): lax.all_to_all(message, 'wide', 0, 0, axis_index_groups=every(CLASSES))  51.6 us
    all_gather x1, blocking collectives, shards(): held = lax.all_gather(feat, 'wide', axis_index_groups=every(2))  45.3 us
    ppermute x2, starting transfers between devices, swap(): return lax.ppermute(x, 'wide', [(i, i ^ 1) for i in range(wide)])  14.5 us
    ppermute x4, waiting for transfers between devices, send(): lax.ppermute(x, 'wide', [(2 * i + k, 2 * ((i + (d if k == 0 else -d)) % c...  10.8 us
    ppermute x4, starting transfers between devices, send(): lax.ppermute(x, 'wide', [(2 * i + k, 2 * ((i + (d if k == 0 else -d)) % c...  10.1 us
    all_to_all x1, starting transfers between devices, shards(): lax.all_to_all(jnp.broadcast_to(grad[None], (groups, row_share, tile)), '...  6.26 us
    all_to_all x1, waiting for transfers between devices, shards(): lax.all_to_all(jnp.broadcast_to(grad[None], (groups, row_share, tile)), '...  5.81 us
  transfers between devices with their start and end apart: 7, of which 5 were waited for; matrix products, arithmetic and copies ran while one was open for 2% of the time, Pallas kernels for 0%

profile of v6, /device:TPU:1, one launch (start us, length us, event | category | flops | bytes accessed | tf_op | source)
XLA Modules:
  0.0 155.2 jit_solution(11285977129252444770)
XLA Ops:
  0.7 45.3 %all_gather.3.own = bf16[16,128,128]{2,1,0:T(8,128)(2,1)S(1)} all-gather(bf16[1,128,128]{2,1,0:T(8,128)(2,1)} %param.6), channel_id=1, replica_groups={{0,64,128,192,256,320,384,448,512,576,640,704,768,832,896,960},{16,80,1..., dimensions={0}, use_global_device_ids=true | all-gather | bytes 557056 | tf_op jit(solution)/shard_map/gather_far/all_gather | solution.py:104
  46.0 2.9 %collective-permute-start = (bf16[16,128,128]{2,1,0:T(8,128)(2,1)S(1)}, bf16[16,128,128]{2,1,0:T(8,128)(2,1)S(1)}, u32[]{:S(2)}, u32[]{:S(2)}) collective-permute-start(bf16[16,128,128]{2,1,0:T(8,128)(2,1)S(1)} %all_gather.3.own), channel_id=1, source_target_pairs={{0,32},{16,1008},{32,64},{48,16},{64,96},{80,48},{96,128},{112,80}... | collective-permute-start | bytes 1572872 | tf_op jit(solution)/shard_map/gather_near/ppermute | solution.py:90
  48.9 9.0 %collective-permute-start.1 = (bf16[1,128,8,128]{3,2,1,0:T(8,128)(2,1)S(1)}, bf16[1,128,8,128]{3,2,1,0:T(8,128)(2,1)S(1)}, u32[]{:S(2)}, u32[]{:S(2)}) collective-permute-start(bf16[1,128,8,128]{3,2,1,0:T(8,128)(2,1)S(1)} %copy-done.3), channel_id=1, source_target_pairs={{0,16},{16,0},{32,48},{48,32},{64,80},{80,64},{96,112},{112,96},{1... | collective-permute-start | bytes 786440 | tf_op jit(solution)/shard_map/prepare/ppermute | solution.py:96
  57.9 0.7 copy-done.4
  58.6 0.1 copy.29
  58.8 0.1 fusion.18
  58.9 0.6 gather_fusion.1
  59.4 0.6 gather_fusion
  60.1 0.1 fusion.8
  60.1 0.2 copy.30
  60.4 0.1 copy.32.rows_mine
  60.5 0.1 add.130
  60.7 0.2 copy.31
  61.0 0.1 copy.33.rows_theirs
  61.2 0.6 copy-done.1
  61.8 0.9 forward.1.mine
  62.7 5.6 %collective-permute-start.2 = (f32[3,128,128]{2,1,0:T(8,128)S(1)}, f32[3,128,128]{2,1,0:T(8,128)S(1)}, u32[]{:S(2)}, u32[]{:S(2)}) collective-permute-start(f32[3,128,128]{2,1,0:T(8,128)S(1)} %forward.1.mine), channel_id=1, source_target_pairs={{0,16},{16,0},{32,48},{48,32},{64,80},{80,64},{96,112},{112,96},{1... | collective-permute-start | bytes 589832 | tf_op jit(solution)/shard_map/pair/ppermute | solution.py:96
  68.3 1.0 collective-permute-done.2.theirs
  69.3 2.1 %backward.1 = (bf16[128,128]{1,0:T(8,128)(2,1)}, bf16[1056,128]{1,0:T(8,128)(2,1)S(1)}, bf16[1056,128]{1,0:T(8,128)(2,1)S(1)}, bf16[1056,128]{1,0:T(8,128)(2,1)S(1)}, bf16[1056,128]{1,0:T(8,128)(2,1)S(1)}) custom-call(s32[2,8]{1,0:T(2,128)S(1)} %fusion.9.pos, f32[3,128,128]{2,1,0:T(8,128)S(1)} %forward.1.mine, ...), custom_call_target="tpu_custom_call" | custom-call | tf_op jit(solution)/shard_map/backward/pallas_call | solution.py:138
  71.4 2.1 %collective-permute-start.5 = (bf16[1056,128]{1,0:T(8,128)(2,1)S(1)}, bf16[1056,128]{1,0:T(8,128)(2,1)S(1)}, u32[]{:S(2)}, u32[]{:S(2)}) collective-permute-start(bf16[1056,128]{1,0:T(8,128)(2,1)S(1)} %get-tuple-element.18), channel_id=1, source_target_pairs={{0,32},{16,1008},{32,64},{48,16},{64,96},{80,48},{96,128},{112,80}... | collective-permute-start | bytes 811016 | tf_op jit(solution)/shard_map/scatter_near/ppermute | solution.py:90
  73.5 2.4 %collective-permute-start.4 = (bf16[1056,128]{1,0:T(8,128)(2,1)S(1)}, bf16[1056,128]{1,0:T(8,128)(2,1)S(1)}, u32[]{:S(2)}, u32[]{:S(2)}) collective-permute-start(bf16[1056,128]{1,0:T(8,128)(2,1)S(1)} %get-tuple-element.17), channel_id=1, source_target_pairs={{0,960},{16,80},{32,992},{48,112},{64,0},{80,144},{96,32},{112,176... | collective-permute-start | bytes 811016 | tf_op jit(solution)/shard_map/scatter_near/ppermute | solution.py:90
  75.9 2.7 %collective-permute-start.3 = (bf16[1056,128]{1,0:T(8,128)(2,1)S(1)}, bf16[1056,128]{1,0:T(8,128)(2,1)S(1)}, u32[]{:S(2)}, u32[]{:S(2)}) collective-permute-start(bf16[1056,128]{1,0:T(8,128)(2,1)S(1)} %get-tuple-element.16), channel_id=1, source_target_pairs={{0,992},{16,48},{32,0},{48,80},{64,32},{80,112},{96,64},{112,144},... | collective-permute-start | bytes 811016 | tf_op jit(solution)/shard_map/scatter_near/ppermute | solution.py:90
  78.6 0.3 collective-permute-done.5
  78.9 5.2 %collective-permute-done.4 = bf16[1056,128]{1,0:T(8,128)(2,1)S(1)} collective-permute-done((bf16[1056,128]{1,0:T(8,128)(2,1)S(1)}, bf16[1056,128]{1,0:T(8,128)(2,1)S(1)}, u32[]{:S(2)}, u32[]{:S(2)}) %collective-permute-start.4) | collective-permute-done | bytes 270368 | tf_op jit(solution)/shard_map/scatter_near/ppermute | solution.py:90
  84.1 5.3 %collective-permute-done.3 = bf16[1056,128]{1,0:T(8,128)(2,1)S(1)} collective-permute-done((bf16[1056,128]{1,0:T(8,128)(2,1)S(1)}, bf16[1056,128]{1,0:T(8,128)(2,1)S(1)}, u32[]{:S(2)}, u32[]{:S(2)}) %collective-permute-start.3) | collective-permute-done | bytes 270368 | tf_op jit(solution)/shard_map/scatter_near/ppermute | solution.py:90
  89.4 0.1 convert_add_fusion
  89.6 51.6 %all_to_all.10 = bf16[8,132,128]{2,1,0:T(8,128)(2,1)S(1)} all-to-all(bf16[8,132,128]{2,1,0:T(8,128)(2,1)S(1)} %pad_maximum_fusion), channel_id=1, replica_groups={{0,128,256,384,512,640,768,896},{16,144,272,400,528,656,784,912},{32,16..., dimensions={0} | all-to-all | bytes 540672 | tf_op jit(solution)/shard_map/scatter_far/all_to_all | solution.py:159
  141.3 0.6 broadcast_in_dim.14
  141.9 6.3 %all-to-all-start.1 = ((f32[16,2,128]{2,1,0:T(2,128)}), f32[16,2,128]{2,1,0:T(2,128)S(1)}, u32[]{:S(2)}, u32[]{:S(2)}) async-start(f32[16,2,128]{2,1,0:T(2,128)} %broadcast_in_dim.14), calls=%async_computation.1 | async-start | bytes 32768 | tf_op jit(solution)/shard_map/weight_sum/all_to_all | solution.py:165
  148.2 0.6 fusion
  148.8 5.8 %all-to-all-done.1 = f32[16,2,128]{2,1,0:T(2,128)S(1)} async-done(((f32[16,2,128]{2,1,0:T(2,128)}), f32[16,2,128]{2,1,0:T(2,128)S(1)}, u32[]{:S(2)}, u32[]{:S(2)}) %all-to-all-start.1) | async-done | bytes 16416 | tf_op jit(solution)/shard_map/weight_sum/all_to_all | solution.py:165
  154.6 0.6 reduce_sum.19
  (21 shorter events, 0.3 us)
Async XLA Ops:
  0.6 58.8 %copy-start = (s32[1,64]{1,0:T(1,128)S(1)}, s32[1,64]{1,0:T(1,128)}, u32[]{:S(2)}) copy-start(s32[1,64]{1,0:T(1,128)} %param.10) | copy-start | bytes 772
  0.6 48.3 %copy-start.3 = (bf16[1,128,8,128]{3,2,1,0:T(8,128)(2,1)S(1)}, bf16[1,128,8,128]{3,2,1,0:T(8,128)(2,1)}, u32[]{:S(2)}) copy-start(bf16[1,128,8,128]{3,2,1,0:T(8,128)(2,1)} %param.8) | copy-start | bytes 786436
  46.0 15.2 %collective-permute-start = (bf16[16,128,128]{2,1,0:T(8,128)(2,1)S(1)}, bf16[16,128,128]{2,1,0:T(8,128)(2,1)S(1)}, u32[]{:S(2)}, u32[]{:S(2)}) collective-permute-start(bf16[16,128,128]{2,1,0:T(8,128)(2,1)S(1)} %all_gather.3.own), channel_id=1, source_target_pairs={{0,32},{16,1008},{32,64},{48,16},{64,96},{80,48},{96,128},{112,80}... | collective-permute-start | bytes 1572872 | tf_op jit(solution)/shard_map/gather_near/ppermute | solution.py:90
  48.9 11.8 %collective-permute-start.1 = (bf16[1,128,8,128]{3,2,1,0:T(8,128)(2,1)S(1)}, bf16[1,128,8,128]{3,2,1,0:T(8,128)(2,1)S(1)}, u32[]{:S(2)}, u32[]{:S(2)}) collective-permute-start(bf16[1,128,8,128]{3,2,1,0:T(8,128)(2,1)S(1)} %copy-done.3), channel_id=1, source_target_pairs={{0,16},{16,0},{32,48},{48,32},{64,80},{80,64},{96,112},{112,96},{1... | collective-permute-start | bytes 786440 | tf_op jit(solution)/shard_map/prepare/ppermute | solution.py:96
  57.9 0.7 copy-start.4
  61.0 0.8 copy-start.1
  61.7 7.5 %copy-start.2 = (bf16[128,128]{1,0:T(8,128)(2,1)S(1)}, bf16[128,128]{1,0:T(8,128)(2,1)}, u32[]{:S(2)}) copy-start(bf16[128,128]{1,0:T(8,128)(2,1)} %weight.1) | copy-start | bytes 98308
  62.7 6.6 %collective-permute-start.2 = (f32[3,128,128]{2,1,0:T(8,128)S(1)}, f32[3,128,128]{2,1,0:T(8,128)S(1)}, u32[]{:S(2)}, u32[]{:S(2)}) collective-permute-start(f32[3,128,128]{2,1,0:T(8,128)S(1)} %forward.1.mine), channel_id=1, source_target_pairs={{0,16},{16,0},{32,48},{48,32},{64,80},{80,64},{96,112},{112,96},{1... | collective-permute-start | bytes 589832 | tf_op jit(solution)/shard_map/pair/ppermute | solution.py:96
  71.4 7.5 %collective-permute-start.5 = (bf16[1056,128]{1,0:T(8,128)(2,1)S(1)}, bf16[1056,128]{1,0:T(8,128)(2,1)S(1)}, u32[]{:S(2)}, u32[]{:S(2)}) collective-permute-start(bf16[1056,128]{1,0:T(8,128)(2,1)S(1)} %get-tuple-element.18), channel_id=1, source_target_pairs={{0,32},{16,1008},{32,64},{48,16},{64,96},{80,48},{96,128},{112,80}... | collective-permute-start | bytes 811016 | tf_op jit(solution)/shard_map/scatter_near/ppermute | solution.py:90
  73.5 10.6 %collective-permute-start.4 = (bf16[1056,128]{1,0:T(8,128)(2,1)S(1)}, bf16[1056,128]{1,0:T(8,128)(2,1)S(1)}, u32[]{:S(2)}, u32[]{:S(2)}) collective-permute-start(bf16[1056,128]{1,0:T(8,128)(2,1)S(1)} %get-tuple-element.17), channel_id=1, source_target_pairs={{0,960},{16,80},{32,992},{48,112},{64,0},{80,144},{96,32},{112,176... | collective-permute-start | bytes 811016 | tf_op jit(solution)/shard_map/scatter_near/ppermute | solution.py:90
  75.9 13.5 %collective-permute-start.3 = (bf16[1056,128]{1,0:T(8,128)(2,1)S(1)}, bf16[1056,128]{1,0:T(8,128)(2,1)S(1)}, u32[]{:S(2)}, u32[]{:S(2)}) collective-permute-start(bf16[1056,128]{1,0:T(8,128)(2,1)S(1)} %get-tuple-element.16), channel_id=1, source_target_pairs={{0,992},{16,48},{32,0},{48,80},{64,32},{80,112},{96,64},{112,144},... | collective-permute-start | bytes 811016 | tf_op jit(solution)/shard_map/scatter_near/ppermute | solution.py:90
  141.9 12.7 %all-to-all-start.1 = ((f32[16,2,128]{2,1,0:T(2,128)}), f32[16,2,128]{2,1,0:T(2,128)S(1)}, u32[]{:S(2)}, u32[]{:S(2)}) async-start(f32[16,2,128]{2,1,0:T(2,128)} %broadcast_in_dim.14), calls=%async_computation.1 | async-start | bytes 32768 | tf_op jit(solution)/shard_map/weight_sum/all_to_all | solution.py:165

commit v7 on v6

--- a/solution.py
+++ b/solution.py
@@ -32,7 +32,7 @@
 
 def backward(
     pos, mine, theirs, cols_mine, cols_theirs, weight, perm,
-    activated, out0, out1, out2, out3, total,
+    activated, ordered, out0, out1, out2, out3, total,
 ):
     slots = pos.shape[1]
     tile = weight.shape[0]
@@ -64,15 +64,13 @@
             total[pos[r, s]] += term
     top = grad.astype(BF16)
     rest = (grad - top.astype(F32)).astype(BF16)
-    ordered_top = jnp.dot(perm[...], top, preferred_element_type=F32).astype(BF16)
-    ordered_rest = jnp.dot(perm[...], rest, preferred_element_type=F32).astype(BF16)
+    ordered[...] = jnp.dot(perm[...], top, preferred_element_type=F32) + jnp.dot(
+        perm[...], rest, preferred_element_type=F32
+    )
     share = blocks // CLASSES
-    rows = perm.shape[0] // CLASSES
     for a, out in enumerate((out0, out1, out2, out3)):
         for k in range(share):
-            out[pl.ds(k * tile, tile), :] = total[a * share + k].astype(BF16)
-        out[pl.ds(share * tile, rows), :] = ordered_top[a * rows : (a + 1) * rows]
-        out[pl.ds(share * tile + rows, rows), :] = ordered_rest[a * rows : (a + 1) * rows]
+            out[k] = total[a * share + k].astype(BF16)
 
 
 def shards(features, weight, tiles, tile_cols, tile_counts, cotangent):
@@ -134,24 +132,32 @@
     )(source, held, beside, *rows, cotangent[0])
     with jax.named_scope("pair"):
         theirs = swap(mixed)
-    extra = share * row_share
-    activated, *parts = pl.pallas_call(
+    activated, grad, *parts = pl.pallas_call(
         backward,
-        out_shape=[jax.ShapeDtypeStruct((tile, tile), BF16)]
-        + [jax.ShapeDtypeStruct((share * tile + 2 * extra, tile), BF16)] * CLASSES,
+        out_shape=[
+            jax.ShapeDtypeStruct((tile, tile), BF16),
+            jax.ShapeDtypeStruct((tile // 2, tile), F32),
+        ]
+        + [jax.ShapeDtypeStruct((share, tile, tile), BF16)] * CLASSES,
         in_specs=[SMEM] + [VMEM] * 6,
-        out_specs=[VMEM] * (1 + CLASSES),
+        out_specs=[VMEM] * (2 + CLASSES),
         scratch_shapes=[pltpu.VMEM((chips + 1, tile, tile), F32)],
         compiler_params=PARAMS,
         name="backward",
     )(place, mixed, theirs, *flipped, weight, perm)
+    with jax.named_scope("weight_groups"):
+        groups = lax.axis_size("narrow")
+        grad = lax.all_to_all(jnp.broadcast_to(grad[None], (groups,) + grad.shape), "narrow", 0, 0).sum(0)
+        grads = grad.reshape(CLASSES, share, row_share, tile)
     with jax.named_scope("scatter_near"):
         whole = parts[0].astype(F32)
         for part, d in zip(parts[1:], NEAR[1:]):
             whole += send(part, -d).astype(F32)
-        main = whole[: share * tile].reshape(share, tile, tile).astype(BF16)
-        grad = whole[share * tile : share * tile + extra] + whole[share * tile + extra :]
-        grad = grad.reshape(share, row_share, tile)
+        main = whole.astype(BF16)
+    with jax.named_scope("weight_near"):
+        grad = grads[0]
+        for a, d in list(enumerate(NEAR))[1:]:
+            grad += send(grads[a], -d)
     with jax.named_scope("scatter_far"):
         top = grad.astype(BF16)
         rest = (grad - top.astype(F32)).astype(BF16)
@@ -159,13 +165,7 @@
         got = lax.all_to_all(message, "wide", 0, 0, axis_index_groups=every(CLASSES))
         whole = got.astype(F32).sum(0)
         feature_grad = whole[:tile].astype(BF16)
-        grad = whole[tile : tile + row_share] + whole[tile + row_share :]
-    with jax.named_scope("weight_sum"):
-        groups = lax.axis_size("narrow")
-        copies = lax.all_to_all(
-            jnp.broadcast_to(grad[None], (groups, row_share, tile)), "narrow", 0, 0
-        )
-        weight_grad = copies.sum(0)
+        weight_grad = whole[tile : tile + row_share] + whole[tile + row_share :]
     return (activated[None], feature_grad[None], weight_grad)
 
 

time: 158 us -> 157 us (level)
  the two profiles are of different devices: /device:TPU:1 before, /device:TPU:32 now
where the time goes in v7:
time: 157 us; the launch traced here: 156 us
  blocking collectives  103 us (66%)
  starting transfers between devices  34.2 us (22%)
  waiting for transfers between devices  9.92 us (6%)
  local copies, waits for them, and re-layouts  4.32 us (3%)
  Pallas kernels  3.04 us (2%)
    all_to_all x1, blocking collectives, shards(): lax.all_to_all(message, 'wide', 0, 0, axis_index_groups=every(CLASSES))  52.9 us
    all_gather x1, blocking collectives, shards(): held = lax.all_gather(feat, 'wide', axis_index_groups=every(2))  50 us
    ppermute x7, starting transfers between devices, send(): lax.ppermute(x, 'wide', [(2 * i + k, 2 * ((i + (d if k == 0 else -d)) % c...  23.3 us
    ppermute x7, waiting for transfers between devices, send(): lax.ppermute(x, 'wide', [(2 * i + k, 2 * ((i + (d if k == 0 else -d)) % c...  7.4 us
    all_to_all x1, starting transfers between devices, shards(): lax.all_to_all(jnp.broadcast_to(grad[None], (groups,) + grad.shape), 'nar...  7.04 us
    ppermute x2, starting transfers between devices, swap(): return lax.ppermute(x, 'wide', [(i, i ^ 1) for i in range(wide)])  3.84 us
  transfers between devices with their start and end apart: 10, of which 4 were waited for; matrix products, arithmetic and copies ran while one was open for 2% of the time, Pallas kernels for 0%

profile of v7, /device:TPU:32, one launch (start us, length us, event | category | flops | bytes accessed | tf_op | source)
XLA Modules:
  0.0 156.4 jit_solution(5808660978584157892)
XLA Ops:
  0.7 50.0 %all_gather.3.own = bf16[16,128,128]{2,1,0:T(8,128)(2,1)S(1)} all-gather(bf16[1,128,128]{2,1,0:T(8,128)(2,1)} %param.6), channel_id=1, replica_groups={{0,64,128,192,256,320,384,448,512,576,640,704,768,832,896,960},{16,80,1..., dimensions={0}, use_global_device_ids=true | all-gather | bytes 557056 | tf_op jit(solution)/shard_map/gather_far/all_gather | solution.py:102
  50.7 1.9 %collective-permute-start = (bf16[16,128,128]{2,1,0:T(8,128)(2,1)S(1)}, bf16[16,128,128]{2,1,0:T(8,128)(2,1)S(1)}, u32[]{:S(2)}, u32[]{:S(2)}) collective-permute-start(bf16[16,128,128]{2,1,0:T(8,128)(2,1)S(1)} %all_gather.3.own), channel_id=1, source_target_pairs={{0,32},{16,1008},{32,64},{48,16},{64,96},{80,48},{96,128},{112,80}... | collective-permute-start | bytes 1572872 | tf_op jit(solution)/shard_map/gather_near/ppermute | solution.py:88
  52.6 1.9 %collective-permute-start.1 = (bf16[1,128,8,128]{3,2,1,0:T(8,128)(2,1)S(1)}, bf16[1,128,8,128]{3,2,1,0:T(8,128)(2,1)S(1)}, u32[]{:S(2)}, u32[]{:S(2)}) collective-permute-start(bf16[1,128,8,128]{3,2,1,0:T(8,128)(2,1)S(1)} %copy-done.3), channel_id=1, source_target_pairs={{0,16},{16,0},{32,48},{48,32},{64,80},{80,64},{96,112},{112,96},{1... | collective-permute-start | bytes 786440 | tf_op jit(solution)/shard_map/prepare/ppermute | solution.py:94
  54.5 0.7 copy-done.4
  55.2 0.1 copy.24
  55.4 0.1 fusion.18
  55.5 0.6 gather_fusion.1
  56.0 0.6 gather_fusion
  56.8 0.2 copy.25
  57.0 0.1 copy.27.rows_mine
  57.1 0.1 add.136
  57.3 0.2 copy.26
  57.6 0.1 copy.28.rows_theirs
  57.8 4.0 %collective-permute-done.beside = bf16[16,128,128]{2,1,0:T(8,128)(2,1)S(1)} collective-permute-done((bf16[16,128,128]{2,1,0:T(8,128)(2,1)S(1)}, bf16[16,128,128]{2,1,0:T(8,128)(2,1)S(1)}, u32[]{:S(2)}, u32[]{:S(2)}) %collective-permute-start) | collective-permute-done | bytes 524320 | tf_op jit(solution)/shard_map/gather_near/ppermute | solution.py:88
  61.7 0.9 forward.1.mine
  62.6 1.9 %collective-permute-start.2 = (f32[3,128,128]{2,1,0:T(8,128)S(1)}, f32[3,128,128]{2,1,0:T(8,128)S(1)}, u32[]{:S(2)}, u32[]{:S(2)}) collective-permute-start(f32[3,128,128]{2,1,0:T(8,128)S(1)} %forward.1.mine), channel_id=1, source_target_pairs={{0,16},{16,0},{32,48},{48,32},{64,80},{80,64},{96,112},{112,96},{1... | collective-permute-start | bytes 589832 | tf_op jit(solution)/shard_map/pair/ppermute | solution.py:94
  64.6 1.4 collective-permute-done.2.theirs
  66.0 2.1 %backward.1 = (bf16[128,128]{1,0:T(8,128)(2,1)}, f32[64,128]{1,0:T(8,128)S(1)}, bf16[8,128,128]{2,1,0:T(8,128)(2,1)S(1)}, bf16[8,128,128]{2,1,0:T(8,128)(2,1)S(1...) custom-call(s32[2,8]{1,0:T(2,128)S(1)} %fusion.9.pos, f32[3,128,128]{2,1,0:T(8,128)S(1)} %forward.1.mine, ...), custom_call_target="tpu_custom_call" | custom-call | tf_op jit(solution)/shard_map/backward/pallas_call | solution.py:135
  68.1 0.8 broadcast_in_dim.13
  69.0 7.0 %all-to-all-start = ((f32[16,64,128]{2,1,0:T(8,128)}), f32[16,64,128]{2,1,0:T(8,128)S(1)}, u32[]{:S(2)}, u32[]{:S(2)}) async-start(f32[16,64,128]{2,1,0:T(8,128)} %broadcast_in_dim.13), calls=%async_computation | async-start | bytes 1048576 | tf_op jit(solution)/shard_map/weight_groups/all_to_all | solution.py:150
  76.0 1.9 %collective-permute-start.5 = (bf16[8,128,128]{2,1,0:T(8,128)(2,1)S(1)}, bf16[8,128,128]{2,1,0:T(8,128)(2,1)S(1)}, u32[]{:S(2)}, u32[]{:S(2)}) collective-permute-start(bf16[8,128,128]{2,1,0:T(8,128)(2,1)S(1)} %get-tuple-element.19), channel_id=1, source_target_pairs={{0,32},{16,1008},{32,64},{48,16},{64,96},{80,48},{96,128},{112,80}... | collective-permute-start | bytes 786440 | tf_op jit(solution)/shard_map/scatter_near/ppermute | solution.py:88
  77.9 6.8 %collective-permute-start.4 = (bf16[8,128,128]{2,1,0:T(8,128)(2,1)S(1)}, bf16[8,128,128]{2,1,0:T(8,128)(2,1)S(1)}, u32[]{:S(2)}, u32[]{:S(2)}) collective-permute-start(bf16[8,128,128]{2,1,0:T(8,128)(2,1)S(1)} %get-tuple-element.18), channel_id=1, source_target_pairs={{0,960},{16,80},{32,992},{48,112},{64,0},{80,144},{96,32},{112,176... | collective-permute-start | bytes 786440 | tf_op jit(solution)/shard_map/scatter_near/ppermute | solution.py:88
  84.8 1.9 %collective-permute-start.3 = (bf16[8,128,128]{2,1,0:T(8,128)(2,1)S(1)}, bf16[8,128,128]{2,1,0:T(8,128)(2,1)S(1)}, u32[]{:S(2)}, u32[]{:S(2)}) collective-permute-start(bf16[8,128,128]{2,1,0:T(8,128)(2,1)S(1)} %get-tuple-element.17), channel_id=1, source_target_pairs={{0,992},{16,48},{32,0},{48,80},{64,32},{80,112},{96,64},{112,144},... | collective-permute-start | bytes 786440 | tf_op jit(solution)/shard_map/scatter_near/ppermute | solution.py:88
  86.7 1.1 all-to-all-done
  87.9 2.8 %collective-permute-start.8 = (f32[8,2,128]{2,1,0:T(2,128)S(1)}, f32[8,2,128]{2,1,0:T(2,128)S(1)}, u32[]{:S(2)}, u32[]{:S(2)}) collective-permute-start(f32[8,2,128]{2,1,0:T(2,128)S(1)} %bitcast.30), channel_id=1, source_target_pairs={{0,32},{16,1008},{32,64},{48,16},{64,96},{80,48},{96,128},{112,80}... | collective-permute-start | bytes 24584 | tf_op jit(solution)/shard_map/weight_near/ppermute | solution.py:88
  90.7 6.0 %collective-permute-start.7 = (f32[8,2,128]{2,1,0:T(2,128)S(1)}, f32[8,2,128]{2,1,0:T(2,128)S(1)}, u32[]{:S(2)}, u32[]{:S(2)}) collective-permute-start(f32[8,2,128]{2,1,0:T(2,128)S(1)} %bitcast.29), channel_id=1, source_target_pairs={{0,960},{16,80},{32,992},{48,112},{64,0},{80,144},{96,32},{112,176... | collective-permute-start | bytes 24584 | tf_op jit(solution)/shard_map/weight_near/ppermute | solution.py:88
  96.7 1.9 %collective-permute-start.6 = (f32[8,2,128]{2,1,0:T(2,128)S(1)}, f32[8,2,128]{2,1,0:T(2,128)S(1)}, u32[]{:S(2)}, u32[]{:S(2)}) collective-permute-start(f32[8,2,128]{2,1,0:T(2,128)S(1)} %bitcast.28), channel_id=1, source_target_pairs={{0,992},{16,48},{32,0},{48,80},{64,32},{80,112},{96,64},{112,144},... | collective-permute-start | bytes 24584 | tf_op jit(solution)/shard_map/weight_near/ppermute | solution.py:88
  98.6 0.1 add_convert_fusion
  98.8 3.4 %collective-permute-done.6 = f32[8,2,128]{2,1,0:T(2,128)S(1)} collective-permute-done((f32[8,2,128]{2,1,0:T(2,128)S(1)}, f32[8,2,128]{2,1,0:T(2,128)S(1)}, u32[]{:S(2)}, u32[]{:S(2)}) %collective-permute-start.6) | collective-permute-done | bytes 8224 | tf_op jit(solution)/shard_map/weight_near/ppermute | solution.py:88
  102.3 52.9 %all_to_all.10 = bf16[8,132,128]{2,1,0:T(8,128)(2,1)S(1)} all-to-all(bf16[8,132,128]{2,1,0:T(8,128)(2,1)S(1)} %pad_maximum_fusion), channel_id=1, replica_groups={{0,128,256,384,512,640,768,896},{16,144,272,400,528,656,784,912},{32,16..., dimensions={0} | all-to-all | bytes 540672 | tf_op jit(solution)/shard_map/scatter_far/all_to_all | solution.py:165
  155.2 0.6 fusion
  155.9 0.6 slice_add_fusion
  (26 shorter events, 0.4 us)
Async XLA Ops:
  0.6 55.4 %copy-start = (s32[1,64]{1,0:T(1,128)S(1)}, s32[1,64]{1,0:T(1,128)}, u32[]{:S(2)}) copy-start(s32[1,64]{1,0:T(1,128)} %param.10) | copy-start | bytes 772
  0.6 51.9 %copy-start.3 = (bf16[1,128,8,128]{3,2,1,0:T(8,128)(2,1)S(1)}, bf16[1,128,8,128]{3,2,1,0:T(8,128)(2,1)}, u32[]{:S(2)}) copy-start(bf16[1,128,8,128]{3,2,1,0:T(8,128)(2,1)} %param.8) | copy-start | bytes 786436
  50.7 11.1 %collective-permute-start = (bf16[16,128,128]{2,1,0:T(8,128)(2,1)S(1)}, bf16[16,128,128]{2,1,0:T(8,128)(2,1)S(1)}, u32[]{:S(2)}, u32[]{:S(2)}) collective-permute-start(bf16[16,128,128]{2,1,0:T(8,128)(2,1)S(1)} %all_gather.3.own), channel_id=1, source_target_pairs={{0,32},{16,1008},{32,64},{48,16},{64,96},{80,48},{96,128},{112,80}... | collective-permute-start | bytes 1572872 | tf_op jit(solution)/shard_map/gather_near/ppermute | solution.py:88
  52.6 4.8 %collective-permute-start.1 = (bf16[1,128,8,128]{3,2,1,0:T(8,128)(2,1)S(1)}, bf16[1,128,8,128]{3,2,1,0:T(8,128)(2,1)S(1)}, u32[]{:S(2)}, u32[]{:S(2)}) collective-permute-start(bf16[1,128,8,128]{3,2,1,0:T(8,128)(2,1)S(1)} %copy-done.3), channel_id=1, source_target_pairs={{0,16},{16,0},{32,48},{48,32},{64,80},{80,64},{96,112},{112,96},{1... | collective-permute-start | bytes 786440 | tf_op jit(solution)/shard_map/prepare/ppermute | solution.py:94
  54.5 0.7 copy-start.4
  57.6 4.1 %copy-start.1 = (bf16[1,128,128]{2,1,0:T(8,128)(2,1)S(1)}, bf16[1,128,128]{2,1,0:T(8,128)(2,1)}, u32[]{:S(2)}) copy-start(bf16[1,128,128]{2,1,0:T(8,128)(2,1)} %param.11) | copy-start | bytes 98308
  61.7 4.3 %copy-start.2 = (bf16[128,128]{1,0:T(8,128)(2,1)S(1)}, bf16[128,128]{1,0:T(8,128)(2,1)}, u32[]{:S(2)}) copy-start(bf16[128,128]{1,0:T(8,128)(2,1)} %weight.1) | copy-start | bytes 98308
  62.6 3.3 %collective-permute-start.2 = (f32[3,128,128]{2,1,0:T(8,128)S(1)}, f32[3,128,128]{2,1,0:T(8,128)S(1)}, u32[]{:S(2)}, u32[]{:S(2)}) collective-permute-start(f32[3,128,128]{2,1,0:T(8,128)S(1)} %forward.1.mine), channel_id=1, source_target_pairs={{0,16},{16,0},{32,48},{48,32},{64,80},{80,64},{96,112},{112,96},{1... | collective-permute-start | bytes 589832 | tf_op jit(solution)/shard_map/pair/ppermute | solution.py:94
  69.0 18.9 %all-to-all-start = ((f32[16,64,128]{2,1,0:T(8,128)}), f32[16,64,128]{2,1,0:T(8,128)S(1)}, u32[]{:S(2)}, u32[]{:S(2)}) async-start(f32[16,64,128]{2,1,0:T(8,128)} %broadcast_in_dim.13), calls=%async_computation | async-start | bytes 1048576 | tf_op jit(solution)/shard_map/weight_groups/all_to_all | solution.py:150
  76.0 20.7 %collective-permute-start.5 = (bf16[8,128,128]{2,1,0:T(8,128)(2,1)S(1)}, bf16[8,128,128]{2,1,0:T(8,128)(2,1)S(1)}, u32[]{:S(2)}, u32[]{:S(2)}) collective-permute-start(bf16[8,128,128]{2,1,0:T(8,128)(2,1)S(1)} %get-tuple-element.19), channel_id=1, source_target_pairs={{0,32},{16,1008},{32,64},{48,16},{64,96},{80,48},{96,128},{112,80}... | collective-permute-start | bytes 786440 | tf_op jit(solution)/shard_map/scatter_near/ppermute | solution.py:88
  77.9 20.7 %collective-permute-start.4 = (bf16[8,128,128]{2,1,0:T(8,128)(2,1)S(1)}, bf16[8,128,128]{2,1,0:T(8,128)(2,1)S(1)}, u32[]{:S(2)}, u32[]{:S(2)}) collective-permute-start(bf16[8,128,128]{2,1,0:T(8,128)(2,1)S(1)} %get-tuple-element.18), channel_id=1, source_target_pairs={{0,960},{16,80},{32,992},{48,112},{64,0},{80,144},{96,32},{112,176... | collective-permute-start | bytes 786440 | tf_op jit(solution)/shard_map/scatter_near/ppermute | solution.py:88
  84.8 13.8 %collective-permute-start.3 = (bf16[8,128,128]{2,1,0:T(8,128)(2,1)S(1)}, bf16[8,128,128]{2,1,0:T(8,128)(2,1)S(1)}, u32[]{:S(2)}, u32[]{:S(2)}) collective-permute-start(bf16[8,128,128]{2,1,0:T(8,128)(2,1)S(1)} %get-tuple-element.17), channel_id=1, source_target_pairs={{0,992},{16,48},{32,0},{48,80},{64,32},{80,112},{96,64},{112,144},... | collective-permute-start | bytes 786440 | tf_op jit(solution)/shard_map/scatter_near/ppermute | solution.py:88
  87.9 10.9 %collective-permute-start.8 = (f32[8,2,128]{2,1,0:T(2,128)S(1)}, f32[8,2,128]{2,1,0:T(2,128)S(1)}, u32[]{:S(2)}, u32[]{:S(2)}) collective-permute-start(f32[8,2,128]{2,1,0:T(2,128)S(1)} %bitcast.30), channel_id=1, source_target_pairs={{0,32},{16,1008},{32,64},{48,16},{64,96},{80,48},{96,128},{112,80}... | collective-permute-start | bytes 24584 | tf_op jit(solution)/shard_map/weight_near/ppermute | solution.py:88
  90.7 8.1 %collective-permute-start.7 = (f32[8,2,128]{2,1,0:T(2,128)S(1)}, f32[8,2,128]{2,1,0:T(2,128)S(1)}, u32[]{:S(2)}, u32[]{:S(2)}) collective-permute-start(f32[8,2,128]{2,1,0:T(2,128)S(1)} %bitcast.29), channel_id=1, source_target_pairs={{0,960},{16,80},{32,992},{48,112},{64,0},{80,144},{96,32},{112,176... | collective-permute-start | bytes 24584 | tf_op jit(solution)/shard_map/weight_near/ppermute | solution.py:88
  96.7 5.5 %collective-permute-start.6 = (f32[8,2,128]{2,1,0:T(2,128)S(1)}, f32[8,2,128]{2,1,0:T(2,128)S(1)}, u32[]{:S(2)}, u32[]{:S(2)}) collective-permute-start(f32[8,2,128]{2,1,0:T(2,128)S(1)} %bitcast.28), channel_id=1, source_target_pairs={{0,992},{16,48},{32,0},{48,80},{64,32},{80,112},{96,64},{112,144},... | collective-permute-start | bytes 24584 | tf_op jit(solution)/shard_map/weight_near/ppermute | solution.py:88

commit v8 on v7

--- a/solution.py
+++ b/solution.py
@@ -149,19 +149,23 @@
         groups = lax.axis_size("narrow")
         grad = lax.all_to_all(jnp.broadcast_to(grad[None], (groups,) + grad.shape), "narrow", 0, 0).sum(0)
         grads = grad.reshape(CLASSES, share, row_share, tile)
+    def split(x):
+        top = x.astype(BF16)
+        return [top, (x - top.astype(F32)).astype(BF16)]
+
+    def joined(x):
+        return x[:, :tile], x[:, tile : tile + row_share] + x[:, tile + row_share :]
+
     with jax.named_scope("scatter_near"):
-        whole = parts[0].astype(F32)
-        for part, d in zip(parts[1:], NEAR[1:]):
-            whole += send(part, -d).astype(F32)
-        main = whole.astype(BF16)
-    with jax.named_scope("weight_near"):
-        grad = grads[0]
-        for a, d in list(enumerate(NEAR))[1:]:
-            grad += send(grads[a], -d)
+        both = send(jnp.concatenate([parts[1], *split(grads[1])], 1), -NEAR[1])
+        near_main, near_grad = joined(both.astype(F32))
+        whole = parts[0].astype(F32) + near_main
+        grad = grads[0] + near_grad
+        for a in (2, 3):
+            whole += send(parts[a], -NEAR[a]).astype(F32)
+            grad += send(grads[a], -NEAR[a])
     with jax.named_scope("scatter_far"):
-        top = grad.astype(BF16)
-        rest = (grad - top.astype(F32)).astype(BF16)
-        message = jnp.concatenate([main, top, rest], 1)
+        message = jnp.concatenate([whole.astype(BF16), *split(grad)], 1)
         got = lax.all_to_all(message, "wide", 0, 0, axis_index_groups=every(CLASSES))
         whole = got.astype(F32).sum(0)
         feature_grad = whole[:tile].astype(BF16)

time: 157 us -> 164 us (1.045)
  blocking collectives: 103 us -> 124 us
  starting transfers between devices: 34.2 us -> 22.6 us
  waiting for transfers between devices: 9.92 us -> 8.26 us
    all_to_all x0 -> x1, blocking collectives: none -> 18.7 us  [shards(): lax.all_to_all(jnp.broadcast_to(grad[None], (groups,) + grad.shape), 'nar...]
    all_to_all x1 -> x0, starting transfers between devices: 7.04 us -> none  [shards(): lax.all_to_all(jnp.broadcast_to(grad[None], (groups,) + grad.shape), 'nar...]
    ppermute x7 -> x6, starting transfers between devices: 23.3 us -> 18.8 us  [send(): lax.ppermute(x, 'wide', [(2 * i + k, 2 * ((i + (d if k == 0 else -d)) % c...]
    all_to_all x1, blocking collectives: 52.9 us -> 55.5 us  [shards(): lax.all_to_all(message, 'wide', 0, 0, axis_index_groups=every(CLASSES))]
    ppermute x7 -> x6, waiting for transfers between devices: 7.4 us -> 6.87 us  [send(): lax.ppermute(x, 'wide', [(2 * i + k, 2 * ((i + (d if k == 0 else -d)) % c...]
  transfers between devices with their start and end apart: 10 -> 8, of which waited for: 4 -> 3; matrix products, arithmetic and copies ran while one was open for 2% -> 2% of each run, Pallas kernels for 0% -> 0%
where the time goes in v8:
time: 164 us
  blocking collectives  124 us (76%)
  starting transfers between devices  22.6 us (14%)
  waiting for transfers between devices  8.26 us (5%)
  local copies, waits for them, and re-layouts  3.52 us (2%)
  Pallas kernels  3.04 us (2%)
    all_to_all x1, blocking collectives, shards(): lax.all_to_all(message, 'wide', 0, 0, axis_index_groups=every(CLASSES))  55.5 us
    all_gather x1, blocking collectives, shards(): held = lax.all_gather(feat, 'wide', axis_index_groups=every(2))  50 us
    ppermute x6, starting transfers between devices, send(): lax.ppermute(x, 'wide', [(2 * i + k, 2 * ((i + (d if k == 0 else -d)) % c...  18.8 us
    all_to_all x1, blocking collectives, shards(): lax.all_to_all(jnp.broadcast_to(grad[None], (groups,) + grad.shape), 'nar...  18.7 us
    ppermute x6, waiting for transfers between devices, send(): lax.ppermute(x, 'wide', [(2 * i + k, 2 * ((i + (d if k == 0 else -d)) % c...  6.87 us
    ppermute x2, starting transfers between devices, swap(): return lax.ppermute(x, 'wide', [(i, i ^ 1) for i in range(wide)])  3.84 us
  transfers between devices with their start and end apart: 8, of which 3 were waited for; matrix products, arithmetic and copies ran while one was open for 2% of the time, Pallas kernels for 0%

profile of v8, /device:TPU:32, one launch (start us, length us, event | category | flops | bytes accessed | tf_op | source)
XLA Modules:
  0.0 163.8 jit_solution(14503883965074103135)
XLA Ops:
  0.7 50.0 %all_gather.3.own = bf16[16,128,128]{2,1,0:T(8,128)(2,1)S(1)} all-gather(bf16[1,128,128]{2,1,0:T(8,128)(2,1)} %param.6), channel_id=1, replica_groups={{0,64,128,192,256,320,384,448,512,576,640,704,768,832,896,960},{16,80,1..., dimensions={0}, use_global_device_ids=true | all-gather | bytes 557056 | tf_op jit(solution)/shard_map/gather_far/all_gather | solution.py:102
  50.7 1.9 %collective-permute-start = (bf16[16,128,128]{2,1,0:T(8,128)(2,1)S(1)}, bf16[16,128,128]{2,1,0:T(8,128)(2,1)S(1)}, u32[]{:S(2)}, u32[]{:S(2)}) collective-permute-start(bf16[16,128,128]{2,1,0:T(8,128)(2,1)S(1)} %all_gather.3.own), channel_id=1, source_target_pairs={{0,32},{16,1008},{32,64},{48,16},{64,96},{80,48},{96,128},{112,80}... | collective-permute-start | bytes 1572872 | tf_op jit(solution)/shard_map/gather_near/ppermute | solution.py:88
  52.6 1.9 %collective-permute-start.1 = (bf16[1,128,8,128]{3,2,1,0:T(8,128)(2,1)S(1)}, bf16[1,128,8,128]{3,2,1,0:T(8,128)(2,1)S(1)}, u32[]{:S(2)}, u32[]{:S(2)}) collective-permute-start(bf16[1,128,8,128]{3,2,1,0:T(8,128)(2,1)S(1)} %copy-done.3), channel_id=1, source_target_pairs={{0,16},{16,0},{32,48},{48,32},{64,80},{80,64},{96,112},{112,96},{1... | collective-permute-start | bytes 786440 | tf_op jit(solution)/shard_map/prepare/ppermute | solution.py:94
  54.5 0.7 copy-done.4
  55.2 0.1 copy.24
  55.3 0.1 iota_add_fusion
  55.4 0.1 fusion.24
  55.5 0.6 gather_fusion.1
  56.0 0.6 gather_fusion
  56.7 0.1 fusion.14
  56.8 0.2 copy.25
  57.0 0.1 copy.27.rows_mine
  57.1 0.1 add.139
  57.3 0.1 fusion.4.perm
  57.3 0.2 copy.26
  57.6 0.1 copy.28.rows_theirs
  57.8 4.0 %collective-permute-done.beside = bf16[16,128,128]{2,1,0:T(8,128)(2,1)S(1)} collective-permute-done((bf16[16,128,128]{2,1,0:T(8,128)(2,1)S(1)}, bf16[16,128,128]{2,1,0:T(8,128)(2,1)S(1)}, u32[]{:S(2)}, u32[]{:S(2)}) %collective-permute-start) | collective-permute-done | bytes 524320 | tf_op jit(solution)/shard_map/gather_near/ppermute | solution.py:88
  61.7 0.9 forward.1.mine
  62.6 1.9 %collective-permute-start.2 = (f32[3,128,128]{2,1,0:T(8,128)S(1)}, f32[3,128,128]{2,1,0:T(8,128)S(1)}, u32[]{:S(2)}, u32[]{:S(2)}) collective-permute-start(f32[3,128,128]{2,1,0:T(8,128)S(1)} %forward.1.mine), channel_id=1, source_target_pairs={{0,16},{16,0},{32,48},{48,32},{64,80},{80,64},{96,112},{112,96},{1... | collective-permute-start | bytes 589832 | tf_op jit(solution)/shard_map/pair/ppermute | solution.py:94
  64.6 1.4 collective-permute-done.2.theirs
  66.0 2.1 %backward.1 = (bf16[128,128]{1,0:T(8,128)(2,1)}, f32[64,128]{1,0:T(8,128)S(1)}, bf16[8,128,128]{2,1,0:T(8,128)(2,1)S(1)}, bf16[8,128,128]{2,1,0:T(8,128)(2,1)S(1...) custom-call(s32[2,8]{1,0:T(2,128)S(1)} %fusion.15.pos, f32[3,128,128]{2,1,0:T(8,128)S(1)} %forward.1.mine, ...), custom_call_target="tpu_custom_call" | custom-call | tf_op jit(solution)/shard_map/backward/pallas_call | solution.py:135
  68.2 18.7 %all_to_all.10 = f32[16,64,128]{2,1,0:T(8,128)S(1)} all-to-all(f32[16,64,128]{2,1,0:T(8,128)S(1)} %broadcast_in_dim.13), channel_id=1, replica_groups=mesh['wide'=64,'narrow'=16] {'narrow'}, dimensions={0} | all-to-all | bytes 1048576 | tf_op jit(solution)/shard_map/weight_groups/all_to_all | solution.py:150
  86.9 4.2 %collective-permute-start.3 = (bf16[8,132,128]{2,1,0:T(8,128)(2,1)S(1)}, bf16[8,132,128]{2,1,0:T(8,128)(2,1)S(1)}, u32[]{:S(2)}, u32[]{:S(2)}) collective-permute-start(bf16[8,132,128]{2,1,0:T(8,128)(2,1)S(1)} %pad_maximum_fusion), channel_id=1, source_target_pairs={{0,992},{16,48},{32,0},{48,80},{64,32},{80,112},{96,64},{112,144},... | collective-permute-start | bytes 811016 | tf_op jit(solution)/shard_map/scatter_near/ppermute | solution.py:88
  91.1 1.9 %collective-permute-start.5 = (bf16[8,128,128]{2,1,0:T(8,128)(2,1)S(1)}, bf16[8,128,128]{2,1,0:T(8,128)(2,1)S(1)}, u32[]{:S(2)}, u32[]{:S(2)}) collective-permute-start(bf16[8,128,128]{2,1,0:T(8,128)(2,1)S(1)} %get-tuple-element.20), channel_id=1, source_target_pairs={{0,32},{16,1008},{32,64},{48,16},{64,96},{80,48},{96,128},{112,80}... | collective-permute-start | bytes 786440 | tf_op jit(solution)/shard_map/scatter_near/ppermute | solution.py:88
  93.1 5.0 %collective-permute-start.4 = (bf16[8,128,128]{2,1,0:T(8,128)(2,1)S(1)}, bf16[8,128,128]{2,1,0:T(8,128)(2,1)S(1)}, u32[]{:S(2)}, u32[]{:S(2)}) collective-permute-start(bf16[8,128,128]{2,1,0:T(8,128)(2,1)S(1)} %get-tuple-element.19), channel_id=1, source_target_pairs={{0,960},{16,80},{32,992},{48,112},{64,0},{80,144},{96,32},{112,176... | collective-permute-start | bytes 786440 | tf_op jit(solution)/shard_map/scatter_near/ppermute | solution.py:88
  98.1 2.3 %collective-permute-start.7 = (f32[8,2,128]{2,1,0:T(2,128)S(1)}, f32[8,2,128]{2,1,0:T(2,128)S(1)}, u32[]{:S(2)}, u32[]{:S(2)}) collective-permute-start(f32[8,2,128]{2,1,0:T(2,128)S(1)} %bitcast.30), channel_id=1, source_target_pairs={{0,32},{16,1008},{32,64},{48,16},{64,96},{80,48},{96,128},{112,80}... | collective-permute-start | bytes 24584 | tf_op jit(solution)/shard_map/scatter_near/ppermute | solution.py:88
  100.4 3.5 %collective-permute-start.6 = (f32[8,2,128]{2,1,0:T(2,128)S(1)}, f32[8,2,128]{2,1,0:T(2,128)S(1)}, u32[]{:S(2)}, u32[]{:S(2)}) collective-permute-start(f32[8,2,128]{2,1,0:T(2,128)S(1)} %bitcast.29), channel_id=1, source_target_pairs={{0,960},{16,80},{32,992},{48,112},{64,0},{80,144},{96,32},{112,176... | collective-permute-start | bytes 24584 | tf_op jit(solution)/shard_map/scatter_near/ppermute | solution.py:88
  103.9 2.9 %collective-permute-done.6 = f32[8,2,128]{2,1,0:T(2,128)S(1)} collective-permute-done((f32[8,2,128]{2,1,0:T(2,128)S(1)}, f32[8,2,128]{2,1,0:T(2,128)S(1)}, u32[]{:S(2)}, u32[]{:S(2)}) %collective-permute-start.6) | collective-permute-done | bytes 8224 | tf_op jit(solution)/shard_map/scatter_near/ppermute | solution.py:88
  106.9 0.1 fusion.2
  107.0 55.5 %all_to_all.11 = bf16[8,132,128]{2,1,0:T(8,128)(2,1)S(1)} all-to-all(bf16[8,132,128]{2,1,0:T(8,128)(2,1)S(1)} %pad_maximum_fusion.1), channel_id=1, replica_groups={{0,128,256,384,512,640,768,896},{16,144,272,400,528,656,784,912},{32,16..., dimensions={0} | all-to-all | bytes 540672 | tf_op jit(solution)/shard_map/scatter_far/all_to_all | solution.py:169
  162.6 0.6 fusion.3
  163.2 0.6 slice_add_fusion.2
  (26 shorter events, 0.3 us)
Async XLA Ops:
  0.6 55.4 %copy-start = (s32[1,64]{1,0:T(1,128)S(1)}, s32[1,64]{1,0:T(1,128)}, u32[]{:S(2)}) copy-start(s32[1,64]{1,0:T(1,128)} %param.10) | copy-start | bytes 772
  0.6 51.9 %copy-start.3 = (bf16[1,128,8,128]{3,2,1,0:T(8,128)(2,1)S(1)}, bf16[1,128,8,128]{3,2,1,0:T(8,128)(2,1)}, u32[]{:S(2)}) copy-start(bf16[1,128,8,128]{3,2,1,0:T(8,128)(2,1)} %param.8) | copy-start | bytes 786436
  50.7 11.1 %collective-permute-start = (bf16[16,128,128]{2,1,0:T(8,128)(2,1)S(1)}, bf16[16,128,128]{2,1,0:T(8,128)(2,1)S(1)}, u32[]{:S(2)}, u32[]{:S(2)}) collective-permute-start(bf16[16,128,128]{2,1,0:T(8,128)(2,1)S(1)} %all_gather.3.own), channel_id=1, source_target_pairs={{0,32},{16,1008},{32,64},{48,16},{64,96},{80,48},{96,128},{112,80}... | collective-permute-start | bytes 1572872 | tf_op jit(solution)/shard_map/gather_near/ppermute | solution.py:88
  52.6 4.8 %collective-permute-start.1 = (bf16[1,128,8,128]{3,2,1,0:T(8,128)(2,1)S(1)}, bf16[1,128,8,128]{3,2,1,0:T(8,128)(2,1)S(1)}, u32[]{:S(2)}, u32[]{:S(2)}) collective-permute-start(bf16[1,128,8,128]{3,2,1,0:T(8,128)(2,1)S(1)} %copy-done.3), channel_id=1, source_target_pairs={{0,16},{16,0},{32,48},{48,32},{64,80},{80,64},{96,112},{112,96},{1... | collective-permute-start | bytes 786440 | tf_op jit(solution)/shard_map/prepare/ppermute | solution.py:94
  54.5 0.7 copy-start.4
  57.6 4.1 %copy-start.1 = (bf16[1,128,128]{2,1,0:T(8,128)(2,1)S(1)}, bf16[1,128,128]{2,1,0:T(8,128)(2,1)}, u32[]{:S(2)}) copy-start(bf16[1,128,128]{2,1,0:T(8,128)(2,1)} %param.11) | copy-start | bytes 98308
  61.7 4.3 %copy-start.2 = (bf16[128,128]{1,0:T(8,128)(2,1)S(1)}, bf16[128,128]{1,0:T(8,128)(2,1)}, u32[]{:S(2)}) copy-start(bf16[128,128]{1,0:T(8,128)(2,1)} %weight.1) | copy-start | bytes 98308
  62.6 3.3 %collective-permute-start.2 = (f32[3,128,128]{2,1,0:T(8,128)S(1)}, f32[3,128,128]{2,1,0:T(8,128)S(1)}, u32[]{:S(2)}, u32[]{:S(2)}) collective-permute-start(f32[3,128,128]{2,1,0:T(8,128)S(1)} %forward.1.mine), channel_id=1, source_target_pairs={{0,16},{16,0},{32,48},{48,32},{64,80},{80,64},{96,112},{112,96},{1... | collective-permute-start | bytes 589832 | tf_op jit(solution)/shard_map/pair/ppermute | solution.py:94
  86.9 16.9 %collective-permute-start.3 = (bf16[8,132,128]{2,1,0:T(8,128)(2,1)S(1)}, bf16[8,132,128]{2,1,0:T(8,128)(2,1)S(1)}, u32[]{:S(2)}, u32[]{:S(2)}) collective-permute-start(bf16[8,132,128]{2,1,0:T(8,128)(2,1)S(1)} %pad_maximum_fusion), channel_id=1, source_target_pairs={{0,992},{16,48},{32,0},{48,80},{64,32},{80,112},{96,64},{112,144},... | collective-permute-start | bytes 811016 | tf_op jit(solution)/shard_map/scatter_near/ppermute | solution.py:88
  91.1 15.7 %collective-permute-start.5 = (bf16[8,128,128]{2,1,0:T(8,128)(2,1)S(1)}, bf16[8,128,128]{2,1,0:T(8,128)(2,1)S(1)}, u32[]{:S(2)}, u32[]{:S(2)}) collective-permute-start(bf16[8,128,128]{2,1,0:T(8,128)(2,1)S(1)} %get-tuple-element.20), channel_id=1, source_target_pairs={{0,32},{16,1008},{32,64},{48,16},{64,96},{80,48},{96,128},{112,80}... | collective-permute-start | bytes 786440 | tf_op jit(solution)/shard_map/scatter_near/ppermute | solution.py:88
  93.1 13.8 %collective-permute-start.4 = (bf16[8,128,128]{2,1,0:T(8,128)(2,1)S(1)}, bf16[8,128,128]{2,1,0:T(8,128)(2,1)S(1)}, u32[]{:S(2)}, u32[]{:S(2)}) collective-permute-start(bf16[8,128,128]{2,1,0:T(8,128)(2,1)S(1)} %get-tuple-element.19), channel_id=1, source_target_pairs={{0,960},{16,80},{32,992},{48,112},{64,0},{80,144},{96,32},{112,176... | collective-permute-start | bytes 786440 | tf_op jit(solution)/shard_map/scatter_near/ppermute | solution.py:88
  98.1 5.8 %collective-permute-start.7 = (f32[8,2,128]{2,1,0:T(2,128)S(1)}, f32[8,2,128]{2,1,0:T(2,128)S(1)}, u32[]{:S(2)}, u32[]{:S(2)}) collective-permute-start(f32[8,2,128]{2,1,0:T(2,128)S(1)} %bitcast.30), channel_id=1, source_target_pairs={{0,32},{16,1008},{32,64},{48,16},{64,96},{80,48},{96,128},{112,80}... | collective-permute-start | bytes 24584 | tf_op jit(solution)/shard_map/scatter_near/ppermute | solution.py:88
  100.4 6.4 %collective-permute-start.6 = (f32[8,2,128]{2,1,0:T(2,128)S(1)}, f32[8,2,128]{2,1,0:T(2,128)S(1)}, u32[]{:S(2)}, u32[]{:S(2)}) collective-permute-start(f32[8,2,128]{2,1,0:T(2,128)S(1)} %bitcast.29), channel_id=1, source_target_pairs={{0,960},{16,80},{32,992},{48,112},{64,0},{80,144},{96,32},{112,176... | collective-permute-start | bytes 24584 | tf_op jit(solution)/shard_map/scatter_near/ppermute | solution.py:88

commit v9 on v7

--- a/solution.py
+++ b/solution.py
@@ -30,16 +30,10 @@
     out[2] = cot[...].astype(F32)
 
 
-def backward(
-    pos, mine, theirs, cols_mine, cols_theirs, weight, perm,
-    activated, ordered, out0, out1, out2, out3, total,
-):
-    slots = pos.shape[1]
+def gradients(mine, theirs, weight, perm, activated, ordered, moved):
     tile = weight.shape[0]
-    blocks = total.shape[0] - 1
-    total[...] = jnp.zeros_like(total)
     grad = jnp.zeros((tile, tile), F32)
-    for r, (cols, cot) in enumerate(((cols_mine, mine), (cols_theirs, theirs))):
+    for r, cot in enumerate((mine, theirs)):
         mixed = mine[r] + theirs[1 - r]
         high = mixed.astype(BF16)
         low = (mixed - high.astype(F32)).astype(BF16)
@@ -50,23 +44,30 @@
         if r == 0:
             activated[...] = (pre * sig).astype(BF16)
         act_grad = (cot[2] * sig * (1.0 + pre * (1.0 - sig))).astype(BF16)
-        moved = lax.dot_general(
+        moved[r] = lax.dot_general(
             act_grad, weight[...], (((1,), (1,)), ((), ())), preferred_element_type=F32
         ).astype(BF16)
         for part in (high, low):
             grad += lax.dot_general(
                 part, act_grad, (((0,), (0,)), ((), ())), preferred_element_type=F32
             )
-        for s in range(slots):
-            term = jnp.dot(
-                cols[pl.ds(s * tile, tile), :], moved, preferred_element_type=F32
-            )
-            total[pos[r, s]] += term
     top = grad.astype(BF16)
     rest = (grad - top.astype(F32)).astype(BF16)
     ordered[...] = jnp.dot(perm[...], top, preferred_element_type=F32) + jnp.dot(
         perm[...], rest, preferred_element_type=F32
     )
+
+
+def backward(pos, moved, cols_mine, cols_theirs, out0, out1, out2, out3, total):
+    slots = pos.shape[1]
+    tile = moved.shape[1]
+    blocks = total.shape[0] - 1
+    total[...] = jnp.zeros_like(total)
+    for r, cols in enumerate((cols_mine, cols_theirs)):
+        for s in range(slots):
+            total[pos[r, s]] += jnp.dot(
+                cols[pl.ds(s * tile, tile), :], moved[r], preferred_element_type=F32
+            )
     share = blocks // CLASSES
     for a, out in enumerate((out0, out1, out2, out3)):
         for k in range(share):
@@ -132,19 +133,27 @@
     )(source, held, beside, *rows, cotangent[0])
     with jax.named_scope("pair"):
         theirs = swap(mixed)
-    activated, grad, *parts = pl.pallas_call(
-        backward,
+    activated, grad, moved = pl.pallas_call(
+        gradients,
         out_shape=[
             jax.ShapeDtypeStruct((tile, tile), BF16),
             jax.ShapeDtypeStruct((tile // 2, tile), F32),
-        ]
-        + [jax.ShapeDtypeStruct((share, tile, tile), BF16)] * CLASSES,
-        in_specs=[SMEM] + [VMEM] * 6,
-        out_specs=[VMEM] * (2 + CLASSES),
+            jax.ShapeDtypeStruct((2, tile, tile), BF16),
+        ],
+        in_specs=[VMEM] * 4,
+        out_specs=[VMEM] * 3,
+        compiler_params=PARAMS,
+        name="gradients",
+    )(mixed, theirs, weight, perm)
+    parts = pl.pallas_call(
+        backward,
+        out_shape=[jax.ShapeDtypeStruct((share, tile, tile), BF16)] * CLASSES,
+        in_specs=[SMEM] + [VMEM] * 3,
+        out_specs=[VMEM] * CLASSES,
         scratch_shapes=[pltpu.VMEM((chips + 1, tile, tile), F32)],
         compiler_params=PARAMS,
         name="backward",
-    )(place, mixed, theirs, *flipped, weight, perm)
+    )(place, moved, *flipped)
     with jax.named_scope("weight_groups"):
         groups = lax.axis_size("narrow")
         grad = lax.all_to_all(jnp.broadcast_to(grad[None], (groups,) + grad.shape), "narrow", 0, 0).sum(0)

time: 157 us -> 158 us (level)
  the two profiles are of different devices: /device:TPU:32 before, /device:TPU:2 now
where the time goes in v9:
time: 158 us; the launch traced here: 157 us
  blocking collectives  104 us (66%)
  starting transfers between devices  31.1 us (20%)
  waiting for transfers between devices  12.4 us (8%)
  local copies, waits for them, and re-layouts  4.54 us (3%)
  Pallas kernels  3 us (2%)
    all_gather x1, blocking collectives, shards(): held = lax.all_gather(feat, 'wide', axis_index_groups=every(2))  52.3 us
    all_to_all x1, blocking collectives, shards(): lax.all_to_all(message, 'wide', 0, 0, axis_index_groups=every(CLASSES))  52 us
    ppermute x7, starting transfers between devices, send(): lax.ppermute(x, 'wide', [(2 * i + k, 2 * ((i + (d if k == 0 else -d)) % c...  19.8 us
    ppermute x7, waiting for transfers between devices, send(): lax.ppermute(x, 'wide', [(2 * i + k, 2 * ((i + (d if k == 0 else -d)) % c...  9.36 us
    all_to_all x1, starting transfers between devices, shards(): lax.all_to_all(jnp.broadcast_to(grad[None], (groups,) + grad.shape), 'nar...  7.48 us
    ppermute x2, starting transfers between devices, swap(): return lax.ppermute(x, 'wide', [(i, i ^ 1) for i in range(wide)])  3.84 us
  transfers between devices with their start and end apart: 10, of which 4 were waited for; matrix products, arithmetic and copies ran while one was open for 2% of the time, Pallas kernels for 1%

profile of v9, /device:TPU:2, one launch (start us, length us, event | category | flops | bytes accessed | tf_op | source)
XLA Modules:
  0.0 157.4 jit_solution(1858309435417548151)
XLA Ops:
  0.6 1.9 %collective-permute-start.1 = (bf16[1,128,8,128]{3,2,1,0:T(8,128)(2,1)}, bf16[1,128,8,128]{3,2,1,0:T(8,128)(2,1)S(1)}, u32[]{:S(2)}, u32[]{:S(2)}) collective-permute-start(bf16[1,128,8,128]{3,2,1,0:T(8,128)(2,1)} %param.8), channel_id=1, source_target_pairs={{0,16},{16,0},{32,48},{48,32},{64,80},{80,64},{96,112},{112,96},{1... | collective-permute-start | bytes 786440 | tf_op jit(solution)/shard_map/prepare/ppermute | solution.py:95
  2.6 52.3 %all_gather.3.own = bf16[16,128,128]{2,1,0:T(8,128)(2,1)S(1)} all-gather(bf16[1,128,128]{2,1,0:T(8,128)(2,1)} %param.6), channel_id=1, replica_groups={{0,64,128,192,256,320,384,448,512,576,640,704,768,832,896,960},{16,80,1..., dimensions={0}, use_global_device_ids=true | all-gather | bytes 557056 | tf_op jit(solution)/shard_map/gather_far/all_gather | solution.py:103
  54.9 2.1 %collective-permute-start = (bf16[16,128,128]{2,1,0:T(8,128)(2,1)S(1)}, bf16[16,128,128]{2,1,0:T(8,128)(2,1)S(1)}, u32[]{:S(2)}, u32[]{:S(2)}) collective-permute-start(bf16[16,128,128]{2,1,0:T(8,128)(2,1)S(1)} %all_gather.3.own), channel_id=1, source_target_pairs={{0,32},{16,1008},{32,64},{48,16},{64,96},{80,48},{96,128},{112,80}... | collective-permute-start | bytes 1572872 | tf_op jit(solution)/shard_map/gather_near/ppermute | solution.py:89
  57.1 0.7 copy-done.4
  58.0 0.6 gather_fusion.1
  58.6 0.6 gather_fusion
  59.3 0.2 copy-done.3
  59.5 0.2 copy.25
  59.8 0.1 copy.27.rows_mine
  59.9 0.1 add.134
  60.1 0.2 copy.26
  60.3 0.1 copy.28.rows_theirs
  60.5 6.7 %collective-permute-done.beside = bf16[16,128,128]{2,1,0:T(8,128)(2,1)S(1)} collective-permute-done((bf16[16,128,128]{2,1,0:T(8,128)(2,1)S(1)}, bf16[16,128,128]{2,1,0:T(8,128)(2,1)S(1)}, u32[]{:S(2)}, u32[]{:S(2)}) %collective-permute-start) | collective-permute-done | bytes 524320 | tf_op jit(solution)/shard_map/gather_near/ppermute | solution.py:89
  67.2 0.9 forward.1.mine
  68.1 1.9 %collective-permute-start.2 = (f32[3,128,128]{2,1,0:T(8,128)S(1)}, f32[3,128,128]{2,1,0:T(8,128)S(1)}, u32[]{:S(2)}, u32[]{:S(2)}) collective-permute-start(f32[3,128,128]{2,1,0:T(8,128)S(1)} %forward.1.mine), channel_id=1, source_target_pairs={{0,16},{16,0},{32,48},{48,32},{64,80},{80,64},{96,112},{112,96},{1... | collective-permute-start | bytes 589832 | tf_op jit(solution)/shard_map/pair/ppermute | solution.py:95
  70.1 1.3 collective-permute-done.2.theirs
  71.4 1.1 gradients.1
  72.5 0.8 broadcast_in_dim.13
  73.4 7.5 %all-to-all-start = ((f32[16,64,128]{2,1,0:T(8,128)}), f32[16,64,128]{2,1,0:T(8,128)S(1)}, u32[]{:S(2)}, u32[]{:S(2)}) async-start(f32[16,64,128]{2,1,0:T(8,128)} %broadcast_in_dim.13), calls=%async_computation | async-start | bytes 1048576 | tf_op jit(solution)/shard_map/weight_groups/all_to_all | solution.py:159
  80.9 1.0 backward.1
  81.9 1.9 %collective-permute-start.3 = (bf16[8,128,128]{2,1,0:T(8,128)(2,1)S(1)}, bf16[8,128,128]{2,1,0:T(8,128)(2,1)S(1)}, u32[]{:S(2)}, u32[]{:S(2)}) collective-permute-start(bf16[8,128,128]{2,1,0:T(8,128)(2,1)S(1)} %get-tuple-element.19), channel_id=1, source_target_pairs={{0,992},{16,48},{32,0},{48,80},{64,32},{80,112},{96,64},{112,144},... | collective-permute-start | bytes 786440 | tf_op jit(solution)/shard_map/scatter_near/ppermute | solution.py:89
  83.8 3.3 %collective-permute-start.4 = (bf16[8,128,128]{2,1,0:T(8,128)(2,1)S(1)}, bf16[8,128,128]{2,1,0:T(8,128)(2,1)S(1)}, u32[]{:S(2)}, u32[]{:S(2)}) collective-permute-start(bf16[8,128,128]{2,1,0:T(8,128)(2,1)S(1)} %get-tuple-element.20), channel_id=1, source_target_pairs={{0,960},{16,80},{32,992},{48,112},{64,0},{80,144},{96,32},{112,176... | collective-permute-start | bytes 786440 | tf_op jit(solution)/shard_map/scatter_near/ppermute | solution.py:89
  87.0 2.6 %collective-permute-start.5 = (bf16[8,128,128]{2,1,0:T(8,128)(2,1)S(1)}, bf16[8,128,128]{2,1,0:T(8,128)(2,1)S(1)}, u32[]{:S(2)}, u32[]{:S(2)}) collective-permute-start(bf16[8,128,128]{2,1,0:T(8,128)(2,1)S(1)} %get-tuple-element.21), channel_id=1, source_target_pairs={{0,32},{16,1008},{32,64},{48,16},{64,96},{80,48},{96,128},{112,80}... | collective-permute-start | bytes 786440 | tf_op jit(solution)/shard_map/scatter_near/ppermute | solution.py:89
  89.6 1.7 %all-to-all-done = f32[16,64,128]{2,1,0:T(8,128)S(1)} async-done(((f32[16,64,128]{2,1,0:T(8,128)}), f32[16,64,128]{2,1,0:T(8,128)S(1)}, u32[]{:S(2)}, u32[]{:S(2)}) %all-to-all-start) | async-done | bytes 524320 | tf_op jit(solution)/shard_map/weight_groups/all_to_all | solution.py:159
  91.4 2.8 %collective-permute-start.6 = (f32[8,2,128]{2,1,0:T(2,128)S(1)}, f32[8,2,128]{2,1,0:T(2,128)S(1)}, u32[]{:S(2)}, u32[]{:S(2)}) collective-permute-start(f32[8,2,128]{2,1,0:T(2,128)S(1)} %bitcast.30), channel_id=1, source_target_pairs={{0,992},{16,48},{32,0},{48,80},{64,32},{80,112},{96,64},{112,144},... | collective-permute-start | bytes 24584 | tf_op jit(solution)/shard_map/weight_near/ppermute | solution.py:89
  94.2 3.2 %collective-permute-start.7 = (f32[8,2,128]{2,1,0:T(2,128)S(1)}, f32[8,2,128]{2,1,0:T(2,128)S(1)}, u32[]{:S(2)}, u32[]{:S(2)}) collective-permute-start(f32[8,2,128]{2,1,0:T(2,128)S(1)} %bitcast.29), channel_id=1, source_target_pairs={{0,960},{16,80},{32,992},{48,112},{64,0},{80,144},{96,32},{112,176... | collective-permute-start | bytes 24584 | tf_op jit(solution)/shard_map/weight_near/ppermute | solution.py:89
  97.4 3.9 %collective-permute-start.8 = (f32[8,2,128]{2,1,0:T(2,128)S(1)}, f32[8,2,128]{2,1,0:T(2,128)S(1)}, u32[]{:S(2)}, u32[]{:S(2)}) collective-permute-start(f32[8,2,128]{2,1,0:T(2,128)S(1)} %bitcast.28), channel_id=1, source_target_pairs={{0,32},{16,1008},{32,64},{48,16},{64,96},{80,48},{96,128},{112,80}... | collective-permute-start | bytes 24584 | tf_op jit(solution)/shard_map/weight_near/ppermute | solution.py:89
  101.3 0.1 add_convert_fusion
  101.5 2.6 %collective-permute-done.8 = f32[8,2,128]{2,1,0:T(2,128)S(1)} collective-permute-done((f32[8,2,128]{2,1,0:T(2,128)S(1)}, f32[8,2,128]{2,1,0:T(2,128)S(1)}, u32[]{:S(2)}, u32[]{:S(2)}) %collective-permute-start.8) | collective-permute-done | bytes 8224 | tf_op jit(solution)/shard_map/weight_near/ppermute | solution.py:89
  104.2 52.0 %all_to_all.10 = bf16[8,132,128]{2,1,0:T(8,128)(2,1)S(1)} all-to-all(bf16[8,132,128]{2,1,0:T(8,128)(2,1)S(1)} %pad_maximum_fusion), channel_id=1, replica_groups={{0,128,256,384,512,640,768,896},{16,144,272,400,528,656,784,912},{32,16..., dimensions={0} | all-to-all | bytes 540672 | tf_op jit(solution)/shard_map/scatter_far/all_to_all | solution.py:174
  156.2 0.6 fusion
  156.8 0.6 slice_add_fusion
  (27 shorter events, 0.6 us)
Async XLA Ops:
  0.6 57.9 %copy-start = (s32[1,64]{1,0:T(1,128)S(1)}, s32[1,64]{1,0:T(1,128)}, u32[]{:S(2)}) copy-start(s32[1,64]{1,0:T(1,128)} %param.10) | copy-start | bytes 772
  0.6 59.4 %collective-permute-start.1 = (bf16[1,128,8,128]{3,2,1,0:T(8,128)(2,1)}, bf16[1,128,8,128]{3,2,1,0:T(8,128)(2,1)S(1)}, u32[]{:S(2)}, u32[]{:S(2)}) collective-permute-start(bf16[1,128,8,128]{3,2,1,0:T(8,128)(2,1)} %param.8), channel_id=1, source_target_pairs={{0,16},{16,0},{32,48},{48,32},{64,80},{80,64},{96,112},{112,96},{1... | collective-permute-start | bytes 786440 | tf_op jit(solution)/shard_map/prepare/ppermute | solution.py:95
  54.9 12.3 %collective-permute-start = (bf16[16,128,128]{2,1,0:T(8,128)(2,1)S(1)}, bf16[16,128,128]{2,1,0:T(8,128)(2,1)S(1)}, u32[]{:S(2)}, u32[]{:S(2)}) collective-permute-start(bf16[16,128,128]{2,1,0:T(8,128)(2,1)S(1)} %all_gather.3.own), channel_id=1, source_target_pairs={{0,32},{16,1008},{32,64},{48,16},{64,96},{80,48},{96,128},{112,80}... | collective-permute-start | bytes 1572872 | tf_op jit(solution)/shard_map/gather_near/ppermute | solution.py:89
  57.1 0.7 copy-start.4
  58.6 1.0 copy-start.3
  60.3 6.9 %copy-start.1 = (bf16[1,128,128]{2,1,0:T(8,128)(2,1)S(1)}, bf16[1,128,128]{2,1,0:T(8,128)(2,1)}, u32[]{:S(2)}) copy-start(bf16[1,128,128]{2,1,0:T(8,128)(2,1)} %param.11) | copy-start | bytes 98308
  67.2 4.3 %copy-start.2 = (bf16[128,128]{1,0:T(8,128)(2,1)S(1)}, bf16[128,128]{1,0:T(8,128)(2,1)}, u32[]{:S(2)}) copy-start(bf16[128,128]{1,0:T(8,128)(2,1)} %weight.1) | copy-start | bytes 98308
  68.1 3.3 %collective-permute-start.2 = (f32[3,128,128]{2,1,0:T(8,128)S(1)}, f32[3,128,128]{2,1,0:T(8,128)S(1)}, u32[]{:S(2)}, u32[]{:S(2)}) collective-permute-start(f32[3,128,128]{2,1,0:T(8,128)S(1)} %forward.1.mine), channel_id=1, source_target_pairs={{0,16},{16,0},{32,48},{48,32},{64,80},{80,64},{96,112},{112,96},{1... | collective-permute-start | bytes 589832 | tf_op jit(solution)/shard_map/pair/ppermute | solution.py:95
  73.4 18.0 %all-to-all-start = ((f32[16,64,128]{2,1,0:T(8,128)}), f32[16,64,128]{2,1,0:T(8,128)S(1)}, u32[]{:S(2)}, u32[]{:S(2)}) async-start(f32[16,64,128]{2,1,0:T(8,128)} %broadcast_in_dim.13), calls=%async_computation | async-start | bytes 1048576 | tf_op jit(solution)/shard_map/weight_groups/all_to_all | solution.py:159
  81.9 15.5 %collective-permute-start.3 = (bf16[8,128,128]{2,1,0:T(8,128)(2,1)S(1)}, bf16[8,128,128]{2,1,0:T(8,128)(2,1)S(1)}, u32[]{:S(2)}, u32[]{:S(2)}) collective-permute-start(bf16[8,128,128]{2,1,0:T(8,128)(2,1)S(1)} %get-tuple-element.19), channel_id=1, source_target_pairs={{0,992},{16,48},{32,0},{48,80},{64,32},{80,112},{96,64},{112,144},... | collective-permute-start | bytes 786440 | tf_op jit(solution)/shard_map/scatter_near/ppermute | solution.py:89
  83.8 17.5 %collective-permute-start.4 = (bf16[8,128,128]{2,1,0:T(8,128)(2,1)S(1)}, bf16[8,128,128]{2,1,0:T(8,128)(2,1)S(1)}, u32[]{:S(2)}, u32[]{:S(2)}) collective-permute-start(bf16[8,128,128]{2,1,0:T(8,128)(2,1)S(1)} %get-tuple-element.20), channel_id=1, source_target_pairs={{0,960},{16,80},{32,992},{48,112},{64,0},{80,144},{96,32},{112,176... | collective-permute-start | bytes 786440 | tf_op jit(solution)/shard_map/scatter_near/ppermute | solution.py:89
  87.0 14.3 %collective-permute-start.5 = (bf16[8,128,128]{2,1,0:T(8,128)(2,1)S(1)}, bf16[8,128,128]{2,1,0:T(8,128)(2,1)S(1)}, u32[]{:S(2)}, u32[]{:S(2)}) collective-permute-start(bf16[8,128,128]{2,1,0:T(8,128)(2,1)S(1)} %get-tuple-element.21), channel_id=1, source_target_pairs={{0,32},{16,1008},{32,64},{48,16},{64,96},{80,48},{96,128},{112,80}... | collective-permute-start | bytes 786440 | tf_op jit(solution)/shard_map/scatter_near/ppermute | solution.py:89
  91.4 10.1 %collective-permute-start.6 = (f32[8,2,128]{2,1,0:T(2,128)S(1)}, f32[8,2,128]{2,1,0:T(2,128)S(1)}, u32[]{:S(2)}, u32[]{:S(2)}) collective-permute-start(f32[8,2,128]{2,1,0:T(2,128)S(1)} %bitcast.30), channel_id=1, source_target_pairs={{0,992},{16,48},{32,0},{48,80},{64,32},{80,112},{96,64},{112,144},... | collective-permute-start | bytes 24584 | tf_op jit(solution)/shard_map/weight_near/ppermute | solution.py:89
  94.2 7.3 %collective-permute-start.7 = (f32[8,2,128]{2,1,0:T(2,128)S(1)}, f32[8,2,128]{2,1,0:T(2,128)S(1)}, u32[]{:S(2)}, u32[]{:S(2)}) collective-permute-start(f32[8,2,128]{2,1,0:T(2,128)S(1)} %bitcast.29), channel_id=1, source_target_pairs={{0,960},{16,80},{32,992},{48,112},{64,0},{80,144},{96,32},{112,176... | collective-permute-start | bytes 24584 | tf_op jit(solution)/shard_map/weight_near/ppermute | solution.py:89
  97.4 6.8 %collective-permute-start.8 = (f32[8,2,128]{2,1,0:T(2,128)S(1)}, f32[8,2,128]{2,1,0:T(2,128)S(1)}, u32[]{:S(2)}, u32[]{:S(2)}) collective-permute-start(f32[8,2,128]{2,1,0:T(2,128)S(1)} %bitcast.28), channel_id=1, source_target_pairs={{0,32},{16,1008},{32,64},{48,16},{64,96},{80,48},{96,128},{112,80}... | collective-permute-start | bytes 24584 | tf_op jit(solution)/shard_map/weight_near/ppermute | solution.py:89
